TPU v7x, 32 devices: a whole 2x2x4 slice. The times are simulated.
32 devices in a mesh: seq: 8 (over z, x), grp: 4 (over y, core).
Axes of the slice: x: 2, y: 2, z: 4, core: 2. Of those that a mesh axis runs over, the one named last changes fastest.
Arguments:
- tokens: bfloat16 [4, 1024, 768], P('grp', 'seq'), may hold values from -20 to 20
- out_grad: bfloat16 [4, 1024, 768], P('grp', 'seq'), may hold values from -6 to 6
- norm_gain: float32 [2, 768], replicated, may hold values from 0.25 to 1.75
- norm_bias: float32 [2, 768], replicated, may hold values from -3 to 3
- in_weight: bfloat16 [768, 2304], replicated, may hold values from -0.21875 to 0.21875
- in_bias: float32 [2304], replicated, may hold values from -3 to 3
- conv_weight: float32 [3, 2304], replicated, may hold values from -3 to 3
- conv_bias: float32 [2304], replicated, may hold values from -3 to 3
- filt_first: float32 [33, 64], replicated, may hold values from -1 to 1
- filt_hidden: float32 [2, 64, 64], replicated, may hold values from -0.75 to 0.75
- filt_bias: float32 [3, 64], replicated, may hold values from -3 to 3
- filt_freq: float32 [3, 64], replicated, may hold values from 2 to 10
- filt_last: float32 [64, 768], replicated, may hold values from -0.1875 to 0.1875
- decay_rates: float32 [768], replicated, may hold values from 0 to 0.034, as said below
- skip_scale: float32 [768], replicated, may hold values from -4 to 4
- out_weight: bfloat16 [768, 768], replicated, may hold values from -0.21875 to 0.21875
- out_bias: float32 [768], replicated, may hold values from -3 to 3
- up_weight: bfloat16 [768, 3072], replicated, may hold values from -0.21875 to 0.21875
- up_bias: float32 [3072], replicated, may hold values from -3 to 3
- down_weight: bfloat16 [3072, 768], replicated, may hold values from -0.109375 to 0.109375
- down_bias: float32 [768], replicated, may hold values from -3 to 3
Outputs:
- output: float32 [4, 1024, 768], P('grp', 'seq')
- grad_tokens: float32 [4, 1024, 768], P('grp', 'seq')
- grad_norm_gain: float32 [2, 768], replicated
- grad_norm_bias: float32 [2, 768], replicated
- grad_in_weight: float32 [1769472], P(('seq', 'grp'))
- grad_in_bias: float32 [2304], replicated
- grad_conv_weight: float32 [3, 2304], replicated
- grad_conv_bias: float32 [2304], replicated
- grad_filt_first: float32 [33, 64], replicated
- grad_filt_hidden: float32 [2, 64, 64], replicated
- grad_filt_bias: float32 [3, 64], replicated
- grad_filt_freq: float32 [3, 64], replicated
- grad_filt_last: float32 [64, 768], replicated
- grad_decay_rates: float32 [768], replicated
- grad_skip_scale: float32 [768], replicated
- grad_out_weight: float32 [589824], P(('seq', 'grp'))
- grad_out_bias: float32 [768], replicated
- grad_up_weight: float32 [2359296], P(('seq', 'grp'))
- grad_up_bias: float32 [3072], replicated
- grad_down_weight: float32 [2359296], P(('seq', 'grp'))
- grad_down_bias: float32 [768], replicated
Inputs may be any that keep to these rules, and one draw needn't show every extreme that they name: `decay_rates`: every rate is positive.
All inputs are finite; a program needn't handle non-finite values.
Results may differ from a plain program's by a relative error of at most 0.0097.
Values may be sent and summed in bfloat16 or wider, within the bound.
A program may use at most 192 MiB of HBM per device.

v0:
```python
import math

import jax
import jax.numpy as jnp
from jax import lax
from jax.sharding import PartitionSpec as P

epsilon = 1e-05


def shifted(array, axis, by):
    peers = lax.axis_size(axis)
    pairs = [(i, i + by) for i in range(peers) if 0 <= i + by < peers]
    return lax.ppermute(array, axis, pairs)


def highest(left_mat, right_mat):
    return jnp.dot(
        left_mat, right_mat, precision=lax.Precision.HIGHEST, preferred_element_type=jnp.float32
    )


def highest_t(left_mat, right_mat):
    return lax.dot_general(
        left_mat,
        right_mat,
        (((0,), (0,)), ((), ())),
        precision=lax.Precision.HIGHEST,
        preferred_element_type=jnp.float32,
    )


def rows_t(left_mat, right_mat):
    return lax.dot_general(
        left_mat, right_mat, (((0,), (0,)), ((), ())), preferred_element_type=jnp.float32
    )


def back_mul(grad_in, weight_mat):
    return lax.dot_general(
        grad_in, weight_mat, (((1,), (1,)), ((), ())), preferred_element_type=jnp.float32
    )


def layer_norm(values, gain_row, shift_row):
    row_mean = jnp.mean(values, axis=-1, keepdims=True)
    centred = values - row_mean
    inv_std = lax.rsqrt(jnp.mean(centred * centred, axis=-1, keepdims=True) + epsilon)
    normed = centred * inv_std
    return (normed * gain_row + shift_row, normed, inv_std)


def norm_back(grad_in, normed, inv_std, gain_row):
    scaled = grad_in * gain_row
    centred_grad = (
        scaled
        - jnp.mean(scaled, axis=-1, keepdims=True)
        - normed * jnp.mean(scaled * normed, axis=-1, keepdims=True)
    )
    return (centred_grad * inv_std, jnp.sum(grad_in * normed, axis=0), jnp.sum(grad_in, axis=0))


def smooth(values):
    return jax.nn.gelu(values, approximate=False)


def filter_rows(params, positions, length):
    filt_first, filt_hidden, filt_bias, filt_freq, filt_last, decay_rates = params
    place = positions.astype(jnp.float32)
    bands = (filt_first.shape[0] - 1) // 2
    band = 0.0001 + jnp.arange(bands, dtype=jnp.float32) * ((bands - 1 - 0.0001) / (bands - 1))
    omega = place[:, None] * (2.0 * math.pi / length)
    phase = omega * band[None, :]
    feats = jnp.concatenate(
        [place[:, None] / (length - 1), jnp.cos(phase), -jnp.sin(phase)], axis=1
    )
    act_one = jnp.sin(filt_freq[0] * (highest(feats, filt_first) + filt_bias[0]))
    act_two = jnp.sin(filt_freq[1] * (highest(act_one, filt_hidden[0]) + filt_bias[1]))
    act_three = jnp.sin(filt_freq[2] * (highest(act_two, filt_hidden[1]) + filt_bias[2]))
    window = jnp.exp(-decay_rates[None, :] * jnp.maximum(place, 0.0)[:, None])
    return highest(act_three, filt_last) * window


def body(
    tokens,
    out_grad,
    norm_gain,
    norm_bias,
    in_weight,
    in_bias,
    conv_weight,
    conv_bias,
    filt_first,
    filt_hidden,
    filt_bias,
    filt_freq,
    filt_last,
    decay_rates,
    skip_scale,
    out_weight,
    out_bias,
    up_weight,
    up_bias,
    down_weight,
    down_bias,
):
    row_count = tokens.shape[1]
    model_width = tokens.shape[2]
    seq_count = lax.axis_size("seq")
    length = row_count * seq_count
    fft_span = 2 * row_count
    fparams = (filt_first, filt_hidden, filt_bias, filt_freq, filt_last, decay_rates)
    fft_grid = jnp.arange(fft_span, dtype=jnp.int32)
    angles = (fft_grid[:, None] * fft_grid[None, :] % fft_span).astype(jnp.float32) * (
        2.0 * math.pi / fft_span
    )
    cos_full = jnp.cos(angles)
    sin_full = jnp.sin(angles)
    cos_left = cos_full[:, :row_count]
    sin_left = sin_full[:, :row_count]
    cos_low = cos_full[row_count:, :]
    sin_low = sin_full[row_count:, :]

    def segment(params, lag_step):
        positions = (lag_step - 1) * row_count + fft_grid
        keep_mask = (positions >= 0).astype(jnp.float32)
        return filter_rows(params, positions, length) * keep_mask[:, None]

    def forward_add(lag_step, source, totals):
        filter_taps = segment(fparams, lag_step)
        g_re = highest(cos_full, filter_taps)
        g_im = -highest(sin_full, filter_taps)
        source_f = source.astype(jnp.float32)
        s_re = highest(cos_left, source_f)
        s_im = -highest(sin_left, source_f)
        return (totals[0] + g_re * s_re - g_im * s_im, totals[1] + g_re * s_im + g_im * s_re)

    inputs = tokens[0].astype(jnp.float32)
    normed1, hat_one, std_one = layer_norm(inputs, norm_gain[0], norm_bias[0])
    normed1_b = normed1.astype(jnp.bfloat16)
    projected = (
        jnp.dot(normed1_b, in_weight, preferred_element_type=jnp.float32) + in_bias
    ).astype(jnp.bfloat16)
    before = shifted(projected[row_count - 2 :], "seq", 1)
    padded = jnp.concatenate([before, projected], axis=0).astype(jnp.float32)
    mixed_conv = (
        conv_weight[0] * padded[:row_count]
        + conv_weight[1] * padded[1 : row_count + 1]
        + conv_weight[2] * padded[2:]
        + conv_bias
    )
    outer_part = mixed_conv[:, :model_width]
    inner_part = mixed_conv[:, model_width : 2 * model_width]
    value_part = mixed_conv[:, 2 * model_width :]
    gated_b = (inner_part * value_part).astype(jnp.bfloat16)
    gated_f = gated_b.astype(jnp.float32)
    zero_totals = (
        jnp.zeros((fft_span, model_width), jnp.float32),
        jnp.zeros((fft_span, model_width), jnp.float32),
    )
    first_pass = forward_add(0, gated_b, zero_totals)

    def forward_step(lag_step, loop_carry):
        source, tot_re, tot_im = loop_carry
        source = shifted(source, "seq", 1)
        tot_re, tot_im = forward_add(lag_step, source, (tot_re, tot_im))
        return (source, tot_re, tot_im)

    unused_src, tot_re, tot_im = lax.fori_loop(
        1, seq_count, forward_step, (gated_b, first_pass[0], first_pass[1])
    )
    conv_out = (highest(cos_low, tot_re) - highest(sin_low, tot_im)) / fft_span
    summed = conv_out + skip_scale * gated_f
    mixed_out_b = (outer_part * summed).astype(jnp.bfloat16)
    residual = (
        inputs + jnp.dot(mixed_out_b, out_weight, preferred_element_type=jnp.float32) + out_bias
    )
    normed2, hat_two, std_two = layer_norm(residual, norm_gain[1], norm_bias[1])
    normed2_b = normed2.astype(jnp.bfloat16)
    pre_act = jnp.dot(normed2_b, up_weight, preferred_element_type=jnp.float32) + up_bias
    act_val, gelu_back = jax.vjp(smooth, pre_act)
    act_b = act_val.astype(jnp.bfloat16)
    result = residual + jnp.dot(act_b, down_weight, preferred_element_type=jnp.float32) + down_bias
    grad_out_b = out_grad[0]
    grad_out_f = grad_out_b.astype(jnp.float32)
    g_down = rows_t(act_b, grad_out_b)
    g_down_bias = jnp.sum(grad_out_f, axis=0)
    g_act = back_mul(grad_out_b, down_weight)
    g_pre_b = gelu_back(g_act)[0].astype(jnp.bfloat16)
    g_up = rows_t(normed2_b, g_pre_b)
    g_up_bias = jnp.sum(g_pre_b.astype(jnp.float32), axis=0)
    g_norm_two = back_mul(g_pre_b, up_weight)
    g_res_norm, g_gain_two, g_shift_two = norm_back(g_norm_two, hat_two, std_two, norm_gain[1])
    g_resid = grad_out_f + g_res_norm
    g_resid_b = g_resid.astype(jnp.bfloat16)
    g_outw = rows_t(mixed_out_b, g_resid_b)
    g_out_bias = jnp.sum(g_resid_b.astype(jnp.float32), axis=0)
    g_mixed = back_mul(g_resid_b, out_weight)
    g_outer = g_mixed * summed
    g_summed = g_mixed * outer_part
    g_skip = jnp.sum(g_summed * gated_f, axis=0)
    g_conv_b = g_summed.astype(jnp.bfloat16)
    v_re = highest(cos_left, gated_f)
    v_im = -highest(sin_left, gated_f)

    def backward_add(lag_step, source, loop_carry):
        tot_re, tot_im, grad_acc = loop_carry
        source_f = source.astype(jnp.float32)
        d_re = highest_t(cos_low, source_f) / fft_span
        d_im = -highest_t(sin_low, source_f) / fft_span

        def lag_taps(params):
            return segment(params, lag_step)

        filter_taps, taps_pull = jax.vjp(lag_taps, fparams)
        g_re = highest(cos_full, filter_taps)
        g_im = -highest(sin_full, filter_taps)
        tot_re = tot_re + g_re * d_re + g_im * d_im
        tot_im = tot_im - g_im * d_re + g_re * d_im
        s_re = v_re * d_re + v_im * d_im
        s_im = v_re * d_im - v_im * d_re
        d_taps = highest_t(cos_full, s_re) - highest_t(sin_full, s_im)
        more_grads = taps_pull(d_taps)[0]
        grad_acc = jax.tree.map(jnp.add, grad_acc, more_grads)
        return (tot_re, tot_im, grad_acc)

    zero_grads = jax.tree.map(jnp.zeros_like, fparams)
    start_carry = (zero_totals[0], zero_totals[1], zero_grads)
    first_back = backward_add(0, g_conv_b, start_carry)

    def backward_step(lag_step, loop_carry):
        source, tot_re, tot_im, grad_acc = loop_carry
        source = shifted(source, "seq", -1)
        tot_re, tot_im, grad_acc = backward_add(lag_step, source, (tot_re, tot_im, grad_acc))
        return (source, tot_re, tot_im, grad_acc)

    unused_src, back_re, back_im, cycle_grads = lax.fori_loop(
        1, seq_count, backward_step, (g_conv_b,) + first_back
    )
    g_long = highest_t(cos_left, back_re) - highest_t(sin_left, back_im)
    g_gated = g_summed * skip_scale + g_long
    g_mix = jnp.concatenate([g_outer, g_gated * value_part, g_gated * inner_part], axis=1)
    g_conv_bias = jnp.sum(g_mix, axis=0)
    g_conv_w = jnp.stack(
        [
            jnp.sum(g_mix * padded[tap_index : tap_index + row_count], axis=0)
            for tap_index in range(3)
        ]
    )
    g_pad = (
        jnp.pad(conv_weight[0] * g_mix, ((0, 2), (0, 0)))
        + jnp.pad(conv_weight[1] * g_mix, ((1, 1), (0, 0)))
        + jnp.pad(conv_weight[2] * g_mix, ((2, 0), (0, 0)))
    )
    after_rows = shifted(g_pad[:2], "seq", -1)
    g_proj_b = (g_pad[2:] + jnp.pad(after_rows, ((row_count - 2, 0), (0, 0)))).astype(jnp.bfloat16)
    g_inw = rows_t(normed1_b, g_proj_b)
    g_in_bias = jnp.sum(g_proj_b.astype(jnp.float32), axis=0)
    g_norm_one = back_mul(g_proj_b, in_weight)
    g_in_norm, g_gain_one, g_shift_one = norm_back(g_norm_one, hat_one, std_one, norm_gain[0])
    g_tokens = g_resid + g_in_norm
    small_grads = lax.psum(
        (
            jnp.stack([g_gain_one, g_gain_two]),
            jnp.stack([g_shift_one, g_shift_two]),
            g_in_bias,
            g_conv_w,
            g_conv_bias,
            cycle_grads[0],
            cycle_grads[1],
            cycle_grads[2],
            cycle_grads[3],
            cycle_grads[4],
            cycle_grads[5],
            g_skip,
            g_out_bias,
            g_up_bias,
            g_down_bias,
        ),
        ("seq", "grp"),
    )
    large_grads = (
        lax.psum_scatter(g_inw.reshape(-1), ("seq", "grp"), scatter_dimension=0, tiled=True),
        lax.psum_scatter(g_outw.reshape(-1), ("seq", "grp"), scatter_dimension=0, tiled=True),
        lax.psum_scatter(g_up.reshape(-1), ("seq", "grp"), scatter_dimension=0, tiled=True),
        lax.psum_scatter(g_down.reshape(-1), ("seq", "grp"), scatter_dimension=0, tiled=True),
    )
    return (
        result[None],
        g_tokens[None],
        small_grads[0],
        small_grads[1],
        large_grads[0],
        small_grads[2],
        small_grads[3],
        small_grads[4],
        small_grads[5],
        small_grads[6],
        small_grads[7],
        small_grads[8],
        small_grads[9],
        small_grads[10],
        small_grads[11],
        large_grads[1],
        small_grads[12],
        large_grads[2],
        small_grads[13],
        large_grads[3],
        small_grads[14],
    )


def solution(mesh):
    return jax.shard_map(
        body,
        mesh=mesh,
        in_specs=(
            P("grp", "seq", None),
            P("grp", "seq", None),
            P(),
            P(),
            P(),
            P(),
            P(),
            P(),
            P(),
            P(),
            P(),
            P(),
            P(),
            P(),
            P(),
            P(),
            P(),
            P(),
            P(),
            P(),
            P(),
        ),
        out_specs=(
            P("grp", "seq", None),
            P("grp", "seq", None),
            P(),
            P(),
            P(("seq", "grp")),
            P(),
            P(),
            P(),
            P(),
            P(),
            P(),
            P(),
            P(),
            P(),
            P(),
            P(("seq", "grp")),
            P(),
            P(("seq", "grp")),
            P(),
            P(("seq", "grp")),
            P(),
        ),
        check_vma=False,
    )
```

profile of v0, /device:TPU:0, one launch (start us, length us, event | category | flops | bytes accessed | tf_op | source)
XLA Modules:
  0.0 1180.4 jit_solution(9341414132691060047)
XLA Ops:
  13.5 5.4 collective-permute-start.2
  23.4 2.9 fusion.164
  26.4 2.9 fusion.163
  39.6 2.4 multiply_add_fusion.7
  41.9 2.3 copy.74
  44.2 2.4 copy.75
  46.6 182.3 %while.57 = (s32[]{:T(128)}, bf16[128,768]{1,0:T(8,128)(2,1)}, f32[256,768]{0,1:T(8,128)}, f32[256,768]{0,1:T(8,128)}, f32[3,64]{1,0:T(4,128)}, /*index=5*/f32[3...) while((s32[]{:T(128)}, bf16[128,768]{1,0:T(8,128)(2,1)}, ...), condition=%wide.region_3.4_spmd.clone, body=%wide.region_2.3_spmd.clone.sunk | while | flops 1999105024 | bytes 26443000 | solution.py:169
  46.8 3.6 collective-permute-start
  62.2 2.2 convolution_bitcast_fusion.12
  64.5 2.2 convolution_bitcast_fusion.13
  73.1 3.4 collective-permute-start
  88.3 2.2 convolution_bitcast_fusion.12
  90.6 2.2 convolution_bitcast_fusion.13
  99.1 3.5 collective-permute-start
  114.5 2.2 convolution_bitcast_fusion.12
  116.8 2.2 convolution_bitcast_fusion.13
  125.3 3.4 collective-permute-start
  140.6 2.2 convolution_bitcast_fusion.12
  142.9 2.2 convolution_bitcast_fusion.13
  151.5 3.4 collective-permute-start
  166.8 2.2 convolution_bitcast_fusion.12
  169.1 2.2 convolution_bitcast_fusion.13
  177.6 3.4 collective-permute-start
  192.9 2.2 convolution_bitcast_fusion.12
  195.2 2.2 convolution_bitcast_fusion.13
  217.6 2.2 convolution_bitcast_fusion.12
  219.9 2.2 convolution_bitcast_fusion.13
  228.9 2.2 fusion.269
  231.1 2.2 multiply_convert_fusion.1
  234.2 8.0 multiply_convert_fusion
  242.3 2.5 convert_reduce_fusion
  244.8 2.3 multiply_reduce_fusion.11
  248.0 3.2 fusion.181
  266.4 2.3 copy.78
  268.7 2.3 copy.76
  271.0 2.3 copy.77
  275.6 2.3 copy.79
  281.9 217.2 %while.58 = (s32[]{:T(128)}, bf16[128,768]{1,0:T(8,128)(2,1)}, f32[256,768]{0,1:T(8,128)}, f32[256,768]{0,1:T(8,128)}, f32[33,64]{1,0:T(8,128)}, /*index=5*/f32[...) while((s32[]{:T(128)}, bf16[128,768]{1,0:T(8,128)(2,1)}, ...), condition=%wide.region_23.24_spmd.clone.clone, body=%wide.region_15.23_spmd.clone.clone.sunk | while | flops 3572547072 | bytes 47359028 | solution.py:237
  304.1 2.4 fusion.422
  307.9 2.7 multiply_add_fusion.16
  335.0 2.4 fusion.422
  338.8 2.7 multiply_add_fusion.16
  365.8 2.4 fusion.422
  369.7 2.7 multiply_add_fusion.16
  396.7 2.4 fusion.422
  400.6 2.7 multiply_add_fusion.16
  427.6 2.4 fusion.422
  431.4 2.7 multiply_add_fusion.16
  458.7 2.4 fusion.422
  462.6 2.7 multiply_add_fusion.16
  490.2 2.4 fusion.422
  494.1 2.7 multiply_add_fusion.16
  501.3 2.2 slice_multiply_fusion
  510.0 5.1 fusion.198
  515.1 5.2 convolution_bitcast_fusion.5
  520.3 3.2 reshape.339
  523.5 9.5 copy.84
  533.0 10.7 reshape.341
  546.8 4.2 fusion.271
  551.0 7.9 reshape.338
  562.4 4.3 fusion.147
  570.5 2.2 fusion.178
  572.7 436.9 %all-reduce.31.cloned.1.call-done = (f32[1769472]{0:T(1024)}, f32[64,768]{1,0:T(8,128)}, f32[589824]{0:T(1024)}, f32[2359296]{0:T(1024)}, f32[2359296]{0:T(1024)}) async-done(((f32[1769472]{0:T(1024)}, f32[64,768]{1,0:T(8,128)}, f32[589824]{0:T(1024)}, f32[2359296]{0:T(1024)}, f32[2359296]{0:T(1024)}), (f32[1769472]{0:T(1024)}, f32[64,768]{1,0:T(8,128)}, f32[589824]{0:T(1024)}, f32[2359296]{0:T(1024)}, ...) | async-done | bytes 28508176
  1016.1 137.1 %all-reduce.29.cloned.1.call-done = (f32[2,768]{1,0:T(2,128)}, f32[2,768]{1,0:T(2,128)}, f32[2304]{0:T(1024)}, f32[3,2304]{1,0:T(4,128)}, f32[2304]{0:T(1024)}, ...) async-done(((f32[2,768]{1,0:T(2,128)}, f32[2,768]{1,0:T(2,128)}, ...) | async-done | bytes 125712 | tf_op jit(solution)/shard_map/psum | solution.py:262
  (1045 shorter events, 394.6 us)
Async XLA Ops:
  7.2 1002.4 %all-reduce.31.cloned.1.call-start = ((), (), s32[]{:S(2)}) async-start(), calls=%async_computation.1 | async-start | bytes 57016320
  11.0 7.9 copy-start.124
  11.0 9.0 copy-start.128
  11.0 9.6 copy-start.56
  11.0 11.3 copy-start.15
  12.8 13.6 %copy-start.55 = (bf16[128,2304]{1,0:T(8,128)(2,1)}, bf16[128,2304]{1,0:T(8,128)(2,1)S(1)}, u32[]{:S(2)}) copy-start(bf16[128,2304]{1,0:T(8,128)(2,1)S(1)} %fusion.136) | copy-start | bytes 1769476
  13.5 21.7 %collective-permute-start.2 = (bf16[2,2304]{1,0:T(2,128)(2,1)}, bf16[2,2304]{1,0:T(2,128)(2,1)}, u32[]{:S(2)}, u32[]{:S(2)}) collective-permute-start(bf16[2,2304]{1,0:T(2,128)(2,1)} %slice.376), channel_id=1, source_target_pairs={{0,4},{4,8},{8,12},{12,16},{16,20},{20,24},{24,28},{1,5},{5,9},{9,... | collective-permute-start | bytes 27656 | tf_op jit(solution)/shard_map/ppermute | solution.py:14
  18.9 15.6 %copy-start.125 = (f32[256,1]{0,1:T(1,128)}, f32[256,1]{0,1:T(1,128)S(1)}, u32[]{:S(2)}) copy-start(f32[256,1]{0,1:T(1,128)S(1)} %convert_multiply_fusion.3) | copy-start | bytes 3076
  18.9 15.6 %copy-start.126 = (f32[256]{0:T(256)}, f32[256]{0:T(256)S(1)}, u32[]{:S(2)}) copy-start(f32[256]{0:T(256)S(1)} %compare_convert_fusion.2) | copy-start | bytes 3076
  19.0 15.6 %copy-start.117 = (f32[256]{0:T(256)}, f32[256]{0:T(256)S(1)}, u32[]{:S(2)}) copy-start(f32[256]{0:T(256)S(1)} %convert_maximum_fusion) | copy-start | bytes 3076
  19.0 14.9 %copy-start.94 = (f32[768]{0:T(1024)}, f32[768]{0:T(1024)S(1)}, u32[]{:S(2)}) copy-start(f32[768]{0:T(1024)S(1)} %neg.152) | copy-start | bytes 9220
  23.4 5.8 copy-start.49
  46.8 20.0 %collective-permute-start = (bf16[128,768]{1,0:T(8,128)(2,1)}, bf16[128,768]{1,0:T(8,128)(2,1)}, u32[]{:S(2)}, u32[]{:S(2)}) collective-permute-start(bf16[128,768]{1,0:T(8,128)(2,1)} %get-tuple-element.1898), channel_id=1, source_target_pairs={{0,4},{4,8},{8,12},{12,16},{16,20},{20,24},{24,28},{1,5},{5,9},{9,... | collective-permute-start | bytes 589832 | tf_op jit(solution)/shard_map/while/body/eval_jaxpr/ppermute | solution.py:14
  62.2 6.2 copy-start.36
  73.1 19.8 %collective-permute-start = (bf16[128,768]{1,0:T(8,128)(2,1)}, bf16[128,768]{1,0:T(8,128)(2,1)}, u32[]{:S(2)}, u32[]{:S(2)}) collective-permute-start(bf16[128,768]{1,0:T(8,128)(2,1)} %get-tuple-element.1898), channel_id=1, source_target_pairs={{0,4},{4,8},{8,12},{12,16},{16,20},{20,24},{24,28},{1,5},{5,9},{9,... | collective-permute-start | bytes 589832 | tf_op jit(solution)/shard_map/while/body/eval_jaxpr/ppermute | solution.py:14
  88.3 6.2 copy-start.36
  99.1 19.9 %collective-permute-start = (bf16[128,768]{1,0:T(8,128)(2,1)}, bf16[128,768]{1,0:T(8,128)(2,1)}, u32[]{:S(2)}, u32[]{:S(2)}) collective-permute-start(bf16[128,768]{1,0:T(8,128)(2,1)} %get-tuple-element.1898), channel_id=1, source_target_pairs={{0,4},{4,8},{8,12},{12,16},{16,20},{20,24},{24,28},{1,5},{5,9},{9,... | collective-permute-start | bytes 589832 | tf_op jit(solution)/shard_map/while/body/eval_jaxpr/ppermute | solution.py:14
  114.5 6.2 copy-start.36
  125.3 19.8 %collective-permute-start = (bf16[128,768]{1,0:T(8,128)(2,1)}, bf16[128,768]{1,0:T(8,128)(2,1)}, u32[]{:S(2)}, u32[]{:S(2)}) collective-permute-start(bf16[128,768]{1,0:T(8,128)(2,1)} %get-tuple-element.1898), channel_id=1, source_target_pairs={{0,4},{4,8},{8,12},{12,16},{16,20},{20,24},{24,28},{1,5},{5,9},{9,... | collective-permute-start | bytes 589832 | tf_op jit(solution)/shard_map/while/body/eval_jaxpr/ppermute | solution.py:14
  140.6 6.2 copy-start.36
  142.9 5.4 copy-start.10
  142.9 5.4 copy-start.12
  142.9 5.4 copy-start.35
  151.5 19.9 %collective-permute-start = (bf16[128,768]{1,0:T(8,128)(2,1)}, bf16[128,768]{1,0:T(8,128)(2,1)}, u32[]{:S(2)}, u32[]{:S(2)}) collective-permute-start(bf16[128,768]{1,0:T(8,128)(2,1)} %get-tuple-element.1898), channel_id=1, source_target_pairs={{0,4},{4,8},{8,12},{12,16},{16,20},{20,24},{24,28},{1,5},{5,9},{9,... | collective-permute-start | bytes 589832 | tf_op jit(solution)/shard_map/while/body/eval_jaxpr/ppermute | solution.py:14
  166.8 6.2 copy-start.36
  169.0 5.4 copy-start.10
  169.1 5.4 copy-start.12
  169.1 5.4 copy-start.35
  177.6 19.8 %collective-permute-start = (bf16[128,768]{1,0:T(8,128)(2,1)}, bf16[128,768]{1,0:T(8,128)(2,1)}, u32[]{:S(2)}, u32[]{:S(2)}) collective-permute-start(bf16[128,768]{1,0:T(8,128)(2,1)} %get-tuple-element.1898), channel_id=1, source_target_pairs={{0,4},{4,8},{8,12},{12,16},{16,20},{20,24},{24,28},{1,5},{5,9},{9,... | collective-permute-start | bytes 589832 | tf_op jit(solution)/shard_map/while/body/eval_jaxpr/ppermute | solution.py:14
  192.9 6.2 copy-start.36
  203.7 18.4 %collective-permute-start = (bf16[128,768]{1,0:T(8,128)(2,1)}, bf16[128,768]{1,0:T(8,128)(2,1)}, u32[]{:S(2)}, u32[]{:S(2)}) collective-permute-start(bf16[128,768]{1,0:T(8,128)(2,1)} %get-tuple-element.1898), channel_id=1, source_target_pairs={{0,4},{4,8},{8,12},{12,16},{16,20},{20,24},{24,28},{1,5},{5,9},{9,... | collective-permute-start | bytes 589832 | tf_op jit(solution)/shard_map/while/body/eval_jaxpr/ppermute | solution.py:14
  217.6 6.2 copy-start.36
  233.3 8.9 slice-start.2
  233.4 11.4 slice-start
  234.0 13.2 %copy-start.18 = (f32[128,768]{1,0:T(8,128)}, f32[128,768]{1,0:T(8,128)S(1)}, u32[]{:S(2)}) copy-start(f32[128,768]{1,0:T(8,128)S(1)} %get-tuple-element.1600) | copy-start | bytes 1179652
  234.0 13.2 %copy-start.112 = (f32[128]{0:T(128)}, f32[128]{0:T(128)S(1)}, u32[]{:S(2)}) copy-start(f32[128]{0:T(128)S(1)} %broadcast_multiply_fusion.7) | copy-start | bytes 1540
  234.2 13.0 %copy-start.119 = (f32[128]{0:T(128)}, f32[128]{0:T(128)S(1)}, u32[]{:S(2)}) copy-start(f32[128]{0:T(128)S(1)} %add_rsqrt_fusion) | copy-start | bytes 1540
  234.2 8.1 slice-start.3
  234.2 8.1 copy-start.66
  234.2 10.5 slice-start.1
  271.0 10.8 copy-start.70
  281.9 10.8 collective-permute-start.1
  288.2 7.5 copy-start.1
  288.2 7.5 copy-start.2
  312.7 10.8 collective-permute-start.1
  319.0 7.5 copy-start.1
  319.1 7.5 copy-start.2
  343.6 10.8 collective-permute-start.1
  349.9 7.5 copy-start.1
  349.9 7.5 copy-start.2
  374.5 10.8 collective-permute-start.1
  380.8 7.5 copy-start.1
  380.8 7.5 copy-start.2
  405.3 10.8 collective-permute-start.1
  411.7 7.5 copy-start.1
  411.7 7.5 copy-start.2
  436.2 11.0 collective-permute-start.1
  442.5 7.8 copy-start.1
  442.5 7.8 copy-start.2
  467.3 11.4 collective-permute-start.1
  473.7 8.1 copy-start.1
  473.7 8.1 copy-start.2
  508.7 35.2 %collective-permute-start.3 = (f32[2,2304]{1,0:T(2,128)}, f32[2,2304]{1,0:T(2,128)}, u32[]{:S(2)}, u32[]{:S(2)}) collective-permute-start(f32[2,2304]{1,0:T(2,128)} %pad_add_fusion.2), channel_id=1, source_target_pairs={{4,0},{8,4},{12,8},{16,12},{20,16},{24,20},{28,24},{5,1},{9,5},{13... | collective-permute-start | bytes 55304 | tf_op jit(solution)/shard_map/ppermute | solution.py:14
  558.9 594.4 %all-reduce.29.cloned.1.call-start = ((), (), s32[]{:S(2)}) async-start(), calls=%async_computation | async-start | bytes 385024 | tf_op jit(solution)/shard_map/psum | solution.py:262
  (268 other events, 759.9 us)
Sparse Core Ops, SparseCore 0:
  559.0 450.5 all-reduce.30
  1018.3 134.9 all-reduce.28
where the time goes:
time: 1200 us; the launch traced here: 1180 us
  waiting for transfers between devices  575 us (48%)
  matrix products  318 us (26%)
  local copies, waits for them, and re-layouts  148 us (12%)
  other arithmetic  78.9 us (7%)
  starting transfers between devices  38.4 us (3%)
  between operations  15.7 us (1%)
    unnamed x3, waiting for transfers between devices  437 us
    dot_general x164, matrix products, highest(): jnp.dot(left_mat, right_mat, precision=lax.Precision.HIGHEST, preferred_e...  218 us
    psum x1, waiting for transfers between devices, body(): lax.psum((jnp.stack([g_gain_one, g_gain_two]), jnp.stack([g_shift_one, g_...  137 us
    dot_general x34, matrix products, highest_t(): lax.dot_general(left_mat, right_mat, (((0,), (0,)), ((), ())), precision=...  59.2 us
    unnamed x235, local copies, waits for them, and re-layouts  54.4 us
    ppermute x16, starting transfers between devices, shifted(): return lax.ppermute(array, axis, pairs)  38.4 us
    while x434, local copies, waits for them, and re-layouts  33.9 us
  transfers between devices with their start and end apart: 18, of which 4 were waited for; matrix products, arithmetic and copies ran while one was open for 21% of the time, Pallas kernels for 0%

commit v1 on v0

--- a/solution.py
+++ b/solution.py
@@ -2,7 +2,11 @@
 
 import jax
 import jax.numpy as jnp
+import ml_dtypes
+import numpy as np
 from jax import lax
+from jax.experimental import pallas as pl
+from jax.experimental.pallas import tpu as pltpu
 from jax.sharding import PartitionSpec as P
 
 epsilon = 1e-05
@@ -310,55 +314,976 @@
     )
 
 
+f32 = jnp.float32
+bf16 = jnp.bfloat16
+MESH_ID = pl.DeviceIdType.MESH
+HIGH = lax.Precision.HIGHEST
+ROWS = 128
+HALO = 16
+
+
+def nn(a, b):
+    return jnp.dot(a, b, preferred_element_type=f32)
+
+
+def nt(a, b):
+    return lax.dot_general(a, b, (((1,), (1,)), ((), ())), preferred_element_type=f32)
+
+
+def nn_high(a, b):
+    return jnp.dot(a, b, precision=HIGH, preferred_element_type=f32)
+
+
+def nt_high(a, b):
+    return lax.dot_general(
+        a, b, (((1,), (1,)), ((), ())), precision=HIGH, preferred_element_type=f32
+    )
+
+
+def tn_high(a, b):
+    return lax.dot_general(
+        a, b, (((0,), (0,)), ((), ())), precision=HIGH, preferred_element_type=f32
+    )
+
+
+def two(v):
+    high = v.astype(bf16)
+    return high, (v - high.astype(f32)).astype(bf16)
+
+
+def sin_cos(v):
+    k = jnp.floor(v * (1.0 / math.pi) + 0.5)
+    r = ((v - k * 3.140625) - k * 0.0009670257568359375) - k * 6.2771141529083252e-07
+    sign = 1.0 - 2.0 * (k - 2.0 * jnp.floor(k * 0.5))
+    q = r * r
+    s = 1.0 / math.factorial(13)
+    for order in (11, 9, 7, 5, 3):
+        s = 1.0 / math.factorial(order) - s * q
+    s = r - r * q * s
+    c = 1.0 / math.factorial(12)
+    for order in (10, 8, 6, 4, 2):
+        c = 1.0 / math.factorial(order) - c * q
+    c = 1.0 - q * c
+    return s * sign, c * sign
+
+
+def gelu_both(v):
+    a = jnp.abs(v)
+    t = 1.0 / (1.0 + (0.3275911 / math.sqrt(2.0)) * a)
+    poly = t * (
+        0.254829592
+        + t * (-0.284496736 + t * (1.421413741 + t * (-1.453152027 + t * 1.061405429)))
+    )
+    bell = jnp.exp(-0.5 * v * v)
+    tail = 0.5 * poly * bell
+    phi = jnp.where(v >= 0, 1.0 - tail, tail)
+    return v * phi, phi + v * bell * (1.0 / math.sqrt(2.0 * math.pi))
+
+
+def col_sum(v):
+    return jnp.sum(v, axis=0, keepdims=True)
+
+
+def row_mean(v):
+    return jnp.mean(v, axis=1, keepdims=True)
+
+
+def norm_rows(v):
+    centred = v - row_mean(v)
+    inv = lax.rsqrt(row_mean(centred * centred) + epsilon)
+    return centred * inv, inv
+
+
+def norm_rows_back(e, hat, inv, gain):
+    k = e * gain
+    return (k - row_mean(k) - hat * row_mean(k * hat)) * inv
+
+
+def fourier_tables():
+    bins = np.arange(128) + 0.5
+    angle = 2.0 * np.pi * bins[:, None] * np.arange(256)[None, :] / 256
+    full = np.concatenate([np.cos(angle), -np.sin(angle)], axis=0).astype(np.float32)
+    out = []
+    for mat in (full, full.T):
+        high = mat.astype(ml_dtypes.bfloat16)
+        out += [high, (mat - high.astype(np.float32)).astype(ml_dtypes.bfloat16)]
+    return np.stack(out)
+
+
+def feature_table(length, bands):
+    place = np.arange(length)
+    band = 1e-4 + np.arange(bands) * ((bands - 1 - 1e-4) / (bands - 1))
+    phase = band[:, None] * (2.0 * np.pi * place / length)[None, :]
+    return np.concatenate(
+        [(place / (length - 1))[None], np.cos(phase), -np.sin(phase)], axis=0
+    ).astype(np.float32)
+
+
+AT_GAIN, AT_SHIFT, AT_IN, AT_CONVW, AT_CONVB = 0, 12, 24, 42, 96
+AT_SKIP, AT_OUTB, AT_UPB, AT_DOWNB, AT_HID, AT_FIRST = 114, 120, 126, 150, 156, 220
+
+
+def step_kernel(
+    tokens, out_grad, in_w_h, out_w_h, up_w_h, down_w_h, tables_h, feats,
+    norm_gain, norm_bias, in_b, conv_w, conv_b, filt_first, filt_hidden, filt_bias,
+    filt_freq, filt_last, decay, skip, out_b, up_b, down_b,
+    o_out, o_gtok, o_gin, o_gout, o_gup, o_gdown, o_small,
+    in_w, out_w, up_w, down_w, tables,
+    tok, n1, hat1, std1, pp, outer, inner, value, gf,
+    stage, gat, xs, es, ys, co_in, taps, wind, hwin,
+    a1, a2, a3, c1, c2, c3, u1, u2, u3,
+    g_act, act, summed, hat2, std2, resid, g_resid, g_sum, g_outer,
+    at_down, at_up, at_in, at_out, lh_down, lh_up, lh_in, lh_out,
+    rh_down, rh_up, rh_in, rh_out,
+    s1a, k1a, r1a, s2a, r2a, zsa, zra, s1b, k1b, r1b, s2b, r2b, zsb, zrb,
+    gc_in, gl_in, gm, gtap, dpre,
+    sm, smr, fl, flr, ag,
+    f_gin, f_gout, f_gup, f_gdown, f_out, f_gtok,
+    ld, a2a_s, a2a_r, halo_s, halo_r, pair_s, pair_r,
+    p1_s, p1_r, p2_s, p2_r, z_s, z_r, sm_s, sm_r, fl_s, fl_r, ag_s, ag_r, st,
+):
+    s = lax.axis_index("seq")
+    g = lax.axis_index("grp")
+    me = s * 4 + g
+    z, x = lax.div(s, 2), lax.rem(s, 2)
+    y, c = lax.div(g, 2), lax.rem(g, 2)
+    other = g + 1 - 2 * c
+    x_step, y_step = 1 - 2 * x, 2 * (1 - 2 * y)
+    first = (s + (1 - c) * x_step, g + c * y_step)
+    second = (s + c * x_step, g + (1 - c) * y_step)
+    b1 = (1 - c) * x + c * y
+    b2 = (1 - c) * y + c * x
+
+    def at(index, size):
+        return pl.ds(pl.multiple_of(index * size, size), size)
+
+    def remote(src, dst, ss, rs, where):
+        return pltpu.make_async_remote_copy(
+            src_ref=src,
+            dst_ref=dst,
+            send_sem=ss,
+            recv_sem=rs,
+            device_id=where,
+            device_id_type=MESH_ID,
+        )
+
+    bar = pltpu.get_barrier_semaphore()
+
+    @pl.loop(1, 32)
+    def _(k):
+        t = lax.rem(me + k, 32)
+        pl.semaphore_signal(
+            bar, inc=1, device_id=(lax.div(t, 4), lax.rem(t, 4)), device_id_type=MESH_ID
+        )
+
+    loads = [
+        pltpu.make_async_copy(tokens.at[0], tok.at[pl.ds(HALO, ROWS)], ld.at[0]),
+        pltpu.make_async_copy(in_w_h, in_w, ld.at[1]),
+        pltpu.make_async_copy(tables_h, tables, ld.at[2]),
+        pltpu.make_async_copy(out_grad.at[0], rh_down.at[pl.ds(0, ROWS)], ld.at[3]),
+        pltpu.make_async_copy(down_w_h, down_w, ld.at[4]),
+        pltpu.make_async_copy(out_w_h, out_w, ld.at[5]),
+        pltpu.make_async_copy(up_w_h, up_w, ld.at[6]),
+    ]
+    for copy in loads:
+        copy.start()
+
+    def pair(index, src, dst):
+        return remote(src, dst, pair_s.at[index], pair_r.at[index], (s, other))
+
+    half = pl.ds(ROWS, ROWS)
+    pairs = [
+        pair(0, rh_down.at[pl.ds(0, ROWS)], rh_down.at[half]),
+        pair(1, at_in.at[1 - c], lh_in.at[:, half]),
+        pair(2, at_down.at[1 - c], lh_down.at[:, half]),
+        pair(3, at_out.at[1 - c], lh_out.at[:, half]),
+        pair(4, at_up.at[1 - c], lh_up.at[:, half]),
+        pair(5, rh_up.at[pl.ds(0, ROWS)], rh_up.at[half]),
+        pair(6, rh_out.at[pl.ds(0, ROWS)], rh_out.at[half]),
+        pair(7, rh_in.at[pl.ds(0, ROWS)], rh_in.at[half]),
+    ]
+
+    def order_rows(v, size, halves):
+        t = jnp.transpose(v)
+        for core in range(2):
+            blocks = []
+            for i1 in range(2):
+                for i2 in range(2):
+                    ix, iy = (i1, i2) if core == 0 else (i2, i1)
+                    for iz in range(4):
+                        at_row = size * (iz * 8 + ix * 4 + iy * 2 + core)
+                        blocks.append(t[at_row : at_row + size])
+            halves[core] = jnp.concatenate(blocks, axis=0).astype(bf16)
+
+    loads[0].wait()
+    hat, inv = norm_rows(tok[pl.ds(HALO, ROWS)].astype(f32))
+    hat1[...] = hat
+    std1[...] = inv
+    own_norm = (hat * norm_gain[0:1] + norm_bias[0:1]).astype(bf16)
+    n1[pl.ds(HALO, ROWS)] = own_norm
+    loads[3].wait()
+    pl.semaphore_wait(bar, 31)
+
+    last_rows = remote(
+        tok.at[pl.ds(ROWS, HALO)], tok.at[pl.ds(0, HALO)], halo_s.at[0], halo_r.at[0], (s + 1, g)
+    )
+
+    @pl.when(s < 7)
+    def _():
+        last_rows.start()
+
+    pairs[0].start()
+    order_rows(own_norm.astype(f32), 24, at_in)
+    lh_in[:, pl.ds(0, ROWS)] = at_in[c]
+    pairs[1].start()
+
+    @pl.when(s > 0)
+    def _():
+        last_rows.wait_recv()
+
+    @pl.when(s == 0)
+    def _():
+        tok[pl.ds(0, HALO)] = jnp.zeros((HALO, tok.shape[1]), bf16)
+
+    hat, inv = norm_rows(tok[pl.ds(0, HALO)].astype(f32))
+    n1[pl.ds(0, HALO)] = (hat * norm_gain[0:1] + norm_bias[0:1]).astype(bf16)
+    loads[1].wait()
+    inside = jnp.where(s > 0, 1.0, 0.0).astype(f32)
+    for part, dest in enumerate((outer, inner, value)):
+        cols = pl.ds(768 * part, 768)
+        proj = (nn(n1[...], in_w[:, cols]) + in_b[:, cols]).astype(bf16).astype(f32)
+        pp[pl.ds(0, HALO), cols] = proj[:HALO] * inside
+        pp[pl.ds(HALO, ROWS), cols] = proj[HALO:]
+        dest[...] = (
+            conv_w[0:1, cols] * pp[pl.ds(HALO - 2, ROWS), cols]
+            + conv_w[1:2, cols] * pp[pl.ds(HALO - 1, ROWS), cols]
+            + conv_w[2:3, cols] * pp[pl.ds(HALO, ROWS), cols]
+            + conv_b[:, cols]
+        )
+    gated = (inner[...] * value[...]).astype(bf16).astype(f32)
+    gf[...] = gated
+
+    def spread(v, which):
+        pad = jnp.zeros((ROWS, 32), f32)
+        for j in range(8):
+            piece = jnp.concatenate([v[:, 96 * j : 96 * j + 96], pad], axis=1)
+            stage[which, :, 128 * j : 128 * j + 128] = piece.astype(bf16)
+
+    def trade(which, dst):
+        @pl.loop(1, 8)
+        def _(k):
+            peer = lax.rem(s + k, 8)
+            remote(
+                stage.at[which, :, at(peer, 128)],
+                dst.at[:, at(s, 128)],
+                a2a_s.at[which, k - 1],
+                a2a_r.at[which, k - 1],
+                (peer, g),
+            ).start()
+
+        dst[:, at(s, 128)] = stage[which, :, at(s, 128)]
+
+    def arrive(which, dst):
+        @pl.loop(1, 8)
+        def _(k):
+            peer = lax.rem(s + 8 - k, 8)
+            remote(
+                stage.at[which, :, at(peer, 128)],
+                dst.at[:, at(peer, 128)],
+                a2a_s.at[which, k - 1],
+                a2a_r.at[which, k - 1],
+                (peer, g),
+            ).wait_recv()
+
+    spread(gated, 0)
+    trade(0, gat)
+
+    loads[2].wait()
+    bias_cols = jnp.transpose(filt_bias[...])
+    freq_cols = jnp.transpose(filt_freq[...])
+    below = feats[...]
+    for i, (u_ref, a_ref, c_ref) in enumerate(((u1, a1, c1), (u2, a2, c2), (u3, a3, c3))):
+        weights = filt_first[...] if i == 0 else filt_hidden[i - 1]
+        u = tn_high(weights, below) + bias_cols[:, i : i + 1]
+        u_ref[...] = u
+        below, cosine = sin_cos(freq_cols[:, i : i + 1] * u)
+        a_ref[...] = below
+        c_ref[...] = cosine
+
+    back = lax.rem(768 - 96 * s, 768)
+    lane = lax.broadcasted_iota(jnp.int32, (1, 128), 1)
+    live = lane < 96
+
+    def my_lanes(v):
+        return jnp.where(live, pltpu.roll(v, back, axis=1)[:, :128], 0.0)
+
+    last = my_lanes(filt_last[...])
+    rate = my_lanes(jnp.broadcast_to(decay[...], (8, 768)))[0:1]
+    hwin[:, pl.ds(0, 128)] = jnp.zeros((512, 128), bf16)
+    for b in range(8):
+        rows = pl.ds(128 * b, 128)
+        place = lax.broadcasted_iota(jnp.int32, (128, 128), 0).astype(f32) + 128.0 * b
+        window = jnp.exp(-rate * place)
+        tap = tn_high(a3[:, rows], last) * window
+        wind[rows] = window
+        taps[rows] = tap
+        high, low = two(tap)
+        hwin[pl.ds(128, 128), rows] = high
+        hwin[pl.ds(384, 128), rows] = low
+        if b < 7:
+            after = pl.ds(128 * b + 128, 128)
+            hwin[pl.ds(0, 128), after] = high
+            hwin[pl.ds(256, 128), after] = low
+
+    def table_mul(which, rows, v):
+        high, low = two(v)
+        return (
+            nn(tables[which, rows], high)
+            + nn(tables[which, rows], low)
+            + nn(tables[which + 1, rows], high)
+        )
+
+    es[...] = (
+        nn(tables[0], hwin[pl.ds(0, 256)])
+        + nn(tables[0], hwin[pl.ds(256, 256)])
+        + nn(tables[1], hwin[pl.ds(0, 256)])
+    )
+
+    arrive(0, gat)
+    xs[...] = nn(tables[0, :, 0:128], gat[...]) + nn(tables[1, :, 0:128], gat[...])
+
+    def pick(ref, tile, b):
+        lanes = pl.ds(128 * b, 128)
+        return ref[at(tile, 8), lanes], ref[pl.ds(pl.multiple_of(128 + tile * 8, 8), 8), lanes]
+
+    def keep(ref, tile, b, pair_of):
+        lanes = pl.ds(128 * b, 128)
+        ref[at(tile, 8), lanes] = pair_of[0]
+        ref[pl.ds(pl.multiple_of(128 + tile * 8, 8), 8), lanes] = pair_of[1]
+
+    @pl.loop(0, 16)
+    def _(tile):
+        e = [pick(es, tile, b) for b in range(8)]
+        v = [pick(xs, tile, b) for b in range(8)]
+        for b in range(8):
+            re, im = 0.0, 0.0
+            for lag in range(b + 1):
+                er, ei = e[lag]
+                vr, vi = v[b - lag]
+                re = re + er * vr - ei * vi
+                im = im + er * vi + ei * vr
+            keep(ys, tile, b, (re, im))
+
+    conv = table_mul(2, pl.ds(128, 128), ys[...]) * (1.0 / 128.0)
+    stage[1] = conv.astype(bf16)
+    trade(1, co_in)
+
+    loads[4].wait()
+    for t in range(4):
+        cols = pl.ds(768 * t, 768)
+        g_act[:, cols] = nt(rh_down[pl.ds(0, ROWS)], down_w[cols])
+
+    def gathered(ref):
+        return jnp.concatenate(
+            [ref[:, 128 * j : 128 * j + 96].astype(f32) for j in range(8)], axis=1
+        )
+
+    arrive(1, co_in)
+    sum_f = gathered(co_in) + skip[...] * gf[...]
+    summed[...] = sum_f
+    mixed = (outer[...] * sum_f).astype(bf16)
+    loads[5].wait()
+    res = tok[pl.ds(HALO, ROWS)].astype(f32) + nn(mixed, out_w[...]) + out_b[...]
+    resid[...] = res
+    hat, inv = norm_rows(res)
+    hat2[...] = hat
+    std2[...] = inv
+    n2 = (hat * norm_gain[1:2] + norm_bias[1:2]).astype(bf16)
+    loads[6].wait()
+    for t in range(4):
+        cols = pl.ds(768 * t, 768)
+        act_f, slope = gelu_both(nn(n2, up_w[:, cols]) + up_b[:, cols])
+        act_b = act_f.astype(bf16)
+        act[:, cols] = act_b
+        rh_up[pl.ds(0, ROWS), cols] = (g_act[:, cols] * slope).astype(bf16)
+        turned = jnp.transpose(act_b.astype(f32)).astype(bf16)
+        for ix in range(2):
+            for iy in range(2):
+                for core in range(2):
+                    i1, i2 = (ix, iy) if core == 0 else (iy, ix)
+                    src = 96 * (ix * 4 + iy * 2 + core)
+                    at_down[core, pl.ds(i1 * 768 + i2 * 384 + t * 96, 96)] = turned[src : src + 96]
+    pairs[2].start()
+    lh_down[:, pl.ds(0, ROWS)] = at_down[c]
+
+    def one_a(p):
+        return remote(s1a.at[p], r1a.at[p], p1_s.at[p], p1_r.at[p], first)
+
+    def two_a(p):
+        return remote(s2a.at[p], r2a.at[p], p2_s.at[p], p2_r.at[p], second)
+
+    def zed_a(p, k):
+        to = lax.rem(z + k, 4)
+        return remote(
+            zsa.at[p, to], zra.at[p, k - 1], z_s.at[p, k - 1], z_r.at[p, k - 1], (to * 2 + x, g)
+        )
+
+    def one_b(p):
+        return remote(s1b.at[p], r1b.at[p], p1_s.at[8 + p], p1_r.at[8 + p], first)
+
+    def two_b(p):
+        return remote(s2b.at[p], r2b.at[p], p2_s.at[8 + p], p2_r.at[8 + p], second)
+
+    def zed_b(p, k):
+        to = lax.rem(z + k, 4)
+        return remote(
+            zsb.at[p, to],
+            zrb.at[p, k - 1],
+            z_s.at[8 + p, k - 1],
+            z_r.at[8 + p, k - 1],
+            (to * 2 + x, g),
+        )
+
+    def make_a(p0, count, lh, rh):
+        @pl.loop(0, count)
+        def _(p):
+            s1a[p0 + p] = nn(lh[at(1 - b1, 192)], rh[:, at(p, 768)]).astype(bf16)
+            one_a(p0 + p).start()
+
+        @pl.loop(0, count)
+        def _(p):
+            k1a[p0 + p] = nn(lh[at(b1, 192)], rh[:, at(p, 768)]).astype(bf16)
+
+    def ph1_a(p):
+        one_a(p).wait_recv()
+        rows = at(1 - b2, 96)
+        s2a[p] = (k1a[p, rows].astype(f32) + r1a[p, rows].astype(f32)).astype(bf16)
+        two_a(p).start()
+
+    def ph2_a(p):
+        two_a(p).wait_recv()
+        rows = at(b2, 96)
+        v = k1a[p, rows].astype(f32) + r1a[p, rows].astype(f32) + r2a[p].astype(f32)
+        for iz in range(4):
+            block = v[24 * iz : 24 * iz + 24]
+            zsa[p, iz] = jnp.concatenate([block[:, :384], block[:, 384:]], axis=0).astype(bf16)
+        for k in range(1, 4):
+            zed_a(p, k).start()
+
+    def ph3_a(p, dest, base, per_row):
+        for k in range(1, 4):
+            zed_a(p, k).wait_recv()
+        v = zsa[p, z].astype(f32)
+        for k in range(3):
+            v = v + zra[p, k].astype(f32)
+        for h in range(2):
+            for j in range(3):
+                dest[pl.ds(base + 3 * h + j, 24, stride=per_row)] = v[
+                    24 * h : 24 * h + 24, 128 * j : 128 * j + 128
+                ]
+
+    def ph1_b(p):
+        one_b(p).wait_recv()
+        rows = at(1 - b2, 384)
+        s2b[p] = (k1b[p, rows].astype(f32) + r1b[p, rows].astype(f32)).astype(bf16)
+        two_b(p).start()
+
+    def ph2_b(p):
+        two_b(p).wait_recv()
+        rows = at(b2, 384)
+        v = k1b[p, rows].astype(f32) + r1b[p, rows].astype(f32) + r2b[p].astype(f32)
+        for iz in range(4):
+            zsb[p, iz] = v[96 * iz : 96 * iz + 96].astype(bf16)
+        for k in range(1, 4):
+            zed_b(p, k).start()
+
+    def ph3_b(p):
+        for k in range(1, 4):
+            zed_b(p, k).wait_recv()
+        v = zsb[p, z].astype(f32)
+        for k in range(3):
+            v = v + zrb[p, k].astype(f32)
+        for j in range(2):
+            f_gdown[pl.ds(2 * p + j, 96, stride=6)] = v[:, 128 * j : 128 * j + 128]
+
+    order_rows(mixed.astype(f32), 24, at_out)
+    pairs[3].start()
+    lh_out[:, pl.ds(0, ROWS)] = at_out[c]
+    order_rows(n2.astype(f32), 24, at_up)
+    pairs[4].start()
+    lh_up[:, pl.ds(0, ROWS)] = at_up[c]
+    pairs[5].start()
+
+    pairs[0].wait_recv()
+    pairs[2].wait_recv()
+
+    for p in range(3):
+        s1b[p] = nn(lh_down[at(1 - b1, 768)], rh_down[:, 256 * p : 256 * p + 256]).astype(bf16)
+        one_b(p).start()
+
+    e = nt(rh_up[pl.ds(0, ROWS)], up_w[...])
+
+    def put(row, v):
+        for j in range(v.shape[1] // 128):
+            sm[row + j : row + j + 1] = v[:, 128 * j : 128 * j + 128]
+
+    hat = hat2[...]
+    put(AT_GAIN + 6, col_sum(e * hat))
+    put(AT_SHIFT + 6, col_sum(e))
+    grad_f = rh_down[pl.ds(0, ROWS)].astype(f32)
+    put(AT_DOWNB, col_sum(grad_f))
+    put(AT_UPB, col_sum(rh_up[pl.ds(0, ROWS)].astype(f32)))
+    g_res = grad_f + norm_rows_back(e, hat, std2[...], norm_gain[1:2])
+    g_resid[...] = g_res
+    g_res_b = g_res.astype(bf16)
+    rh_out[pl.ds(0, ROWS)] = g_res_b
+    pairs[6].start()
+    put(AT_OUTB, col_sum(g_res_b.astype(f32)))
+    g_mixed = nt(g_res_b, out_w[...])
+    g_outer[...] = g_mixed * summed[...]
+    g_summed = g_mixed * outer[...]
+    g_sum[...] = g_summed
+    spread(g_summed, 2)
+    trade(2, gc_in)
+    put(AT_SKIP, col_sum(g_summed * gf[...]))
+
+    pairs[4].wait_recv()
+    pairs[5].wait_recv()
+    make_a(0, 4, lh_up, rh_up)
+    for p in range(3):
+        k1b[p] = nn(lh_down[at(b1, 768)], rh_down[:, 256 * p : 256 * p + 256]).astype(bf16)
+    pairs[3].wait_recv()
+    pairs[6].wait_recv()
+    make_a(4, 1, lh_out, rh_out)
+    ph1_b(0)
+
+    arrive(2, gc_in)
+    ys[...] = (nn(tables[0, :, 128:256], gc_in[...]) + nn(tables[1, :, 128:256], gc_in[...])) * (
+        1.0 / 128.0
+    )
+
+    @pl.loop(0, 16)
+    def _(tile):
+        e = [pick(es, tile, b) for b in range(8)]
+        d = [pick(ys, tile, b) for b in range(8)]
+        for b in range(8):
+            re, im = 0.0, 0.0
+            for lag in range(8 - b):
+                er, ei = e[lag]
+                dr, di = d[b + lag]
+                re = re + er * dr + ei * di
+                im = im + er * di - ei * dr
+            keep(es, tile, b, (re, im))
+
+    g_long = table_mul(2, pl.ds(0, 128), es[...])
+    stage[3] = g_long.astype(bf16)
+    trade(3, gl_in)
+
+    f_out[...] = resid[...] + nn(act[...], down_w[...]) + down_b[...]
+    store_out = pltpu.make_async_copy(f_out, o_out, st.at[0])
+    store_out.start()
+    ph1_b(1)
+
+    @pl.loop(0, 16)
+    def _(tile):
+        v = [pick(xs, tile, b) for b in range(8)]
+        d = [pick(ys, tile, b) for b in range(8)]
+        for lag in range(8):
+            re, im = 0.0, 0.0
+            for b in range(8 - lag):
+                vr, vi = v[b]
+                dr, di = d[b + lag]
+                re = re + vr * dr + vi * di
+                im = im + vr * di - vi * dr
+            keep(xs, tile, lag, (re, im))
+
+    gtap[...] = table_mul(2, pl.ds(0, 256), xs[...])
+    g_rate = jnp.zeros((1, 128), f32)
+    for b in range(8):
+        rows = pl.ds(128 * b, 128)
+        gt = gtap[pl.ds(128, 128), rows]
+        if b < 7:
+            gt = gt + gtap[pl.ds(0, 128), pl.ds(128 * b + 128, 128)]
+        place = lax.broadcasted_iota(jnp.int32, (128, 128), 0).astype(f32) + 128.0 * b
+        g_rate = g_rate - col_sum(place * taps[rows] * gt)
+        dpre[rows] = gt * wind[rows]
+    g_last = nn_high(a3[...], dpre[...])
+    decay_rows = jnp.concatenate(
+        [pltpu.roll(jnp.broadcast_to(g_rate, (8, 128)), 96 - 32 * j, axis=1)[0:1] for j in range(3)]
+        + [jnp.zeros((61, 128), f32)],
+        axis=0,
+    )
+    g_last = jnp.where(live, g_last, decay_rows)
+    for j in range(4):
+        fl[j] = g_last[16 * j : 16 * j + 16]
+    ones = jnp.ones((8, 1024), f32)
+    g_a = nt_high(last, dpre[...])
+    for i, (u_ref, c_ref, a_ref) in enumerate(((u3, c3, a2), (u2, c2, a1), (u1, c1, None))):
+        layer = 2 - i
+        g_arg = g_a * c_ref[...]
+        g_freq = nt_high(ones, g_arg * u_ref[...])[0:1]
+        g_u = g_arg * freq_cols[:, layer : layer + 1]
+        g_bias = nt_high(ones, g_u)[0:1]
+        sm[AT_FIRST + layer : AT_FIRST + layer + 1, 64:128] = g_bias
+        sm[AT_FIRST + 3 + layer : AT_FIRST + 4 + layer, 64:128] = g_freq
+        if layer > 0:
+            g_w = nt_high(a_ref[...], g_u)
+            sm[pl.ds(AT_HID, 64), 64 * (layer - 1) : 64 * layer] = g_w
+            g_a = nn_high(filt_hidden[layer - 1], g_u)
+        else:
+            sm[pl.ds(AT_FIRST, 33), 0:64] = nt_high(feats[...], g_u)
+
+    ph1_b(2)
+
+    arrive(3, gl_in)
+    g_gated = skip[...] * g_sum[...] + gathered(gl_in)
+    mixes = (g_outer[...], g_gated * value[...], g_gated * inner[...])
+    for part in range(3):
+        gm[pl.ds(0, ROWS), 768 * part : 768 * part + 768] = mixes[part]
+    first_rows = remote(
+        gm.at[pl.ds(0, 8)], gm.at[pl.ds(ROWS, 8)], halo_s.at[1], halo_r.at[1], (s - 1, g)
+    )
+
+    @pl.when(s > 0)
+    def _():
+        first_rows.start()
+
+    for part in range(3):
+        cols = pl.ds(768 * part, 768)
+        mix = gm[pl.ds(0, ROWS), cols]
+        put(AT_CONVB + 6 * part, col_sum(mix))
+        for tap in range(3):
+            put(
+                AT_CONVW + 18 * tap + 6 * part,
+                col_sum(mix * pp[pl.ds(HALO - 2 + tap, ROWS), cols]),
+            )
+
+    @pl.when(s < 7)
+    def _():
+        first_rows.wait_recv()
+
+    @pl.when(s == 7)
+    def _():
+        gm[pl.ds(ROWS, 8)] = jnp.zeros((8, gm.shape[1]), f32)
+
+    for part in range(3):
+        cols = pl.ds(768 * part, 768)
+        g_proj = (
+            conv_w[0:1, cols] * gm[pl.ds(2, ROWS), cols]
+            + conv_w[1:2, cols] * gm[pl.ds(1, ROWS), cols]
+            + conv_w[2:3, cols] * gm[pl.ds(0, ROWS), cols]
+        ).astype(bf16)
+        rh_in[pl.ds(0, ROWS), cols] = g_proj
+        put(AT_IN + 6 * part, col_sum(g_proj.astype(f32)))
+    pairs[7].start()
+    e = nt(rh_in[pl.ds(0, ROWS)], in_w[...])
+    hat = hat1[...]
+    put(AT_GAIN, col_sum(e * hat))
+    put(AT_SHIFT, col_sum(e))
+
+    @pl.loop(1, 32)
+    def _(k):
+        t = lax.rem(me + k, 32)
+        remote(
+            sm.at[at(t, 8)],
+            smr.at[k],
+            sm_s.at[k],
+            sm_r.at[k],
+            (lax.div(t, 4), lax.rem(t, 4)),
+        ).start()
+
+    @pl.loop(1, 4)
+    def _(k):
+        t = lax.rem(g + k, 4)
+        remote(fl.at[t], flr.at[k], fl_s.at[k], fl_r.at[k], (s, t)).start()
+
+    pairs[1].wait_recv()
+    pairs[7].wait_recv()
+    make_a(5, 3, lh_in, rh_in)
+    f_gtok[...] = g_resid[...] + norm_rows_back(e, hat, std1[...], norm_gain[0:1])
+    store_tok = pltpu.make_async_copy(f_gtok, o_gtok, st.at[1])
+    store_tok.start()
+
+    for p in range(3):
+        ph2_b(p)
+
+    @pl.loop(0, 5)
+    def _(p):
+        ph1_a(p)
+
+    @pl.loop(1, 32)
+    def _(k):
+        remote(sm.at[pl.ds(0, 8)], smr.at[k], sm_s.at[k], sm_r.at[k], (s, other)).wait_recv()
+
+    @pl.loop(1, 4)
+    def _(k):
+        remote(fl.at[0], flr.at[k], fl_s.at[k], fl_r.at[k], (s, other)).wait_recv()
+
+    smr[0] = sm[at(me, 8)]
+    flr[0] = fl[g]
+    ag[me, pl.ds(0, 8)] = jnp.sum(smr[...], axis=0)
+    ag[me, pl.ds(8, 16)] = jnp.sum(flr[...], axis=0)
+
+    @pl.loop(1, 32)
+    def _(k):
+        t = lax.rem(me + k, 32)
+        remote(
+            ag.at[me], ag.at[me], ag_s.at[k], ag_r.at[k], (lax.div(t, 4), lax.rem(t, 4))
+        ).start()
+
+    for p in range(3):
+        ph3_b(p)
+
+    @pl.loop(0, 5)
+    def _(p):
+        ph2_a(p)
+
+    @pl.loop(5, 8)
+    def _(p):
+        ph1_a(p)
+
+    @pl.loop(0, 4)
+    def _(p):
+        ph3_a(p, f_gup, 6 * p, 24)
+
+    ph3_a(4, f_gout, 0, 6)
+
+    stores = [
+        store_out,
+        store_tok,
+        pltpu.make_async_copy(f_gdown, o_gdown, st.at[2]),
+        pltpu.make_async_copy(f_gup, o_gup, st.at[3]),
+        pltpu.make_async_copy(f_gout, o_gout, st.at[4]),
+        pltpu.make_async_copy(f_gin, o_gin, st.at[5]),
+        pltpu.make_async_copy(ag, o_small, st.at[6]),
+    ]
+    for copy in stores[2:5]:
+        copy.start()
+
+    @pl.loop(5, 8)
+    def _(p):
+        ph2_a(p)
+
+    @pl.loop(1, 32)
+    def _(k):
+        t = lax.rem(me + 32 - k, 32)
+        remote(ag.at[t], ag.at[t], ag_s.at[k], ag_r.at[k], (s, other)).wait_recv()
+
+    stores[6].start()
+
+    @pl.loop(0, 3)
+    def _(p):
+        ph3_a(5 + p, f_gin, 6 * p, 18)
+
+    stores[5].start()
+
+    @pl.when(s < 7)
+    def _():
+        last_rows.wait_send()
+
+    @pl.when(s > 0)
+    def _():
+        first_rows.wait_send()
+
+    for copy in pairs:
+        copy.wait_send()
+
+    @pl.loop(0, 4)
+    def _(which):
+        @pl.loop(1, 8)
+        def _(k):
+            remote(
+                stage.at[which, :, pl.ds(0, 128)],
+                gat.at[:, pl.ds(0, 128)],
+                a2a_s.at[which, k - 1],
+                a2a_r.at[which, k - 1],
+                (s, other),
+            ).wait_send()
+
+    @pl.loop(0, 8)
+    def _(p):
+        one_a(p).wait_send()
+        two_a(p).wait_send()
+        for k in range(1, 4):
+            zed_a(p, k).wait_send()
+
+    @pl.loop(0, 3)
+    def _(p):
+        one_b(p).wait_send()
+        two_b(p).wait_send()
+        for k in range(1, 4):
+            zed_b(p, k).wait_send()
+
+    @pl.loop(1, 32)
+    def _(k):
+        remote(sm.at[pl.ds(0, 8)], smr.at[k], sm_s.at[k], sm_r.at[k], (s, other)).wait_send()
+        remote(ag.at[me], ag.at[me], ag_s.at[k], ag_r.at[k], (s, other)).wait_send()
+
+    @pl.loop(1, 4)
+    def _(k):
+        remote(fl.at[0], flr.at[k], fl_s.at[k], fl_r.at[k], (s, other)).wait_send()
+
+    for copy in stores:
+        copy.wait()
+
+
+def finish_kernel(
+    i_out, i_gtok, i_gin, i_gout, i_gup, i_gdown, small,
+    out, gtok, gain, shift, gin, in_b, conv_w, conv_b, first, hidden, bias, freq,
+    last, decay, skip, gout, out_b, gup, up_b, gdown, down_b, sem,
+):
+    copies = [
+        pltpu.make_async_copy(a, b, sem.at[i])
+        for i, (a, b) in enumerate(
+            (
+                (i_out, out.at[0]),
+                (i_gtok, gtok.at[0]),
+                (i_gin, gin),
+                (i_gout, gout),
+                (i_gup, gup),
+                (i_gdown, gdown),
+            )
+        )
+    ]
+    for copy in copies:
+        copy.start()
+
+    def row(at_row):
+        return small[at_row // 8, at_row % 8 : at_row % 8 + 1, :]
+
+    def fetch(at_row, dest, dest_row, wide):
+        for j in range(wide):
+            dest[dest_row : dest_row + 1, 128 * j : 128 * j + 128] = row(at_row + j)
+
+    for i in range(2):
+        fetch(AT_GAIN + 6 * i, gain, i, 6)
+        fetch(AT_SHIFT + 6 * i, shift, i, 6)
+    for i in range(3):
+        fetch(AT_CONVW + 18 * i, conv_w, i, 18)
+    fetch(AT_IN, in_b, 0, 18)
+    fetch(AT_CONVB, conv_b, 0, 18)
+    fetch(AT_SKIP, skip, 0, 6)
+    fetch(AT_OUTB, out_b, 0, 6)
+    fetch(AT_UPB, up_b, 0, 24)
+    fetch(AT_DOWNB, down_b, 0, 6)
+    rows = jnp.concatenate([small[i, 0:8, :] for i in range(32)], axis=0)
+    for i in range(2):
+        hidden[i] = rows[AT_HID : AT_HID + 64, 64 * i : 64 * i + 64]
+    first[...] = rows[AT_FIRST : AT_FIRST + 33, 0:64]
+    bias[...] = rows[AT_FIRST : AT_FIRST + 3, 64:128]
+    freq[...] = rows[AT_FIRST + 3 : AT_FIRST + 6, 64:128]
+    lasts, rates = [], []
+    for i in range(8):
+        mine = jnp.concatenate([small[4 * i + j, 8:24, :] for j in range(4)], axis=0)
+        lasts.append(mine[:, :96])
+        rates += [mine[j : j + 1, 96:128] for j in range(3)]
+    last[...] = jnp.concatenate(lasts, axis=1)
+    decay[...] = jnp.concatenate(rates, axis=1)
+    for copy in copies:
+        copy.wait()
+
+
+def one_kernel_body(tokens, out_grad, norm_gain, norm_bias, in_weight, in_bias, conv_weight, conv_bias,
+                    filt_first, filt_hidden, filt_bias, filt_freq, filt_last, decay_rates, skip_scale,
+                    out_weight, out_bias, up_weight, up_bias, down_weight, down_bias):
+    width, hidden = up_weight.shape
+    length = tokens.shape[1] * lax.axis_size("seq")
+    any_spec = pl.BlockSpec(memory_space=pl.ANY)
+    vmem_spec = pl.BlockSpec(memory_space=pltpu.VMEM)
+
+    def row(v):
+        return v.reshape(1, -1)
+
+    def vm(*shape, dtype=f32):
+        return pltpu.VMEM(shape, dtype)
+
+    def vb(*shape):
+        return pltpu.VMEM(shape, bf16)
+
+    def dma(*shape):
+        return pltpu.SemaphoreType.DMA(shape)
+
+    def shape(*dims):
+        return jax.ShapeDtypeStruct(dims, f32)
+
+    scratch = [
+        vb(width, 3 * width), vb(width, width), vb(width, hidden), vb(hidden, width), vb(4, 256, 256),
+        vb(144, width), vb(144, width), vm(128, width), vm(128, 1), vm(144, 3 * width),
+        vm(128, width), vm(128, width), vm(128, width), vm(128, width),
+        vb(4, 128, 1024), vb(128, 1024), vm(256, 1024), vm(256, 1024), vm(256, 1024), vb(128, 1024),
+        vm(1024, 128), vm(1024, 128), vb(512, 1024),
+        vm(64, 1024), vm(64, 1024), vm(64, 1024), vm(64, 1024), vm(64, 1024), vm(64, 1024),
+        vm(64, 1024), vm(64, 1024), vm(64, 1024),
+        vm(128, hidden), vb(128, hidden), vm(128, width), vm(128, width), vm(128, 1),
+        vm(128, width), vm(128, width), vm(128, width), vm(128, width),
+        vb(2, 1536, 128), vb(2, 384, 128), vb(2, 384, 128), vb(2, 384, 128),
+        vb(1536, 256), vb(384, 256), vb(384, 256), vb(384, 256),
+        vb(256, width), vb(256, hidden), vb(256, 3 * width), vb(256, width),
+        vb(8, 192, 768), vb(8, 192, 768), vb(8, 192, 768), vb(8, 96, 768), vb(8, 96, 768),
+        vb(8, 4, 48, 384), vb(8, 3, 48, 384),
+        vb(3, 768, 256), vb(3, 768, 256), vb(3, 768, 256), vb(3, 384, 256), vb(3, 384, 256),
+        vb(3, 4, 96, 256), vb(3, 3, 96, 256),
+        vb(128, 1024), vb(128, 1024), vm(136, 3 * width), vm(256, 1024), vm(1024, 128),
+        vm(256, 128), vm(32, 8, 128), vm(4, 16, 128), vm(4, 16, 128), vm(32, 24, 128),
+        vm(432, 128), vm(144, 128), vm(576, 128), vm(576, 128), vm(128, width), vm(128, width),
+        dma(7), dma(4, 7), dma(4, 7), dma(2), dma(2), dma(8), dma(8),
+        dma(11), dma(11), dma(11), dma(11), dma(11, 3), dma(11, 3),
+        dma(32), dma(32), dma(4), dma(4), dma(32), dma(32), dma(7),
+    ]
+    outs = pl.pallas_call(
+        step_kernel,
+        out_shape=[
+            shape(128, width), shape(128, width), shape(432, 128), shape(144, 128),
+            shape(576, 128), shape(576, 128), shape(32, 24, 128),
+        ],
+        in_specs=[any_spec] * 7 + [vmem_spec] * 16,
+        out_specs=[any_spec] * 7,
+        scratch_shapes=scratch,
+        compiler_params=pltpu.CompilerParams(
+            collective_id=0, has_side_effects=True, vmem_limit_bytes=62 * 1024 * 1024
+        ),
+        name="hyena_step",
+    )(
+        tokens, out_grad, in_weight, out_weight, up_weight, down_weight,
+        jnp.asarray(fourier_tables()),
+        jnp.asarray(feature_table(length, (filt_first.shape[0] - 1) // 2)),
+        norm_gain, norm_bias, row(in_bias), conv_weight, row(conv_bias), filt_first, filt_hidden,
+        filt_bias, filt_freq, filt_last, row(decay_rates), row(skip_scale), row(out_bias),
+        row(up_bias), row(down_bias),
+    )
+    done = pl.pallas_call(
+        finish_kernel,
+        out_shape=[
+            shape(1, 128, width), shape(1, 128, width), shape(2, width), shape(2, width), shape(432, 128),
+            shape(1, 3 * width), shape(3, 3 * width), shape(1, 3 * width), shape(33, 64), shape(2, 64, 64),
+            shape(3, 64), shape(3, 64), shape(64, width), shape(1, width), shape(1, width), shape(144, 128),
+            shape(1, width), shape(576, 128), shape(1, hidden), shape(576, 128), shape(1, width),
+        ],
+        in_specs=[any_spec] * 6 + [vmem_spec],
+        out_specs=[any_spec, any_spec, vmem_spec, vmem_spec, any_spec]
+        + [vmem_spec] * 10
+        + [any_spec, vmem_spec, any_spec, vmem_spec, any_spec, vmem_spec],
+        scratch_shapes=[dma(6)],
+        name="hyena_finish",
+    )(*outs)
+    flat = (4, 5, 7, 13, 14, 15, 16, 17, 18, 19, 20)
+    return tuple(v.reshape(-1) if i in flat else v for i, v in enumerate(done))
+
+
 def solution(mesh):
+    small_mesh = mesh.shape["seq"] == 8 and mesh.shape["grp"] == 4
     return jax.shard_map(
-        body,
+        one_kernel_body if small_mesh else body,
         mesh=mesh,
-        in_specs=(
-            P("grp", "seq", None),
-            P("grp", "seq", None),
-            P(),
-            P(),
-            P(),
-            P(),
-            P(),
-            P(),
-            P(),
-            P(),
-            P(),
-            P(),
-            P(),
-            P(),
-            P(),
-            P(),
-            P(),
-            P(),
-            P(),
-            P(),
-            P(),
-        ),
+        in_specs=(P("grp", "seq", None), P("grp", "seq", None)) + (P(),) * 19,
         out_specs=(
             P("grp", "seq", None),
             P("grp", "seq", None),
             P(),
             P(),
             P(("seq", "grp")),
-            P(),
-            P(),
-            P(),
-            P(),
-            P(),
-            P(),
-            P(),
-            P(),
-            P(),
-            P(),
-            P(("seq", "grp")),
-            P(),
-            P(("seq", "grp")),
-            P(),
-            P(("seq", "grp")),
-            P(),
-        ),
+        )
+        + (P(),) * 10
+        + (P(("seq", "grp")), P(), P(("seq", "grp")), P(), P(("seq", "grp")), P()),
         check_vma=False,
     )

time: 1200 us -> 207 us (0.17); the launches traced: 1180 us -> 206 us
  waiting for transfers between devices: 575 us -> 0 us
  matrix products: 318 us -> 0 us
  Pallas kernels: 0 us -> 190 us
  local copies, waits for them, and re-layouts: 148 us -> 7.69 us
  other arithmetic: 78.9 us -> 7.8 us
  starting transfers between devices: 38.4 us -> 0 us
  between operations: 15.7 us -> 0.68 us
    unnamed x3 -> x0, waiting for transfers between devices: 437 us -> none
    dot_general x210 -> x0, matrix products: 318 us -> none  [the longest x164 218 us: highest(): jnp.dot(left_mat, right_mat, precision=lax.Precision.HIGHEST, preferred_e...]
    pallas_call x0 -> x2, Pallas kernels: none -> 190 us  [the longest x1 136 us: one_kernel_body(): pl.pallas_call(step_kernel, out_shape=[shape(128, width), shape(128, widt...]
    psum x1 -> x0, waiting for transfers between devices: 137 us -> none  [body(): lax.psum((jnp.stack([g_gain_one, g_gain_two]), jnp.stack([g_shift_one, g_...]
    unnamed x235 -> x0, local copies, waits for them, and re-layouts: 54.4 us -> none
    ppermute x16 -> x0, starting transfers between devices: 38.4 us -> none  [shifted(): return lax.ppermute(array, axis, pairs)]
    while x434 -> x0, local copies, waits for them, and re-layouts: 33.9 us -> none
    add x15 -> x0, local copies, waits for them, and re-layouts: 20.3 us -> none  [filter_rows(): highest(act_two, filt_hidden[1]) + filt_bias[2]]
  transfers between devices with their start and end apart: 18 -> 0, of which waited for: 4 -> 0; matrix products, arithmetic and copies ran while one was open for 21% -> 0% of each run, Pallas kernels for 0% -> 0%
where the time goes in v1:
time: 207 us; the launch traced here: 206 us
  Pallas kernels  190 us (92%)
  other arithmetic  7.8 us (4%)
  local copies, waits for them, and re-layouts  7.69 us (4%)
    pallas_call x1, Pallas kernels, one_kernel_body(): pl.pallas_call(step_kernel, out_shape=[shape(128, width), shape(128, widt...  136 us
    pallas_call x1, Pallas kernels, one_kernel_body(): pl.pallas_call(finish_kernel, out_shape=[shape(1, 128, width), shape(1, 1...  53.5 us
    pallas_call x6, other arithmetic, one_kernel_body(): pl.pallas_call(finish_kernel, out_shape=[shape(1, 128, width), shape(1, 1...  7.8 us
    reshape x6, local copies, waits for them, and re-layouts, row(): return v.reshape(1, -1)  7.69 us

profile of v1, /device:TPU:0, one launch (start us, length us, event | category | flops | bytes accessed | tf_op | source)
XLA Modules:
  0.0 205.9 jit_solution(1467739864762280679)
XLA Ops:
  0.7 1.3 reshape.98.decay
  1.9 1.3 reshape.99.skip
  3.2 1.3 reshape.100.out_b
  4.5 1.3 reshape.102.down_b
  5.7 1.3 reshape.96.in_b
  7.0 1.3 reshape.97.conv_b
  8.3 136.2 %hyena_step.1 = (f32[128,768]{1,0:T(8,128)}, f32[128,768]{1,0:T(8,128)}, f32[432,128]{1,0:T(8,128)}, f32[144,128]{1,0:T(8,128)}, f32[576,128]{1,0:T(8,128)}, /*index=5*/f32[576,128]{1,0:T(8,128)}, f32[32,24,128]{2,1,0:T(8,128)}) custom-call(bf16[1,128,768]{2,1,0:T(8,128)(2,1)} %tokens.1, bf16[1,128,768]{2,1,0:T(8,128)(2,1)} %out_grad.1, ...), custom_call_target="tpu_custom_call" | custom-call | tf_op jit(solution)/shard_map/hyena_step/pallas_call | solution.py:1233
  144.5 53.5 %hyena_finish.1 = (f32[1,128,768]{2,1,0:T(8,128)}, f32[1,128,768]{2,1,0:T(8,128)}, f32[2,768]{1,0:T(2,128)}, f32[2,768]{1,0:T(2,128)}, f32[432,128]{1,0:T(8,128)...) custom-call(f32[128,768]{1,0:T(8,128)} %get-tuple-element.49.i_out, ...), custom_call_target="tpu_custom_call" | custom-call | tf_op jit(solution)/shard_map/hyena_finish/pallas_call | solution.py:1254
  198.1 1.3 reduce.2
  199.4 1.3 reduce.3
  200.7 1.3 reduce.4
  201.9 1.3 reduce.5
  203.2 1.3 reduce
  204.6 1.3 reduce.1

commit v2 on v1

--- a/solution.py
+++ b/solution.py
@@ -425,10 +425,10 @@
 
 def step_kernel(
     tokens, out_grad, in_w_h, out_w_h, up_w_h, down_w_h, tables_h, feats,
-    norm_gain, norm_bias, in_b, conv_w, conv_b, filt_first, filt_hidden, filt_bias,
-    filt_freq, filt_last, decay, skip, out_b, up_b, down_b,
+    norm_gain, norm_bias, in_b1, conv_w, conv_b1, filt_first, filt_hidden, filt_bias,
+    filt_freq, filt_last, decay1, skip1, out_b1, up_b1, down_b1,
     o_out, o_gtok, o_gin, o_gout, o_gup, o_gdown, o_small,
-    in_w, out_w, up_w, down_w, tables,
+    in_w, out_w, up_w, down_w, tables, in_b, conv_b, decay, skip, out_b, up_b, down_b,
     tok, n1, hat1, std1, pp, outer, inner, value, gf,
     stage, gat, xs, es, ys, co_in, taps, wind, hwin,
     a1, a2, a3, c1, c2, c3, u1, u2, u3,
@@ -487,6 +487,12 @@
     ]
     for copy in loads:
         copy.start()
+
+    for line, flat in (
+        (in_b, in_b1), (conv_b, conv_b1), (decay, decay1), (skip, skip1),
+        (out_b, out_b1), (up_b, up_b1), (down_b, down_b1),
+    ):
+        line[...] = flat[...].reshape(line.shape)
 
     def pair(index, src, dst):
         return remote(src, dst, pair_s.at[index], pair_r.at[index], (s, other))
@@ -1128,45 +1134,50 @@
 
 
 def finish_kernel(
-    i_out, i_gtok, i_gin, i_gout, i_gup, i_gdown, small,
+    i_out, i_gtok, i_gin, i_gout, i_gup, i_gdown, i_small,
     out, gtok, gain, shift, gin, in_b, conv_w, conv_b, first, hidden, bias, freq,
-    last, decay, skip, gout, out_b, gup, up_b, gdown, down_b, sem,
+    last, decay, skip, gout, out_b, gup, up_b, gdown, down_b,
+    h_out, h_gtok, h_gin, h_gout, h_gup, h_gdown, small, sem_in, sem_out,
 ):
-    copies = [
-        pltpu.make_async_copy(a, b, sem.at[i])
-        for i, (a, b) in enumerate(
-            (
-                (i_out, out.at[0]),
-                (i_gtok, gtok.at[0]),
-                (i_gin, gin),
-                (i_gout, gout),
-                (i_gup, gup),
-                (i_gdown, gdown),
-            )
-        )
+    bulk = (
+        (i_small, small, None),
+        (i_out, h_out, out.at[0]),
+        (i_gtok, h_gtok, gtok.at[0]),
+        (i_gin, h_gin, gin),
+        (i_gout, h_gout, gout),
+        (i_gup, h_gup, gup),
+        (i_gdown, h_gdown, gdown),
+    )
+    enter = [pltpu.make_async_copy(a, b, sem_in.at[i]) for i, (a, b, _) in enumerate(bulk)]
+    leave = [
+        pltpu.make_async_copy(b, d, sem_out.at[i]) for i, (_, b, d) in enumerate(bulk) if i > 0
     ]
-    for copy in copies:
+    for copy in enter:
         copy.start()
-
-    def row(at_row):
-        return small[at_row // 8, at_row % 8 : at_row % 8 + 1, :]
+    for i in range(6):
+        enter[i + 1].wait()
+        leave[i].start()
+    enter[0].wait()
+    rows = jnp.concatenate([small[i, 0:8, :] for i in range(32)], axis=0)
 
     def fetch(at_row, dest, dest_row, wide):
         for j in range(wide):
-            dest[dest_row : dest_row + 1, 128 * j : 128 * j + 128] = row(at_row + j)
+            dest[dest_row : dest_row + 1, 128 * j : 128 * j + 128] = rows[at_row + j : at_row + j + 1]
+
+    def line(at_row, dest):
+        dest[...] = rows[at_row : at_row + dest.shape[0] // 128].reshape(dest.shape[0])
 
     for i in range(2):
         fetch(AT_GAIN + 6 * i, gain, i, 6)
         fetch(AT_SHIFT + 6 * i, shift, i, 6)
     for i in range(3):
         fetch(AT_CONVW + 18 * i, conv_w, i, 18)
-    fetch(AT_IN, in_b, 0, 18)
-    fetch(AT_CONVB, conv_b, 0, 18)
-    fetch(AT_SKIP, skip, 0, 6)
-    fetch(AT_OUTB, out_b, 0, 6)
-    fetch(AT_UPB, up_b, 0, 24)
-    fetch(AT_DOWNB, down_b, 0, 6)
-    rows = jnp.concatenate([small[i, 0:8, :] for i in range(32)], axis=0)
+    line(AT_IN, in_b)
+    line(AT_CONVB, conv_b)
+    line(AT_SKIP, skip)
+    line(AT_OUTB, out_b)
+    line(AT_UPB, up_b)
+    line(AT_DOWNB, down_b)
     for i in range(2):
         hidden[i] = rows[AT_HID : AT_HID + 64, 64 * i : 64 * i + 64]
     first[...] = rows[AT_FIRST : AT_FIRST + 33, 0:64]
@@ -1178,8 +1189,11 @@
         lasts.append(mine[:, :96])
         rates += [mine[j : j + 1, 96:128] for j in range(3)]
     last[...] = jnp.concatenate(lasts, axis=1)
-    decay[...] = jnp.concatenate(rates, axis=1)
-    for copy in copies:
+    rate = jnp.concatenate(rates, axis=1)
+    decay[...] = jnp.concatenate(
+        [rate[:, 128 * j : 128 * j + 128] for j in range(6)], axis=0
+    ).reshape(768)
+    for copy in leave:
         copy.wait()
 
 
@@ -1191,9 +1205,6 @@
     any_spec = pl.BlockSpec(memory_space=pl.ANY)
     vmem_spec = pl.BlockSpec(memory_space=pltpu.VMEM)
 
-    def row(v):
-        return v.reshape(1, -1)
-
     def vm(*shape, dtype=f32):
         return pltpu.VMEM(shape, dtype)
 
@@ -1208,6 +1219,7 @@
 
     scratch = [
         vb(width, 3 * width), vb(width, width), vb(width, hidden), vb(hidden, width), vb(4, 256, 256),
+        vm(1, 3 * width), vm(1, 3 * width), vm(1, width), vm(1, width), vm(1, width), vm(1, hidden), vm(1, width),
         vb(144, width), vb(144, width), vm(128, width), vm(128, 1), vm(144, 3 * width),
         vm(128, width), vm(128, width), vm(128, width), vm(128, width),
         vb(4, 128, 1024), vb(128, 1024), vm(256, 1024), vm(256, 1024), vm(256, 1024), vb(128, 1024),
@@ -1247,26 +1259,29 @@
         tokens, out_grad, in_weight, out_weight, up_weight, down_weight,
         jnp.asarray(fourier_tables()),
         jnp.asarray(feature_table(length, (filt_first.shape[0] - 1) // 2)),
-        norm_gain, norm_bias, row(in_bias), conv_weight, row(conv_bias), filt_first, filt_hidden,
-        filt_bias, filt_freq, filt_last, row(decay_rates), row(skip_scale), row(out_bias),
-        row(up_bias), row(down_bias),
+        norm_gain, norm_bias, in_bias, conv_weight, conv_bias, filt_first, filt_hidden,
+        filt_bias, filt_freq, filt_last, decay_rates, skip_scale, out_bias, up_bias, down_bias,
     )
     done = pl.pallas_call(
         finish_kernel,
         out_shape=[
             shape(1, 128, width), shape(1, 128, width), shape(2, width), shape(2, width), shape(432, 128),
-            shape(1, 3 * width), shape(3, 3 * width), shape(1, 3 * width), shape(33, 64), shape(2, 64, 64),
-            shape(3, 64), shape(3, 64), shape(64, width), shape(1, width), shape(1, width), shape(144, 128),
-            shape(1, width), shape(576, 128), shape(1, hidden), shape(576, 128), shape(1, width),
+            shape(3 * width), shape(3, 3 * width), shape(3 * width), shape(33, 64), shape(2, 64, 64),
+            shape(3, 64), shape(3, 64), shape(64, width), shape(width), shape(width), shape(144, 128),
+            shape(width), shape(576, 128), shape(hidden), shape(576, 128), shape(width),
         ],
-        in_specs=[any_spec] * 6 + [vmem_spec],
+        in_specs=[any_spec] * 7,
         out_specs=[any_spec, any_spec, vmem_spec, vmem_spec, any_spec]
         + [vmem_spec] * 10
         + [any_spec, vmem_spec, any_spec, vmem_spec, any_spec, vmem_spec],
-        scratch_shapes=[dma(6)],
+        scratch_shapes=[
+            vm(128, width), vm(128, width), vm(432, 128), vm(144, 128), vm(576, 128), vm(576, 128),
+            vm(32, 24, 128), dma(7), dma(7),
+        ],
+        compiler_params=pltpu.CompilerParams(vmem_limit_bytes=32 * 1024 * 1024),
         name="hyena_finish",
     )(*outs)
-    flat = (4, 5, 7, 13, 14, 15, 16, 17, 18, 19, 20)
+    flat = (4, 15, 17, 19)
     return tuple(v.reshape(-1) if i in flat else v for i, v in enumerate(done))
 
 

time: 207 us -> 147 us (0.71)
  Pallas kernels: 190 us -> 140 us
  other arithmetic: 7.8 us -> 0 us
    pallas_call x1, Pallas kernels: 53.5 us -> 3.29 us  [one_kernel_body(): pl.pallas_call(finish_kernel, out_shape=[shape(1, 128, width), shape(1, 1...]
    pallas_call x6 -> x0, other arithmetic: 7.8 us -> none  [one_kernel_body(): pl.pallas_call(finish_kernel, out_shape=[shape(1, 128, width), shape(1, 1...]
    reshape x6 -> x0, local copies, waits for them, and re-layouts: 7.69 us -> none  [row(): return v.reshape(1, -1)]
    unnamed x0 -> x14, local copies, waits for them, and re-layouts: none -> 6.72 us
where the time goes in v2:
time: 147 us
  Pallas kernels  140 us (95%)
  local copies, waits for them, and re-layouts  6.72 us (5%)
    pallas_call x1, Pallas kernels, one_kernel_body(): pl.pallas_call(step_kernel, out_shape=[shape(128, width), shape(128, widt...  136 us
    unnamed x14, local copies, waits for them, and re-layouts  6.72 us
    pallas_call x1, Pallas kernels, one_kernel_body(): pl.pallas_call(finish_kernel, out_shape=[shape(1, 128, width), shape(1, 1...  3.29 us

profile of v2, /device:TPU:0, one launch (start us, length us, event | category | flops | bytes accessed | tf_op | source)
XLA Modules:
  0.0 147.1 jit_solution(2678384148754583520)
XLA Ops:
  0.7 136.2 %hyena_step.1 = (f32[128,768]{1,0:T(8,128)}, f32[128,768]{1,0:T(8,128)}, f32[432,128]{1,0:T(8,128)}, f32[144,128]{1,0:T(8,128)}, f32[576,128]{1,0:T(8,128)}, /*index=5*/f32[576,128]{1,0:T(8,128)}, f32[32,24,128]{2,1,0:T(8,128)}) custom-call(bf16[1,128,768]{2,1,0:T(8,128)(2,1)} %tokens.1, bf16[1,128,768]{2,1,0:T(8,128)(2,1)} %out_grad.1, ...), custom_call_target="tpu_custom_call" | custom-call | tf_op jit(solution)/shard_map/hyena_step/pallas_call | solution.py:1245
  136.9 0.0 copy-start
  136.9 1.0 copy-done
  137.9 0.0 copy-start.1
  137.9 1.0 copy-done.1
  138.9 0.0 copy-start.2
  138.9 1.0 copy-done.2
  139.9 0.0 copy-start.3
  139.9 1.0 copy-done.3
  140.9 0.0 copy-start.4
  140.9 1.0 copy-done.4
  141.8 0.0 copy-start.5
  141.8 0.9 copy-done.5
  142.8 0.0 copy-start.6
  142.8 0.9 copy-done.6
  143.6 3.3 %hyena_finish.1 = (f32[1,128,768]{2,1,0:T(8,128)}, f32[1,128,768]{2,1,0:T(8,128)}, f32[2,768]{1,0:T(2,128)}, f32[2,768]{1,0:T(2,128)}, f32[432,128]{1,0:T(8,128)...) custom-call(f32[128,768]{1,0:T(8,128)S(1)} %copy-done, ...), custom_call_target="tpu_custom_call" | custom-call | tf_op jit(solution)/shard_map/hyena_finish/pallas_call | solution.py:1265
Async XLA Ops:
  136.9 1.0 copy-start
  137.9 1.0 copy-start.1
  138.9 1.0 copy-start.2
  139.9 1.0 copy-start.3
  140.9 1.0 copy-start.4
  141.8 0.9 copy-start.5
  142.8 0.9 copy-start.6

commit v3 on v2

v3 whole, which is shorter than its diff:
```python
import math
import types

import jax
import jax.numpy as jnp
import ml_dtypes
import numpy as np
from jax import lax
from jax.experimental import pallas as pl
from jax.experimental.pallas import tpu as pltpu
from jax.sharding import PartitionSpec as P

epsilon = 1e-05


def shifted(array, axis, by):
    peers = lax.axis_size(axis)
    pairs = [(i, i + by) for i in range(peers) if 0 <= i + by < peers]
    return lax.ppermute(array, axis, pairs)


def highest(left_mat, right_mat):
    return jnp.dot(
        left_mat, right_mat, precision=lax.Precision.HIGHEST, preferred_element_type=jnp.float32
    )


def highest_t(left_mat, right_mat):
    return lax.dot_general(
        left_mat,
        right_mat,
        (((0,), (0,)), ((), ())),
        precision=lax.Precision.HIGHEST,
        preferred_element_type=jnp.float32,
    )


def rows_t(left_mat, right_mat):
    return lax.dot_general(
        left_mat, right_mat, (((0,), (0,)), ((), ())), preferred_element_type=jnp.float32
    )


def back_mul(grad_in, weight_mat):
    return lax.dot_general(
        grad_in, weight_mat, (((1,), (1,)), ((), ())), preferred_element_type=jnp.float32
    )


def layer_norm(values, gain_row, shift_row):
    row_mean = jnp.mean(values, axis=-1, keepdims=True)
    centred = values - row_mean
    inv_std = lax.rsqrt(jnp.mean(centred * centred, axis=-1, keepdims=True) + epsilon)
    normed = centred * inv_std
    return (normed * gain_row + shift_row, normed, inv_std)


def norm_back(grad_in, normed, inv_std, gain_row):
    scaled = grad_in * gain_row
    centred_grad = (
        scaled
        - jnp.mean(scaled, axis=-1, keepdims=True)
        - normed * jnp.mean(scaled * normed, axis=-1, keepdims=True)
    )
    return (centred_grad * inv_std, jnp.sum(grad_in * normed, axis=0), jnp.sum(grad_in, axis=0))


def smooth(values):
    return jax.nn.gelu(values, approximate=False)


def filter_rows(params, positions, length):
    filt_first, filt_hidden, filt_bias, filt_freq, filt_last, decay_rates = params
    place = positions.astype(jnp.float32)
    bands = (filt_first.shape[0] - 1) // 2
    band = 0.0001 + jnp.arange(bands, dtype=jnp.float32) * ((bands - 1 - 0.0001) / (bands - 1))
    omega = place[:, None] * (2.0 * math.pi / length)
    phase = omega * band[None, :]
    feats = jnp.concatenate(
        [place[:, None] / (length - 1), jnp.cos(phase), -jnp.sin(phase)], axis=1
    )
    act_one = jnp.sin(filt_freq[0] * (highest(feats, filt_first) + filt_bias[0]))
    act_two = jnp.sin(filt_freq[1] * (highest(act_one, filt_hidden[0]) + filt_bias[1]))
    act_three = jnp.sin(filt_freq[2] * (highest(act_two, filt_hidden[1]) + filt_bias[2]))
    window = jnp.exp(-decay_rates[None, :] * jnp.maximum(place, 0.0)[:, None])
    return highest(act_three, filt_last) * window


def body(
    tokens,
    out_grad,
    norm_gain,
    norm_bias,
    in_weight,
    in_bias,
    conv_weight,
    conv_bias,
    filt_first,
    filt_hidden,
    filt_bias,
    filt_freq,
    filt_last,
    decay_rates,
    skip_scale,
    out_weight,
    out_bias,
    up_weight,
    up_bias,
    down_weight,
    down_bias,
):
    row_count = tokens.shape[1]
    model_width = tokens.shape[2]
    seq_count = lax.axis_size("seq")
    length = row_count * seq_count
    fft_span = 2 * row_count
    fparams = (filt_first, filt_hidden, filt_bias, filt_freq, filt_last, decay_rates)
    fft_grid = jnp.arange(fft_span, dtype=jnp.int32)
    angles = (fft_grid[:, None] * fft_grid[None, :] % fft_span).astype(jnp.float32) * (
        2.0 * math.pi / fft_span
    )
    cos_full = jnp.cos(angles)
    sin_full = jnp.sin(angles)
    cos_left = cos_full[:, :row_count]
    sin_left = sin_full[:, :row_count]
    cos_low = cos_full[row_count:, :]
    sin_low = sin_full[row_count:, :]

    def segment(params, lag_step):
        positions = (lag_step - 1) * row_count + fft_grid
        keep_mask = (positions >= 0).astype(jnp.float32)
        return filter_rows(params, positions, length) * keep_mask[:, None]

    def forward_add(lag_step, source, totals):
        filter_taps = segment(fparams, lag_step)
        g_re = highest(cos_full, filter_taps)
        g_im = -highest(sin_full, filter_taps)
        source_f = source.astype(jnp.float32)
        s_re = highest(cos_left, source_f)
        s_im = -highest(sin_left, source_f)
        return (totals[0] + g_re * s_re - g_im * s_im, totals[1] + g_re * s_im + g_im * s_re)

    inputs = tokens[0].astype(jnp.float32)
    normed1, hat_one, std_one = layer_norm(inputs, norm_gain[0], norm_bias[0])
    normed1_b = normed1.astype(jnp.bfloat16)
    projected = (
        jnp.dot(normed1_b, in_weight, preferred_element_type=jnp.float32) + in_bias
    ).astype(jnp.bfloat16)
    before = shifted(projected[row_count - 2 :], "seq", 1)
    padded = jnp.concatenate([before, projected], axis=0).astype(jnp.float32)
    mixed_conv = (
        conv_weight[0] * padded[:row_count]
        + conv_weight[1] * padded[1 : row_count + 1]
        + conv_weight[2] * padded[2:]
        + conv_bias
    )
    outer_part = mixed_conv[:, :model_width]
    inner_part = mixed_conv[:, model_width : 2 * model_width]
    value_part = mixed_conv[:, 2 * model_width :]
    gated_b = (inner_part * value_part).astype(jnp.bfloat16)
    gated_f = gated_b.astype(jnp.float32)
    zero_totals = (
        jnp.zeros((fft_span, model_width), jnp.float32),
        jnp.zeros((fft_span, model_width), jnp.float32),
    )
    first_pass = forward_add(0, gated_b, zero_totals)

    def forward_step(lag_step, loop_carry):
        source, tot_re, tot_im = loop_carry
        source = shifted(source, "seq", 1)
        tot_re, tot_im = forward_add(lag_step, source, (tot_re, tot_im))
        return (source, tot_re, tot_im)

    unused_src, tot_re, tot_im = lax.fori_loop(
        1, seq_count, forward_step, (gated_b, first_pass[0], first_pass[1])
    )
    conv_out = (highest(cos_low, tot_re) - highest(sin_low, tot_im)) / fft_span
    summed = conv_out + skip_scale * gated_f
    mixed_out_b = (outer_part * summed).astype(jnp.bfloat16)
    residual = (
        inputs + jnp.dot(mixed_out_b, out_weight, preferred_element_type=jnp.float32) + out_bias
    )
    normed2, hat_two, std_two = layer_norm(residual, norm_gain[1], norm_bias[1])
    normed2_b = normed2.astype(jnp.bfloat16)
    pre_act = jnp.dot(normed2_b, up_weight, preferred_element_type=jnp.float32) + up_bias
    act_val, gelu_back = jax.vjp(smooth, pre_act)
    act_b = act_val.astype(jnp.bfloat16)
    result = residual + jnp.dot(act_b, down_weight, preferred_element_type=jnp.float32) + down_bias
    grad_out_b = out_grad[0]
    grad_out_f = grad_out_b.astype(jnp.float32)
    g_down = rows_t(act_b, grad_out_b)
    g_down_bias = jnp.sum(grad_out_f, axis=0)
    g_act = back_mul(grad_out_b, down_weight)
    g_pre_b = gelu_back(g_act)[0].astype(jnp.bfloat16)
    g_up = rows_t(normed2_b, g_pre_b)
    g_up_bias = jnp.sum(g_pre_b.astype(jnp.float32), axis=0)
    g_norm_two = back_mul(g_pre_b, up_weight)
    g_res_norm, g_gain_two, g_shift_two = norm_back(g_norm_two, hat_two, std_two, norm_gain[1])
    g_resid = grad_out_f + g_res_norm
    g_resid_b = g_resid.astype(jnp.bfloat16)
    g_outw = rows_t(mixed_out_b, g_resid_b)
    g_out_bias = jnp.sum(g_resid_b.astype(jnp.float32), axis=0)
    g_mixed = back_mul(g_resid_b, out_weight)
    g_outer = g_mixed * summed
    g_summed = g_mixed * outer_part
    g_skip = jnp.sum(g_summed * gated_f, axis=0)
    g_conv_b = g_summed.astype(jnp.bfloat16)
    v_re = highest(cos_left, gated_f)
    v_im = -highest(sin_left, gated_f)

    def backward_add(lag_step, source, loop_carry):
        tot_re, tot_im, grad_acc = loop_carry
        source_f = source.astype(jnp.float32)
        d_re = highest_t(cos_low, source_f) / fft_span
        d_im = -highest_t(sin_low, source_f) / fft_span

        def lag_taps(params):
            return segment(params, lag_step)

        filter_taps, taps_pull = jax.vjp(lag_taps, fparams)
        g_re = highest(cos_full, filter_taps)
        g_im = -highest(sin_full, filter_taps)
        tot_re = tot_re + g_re * d_re + g_im * d_im
        tot_im = tot_im - g_im * d_re + g_re * d_im
        s_re = v_re * d_re + v_im * d_im
        s_im = v_re * d_im - v_im * d_re
        d_taps = highest_t(cos_full, s_re) - highest_t(sin_full, s_im)
        more_grads = taps_pull(d_taps)[0]
        grad_acc = jax.tree.map(jnp.add, grad_acc, more_grads)
        return (tot_re, tot_im, grad_acc)

    zero_grads = jax.tree.map(jnp.zeros_like, fparams)
    start_carry = (zero_totals[0], zero_totals[1], zero_grads)
    first_back = backward_add(0, g_conv_b, start_carry)

    def backward_step(lag_step, loop_carry):
        source, tot_re, tot_im, grad_acc = loop_carry
        source = shifted(source, "seq", -1)
        tot_re, tot_im, grad_acc = backward_add(lag_step, source, (tot_re, tot_im, grad_acc))
        return (source, tot_re, tot_im, grad_acc)

    unused_src, back_re, back_im, cycle_grads = lax.fori_loop(
        1, seq_count, backward_step, (g_conv_b,) + first_back
    )
    g_long = highest_t(cos_left, back_re) - highest_t(sin_left, back_im)
    g_gated = g_summed * skip_scale + g_long
    g_mix = jnp.concatenate([g_outer, g_gated * value_part, g_gated * inner_part], axis=1)
    g_conv_bias = jnp.sum(g_mix, axis=0)
    g_conv_w = jnp.stack(
        [
            jnp.sum(g_mix * padded[tap_index : tap_index + row_count], axis=0)
            for tap_index in range(3)
        ]
    )
    g_pad = (
        jnp.pad(conv_weight[0] * g_mix, ((0, 2), (0, 0)))
        + jnp.pad(conv_weight[1] * g_mix, ((1, 1), (0, 0)))
        + jnp.pad(conv_weight[2] * g_mix, ((2, 0), (0, 0)))
    )
    after_rows = shifted(g_pad[:2], "seq", -1)
    g_proj_b = (g_pad[2:] + jnp.pad(after_rows, ((row_count - 2, 0), (0, 0)))).astype(jnp.bfloat16)
    g_inw = rows_t(normed1_b, g_proj_b)
    g_in_bias = jnp.sum(g_proj_b.astype(jnp.float32), axis=0)
    g_norm_one = back_mul(g_proj_b, in_weight)
    g_in_norm, g_gain_one, g_shift_one = norm_back(g_norm_one, hat_one, std_one, norm_gain[0])
    g_tokens = g_resid + g_in_norm
    small_grads = lax.psum(
        (
            jnp.stack([g_gain_one, g_gain_two]),
            jnp.stack([g_shift_one, g_shift_two]),
            g_in_bias,
            g_conv_w,
            g_conv_bias,
            cycle_grads[0],
            cycle_grads[1],
            cycle_grads[2],
            cycle_grads[3],
            cycle_grads[4],
            cycle_grads[5],
            g_skip,
            g_out_bias,
            g_up_bias,
            g_down_bias,
        ),
        ("seq", "grp"),
    )
    large_grads = (
        lax.psum_scatter(g_inw.reshape(-1), ("seq", "grp"), scatter_dimension=0, tiled=True),
        lax.psum_scatter(g_outw.reshape(-1), ("seq", "grp"), scatter_dimension=0, tiled=True),
        lax.psum_scatter(g_up.reshape(-1), ("seq", "grp"), scatter_dimension=0, tiled=True),
        lax.psum_scatter(g_down.reshape(-1), ("seq", "grp"), scatter_dimension=0, tiled=True),
    )
    return (
        result[None],
        g_tokens[None],
        small_grads[0],
        small_grads[1],
        large_grads[0],
        small_grads[2],
        small_grads[3],
        small_grads[4],
        small_grads[5],
        small_grads[6],
        small_grads[7],
        small_grads[8],
        small_grads[9],
        small_grads[10],
        small_grads[11],
        large_grads[1],
        small_grads[12],
        large_grads[2],
        small_grads[13],
        large_grads[3],
        small_grads[14],
    )


f32 = jnp.float32
bf16 = jnp.bfloat16
MESH_ID = pl.DeviceIdType.MESH
HIGH = lax.Precision.HIGHEST
ROWS = 128
HALO = 16


def nn(a, b):
    return jnp.dot(a, b, preferred_element_type=f32)


def nt(a, b):
    return lax.dot_general(a, b, (((1,), (1,)), ((), ())), preferred_element_type=f32)


def nn_high(a, b):
    return jnp.dot(a, b, precision=HIGH, preferred_element_type=f32)


def nt_high(a, b):
    return lax.dot_general(
        a, b, (((1,), (1,)), ((), ())), precision=HIGH, preferred_element_type=f32
    )


def tn_high(a, b):
    return lax.dot_general(
        a, b, (((0,), (0,)), ((), ())), precision=HIGH, preferred_element_type=f32
    )


def two(v):
    high = v.astype(bf16)
    return high, (v - high.astype(f32)).astype(bf16)


def sin_cos(v):
    k = jnp.floor(v * (1.0 / math.pi) + 0.5)
    r = ((v - k * 3.140625) - k * 0.0009670257568359375) - k * 6.2771141529083252e-07
    sign = 1.0 - 2.0 * (k - 2.0 * jnp.floor(k * 0.5))
    q = r * r
    s = 1.0 / math.factorial(13)
    for order in (11, 9, 7, 5, 3):
        s = 1.0 / math.factorial(order) - s * q
    s = r - r * q * s
    c = 1.0 / math.factorial(12)
    for order in (10, 8, 6, 4, 2):
        c = 1.0 / math.factorial(order) - c * q
    c = 1.0 - q * c
    return s * sign, c * sign


def gelu_both(v):
    a = jnp.abs(v)
    t = 1.0 / (1.0 + (0.3275911 / math.sqrt(2.0)) * a)
    poly = t * (
        0.254829592
        + t * (-0.284496736 + t * (1.421413741 + t * (-1.453152027 + t * 1.061405429)))
    )
    bell = jnp.exp(-0.5 * v * v)
    tail = 0.5 * poly * bell
    phi = jnp.where(v >= 0, 1.0 - tail, tail)
    return v * phi, phi + v * bell * (1.0 / math.sqrt(2.0 * math.pi))


def col_sum(v):
    return jnp.sum(v, axis=0, keepdims=True)


def row_mean(v):
    return jnp.mean(v, axis=1, keepdims=True)


def norm_rows(v):
    centred = v - row_mean(v)
    inv = lax.rsqrt(row_mean(centred * centred) + epsilon)
    return centred * inv, inv


def norm_rows_back(e, hat, inv, gain):
    k = e * gain
    return (k - row_mean(k) - hat * row_mean(k * hat)) * inv


def fourier_tables():
    bins = np.arange(128) + 0.5
    angle = 2.0 * np.pi * bins[:, None] * np.arange(256)[None, :] / 256
    full = np.concatenate([np.cos(angle), -np.sin(angle)], axis=0).astype(np.float32)
    out = []
    for mat in (full, full.T):
        high = mat.astype(ml_dtypes.bfloat16)
        out += [high, (mat - high.astype(np.float32)).astype(ml_dtypes.bfloat16)]
    return np.stack(out)


def feature_table(length, bands):
    place = np.arange(length)
    band = 1e-4 + np.arange(bands) * ((bands - 1 - 1e-4) / (bands - 1))
    phase = band[:, None] * (2.0 * np.pi * place / length)[None, :]
    return np.concatenate(
        [(place / (length - 1))[None], np.cos(phase), -np.sin(phase)], axis=0
    ).astype(np.float32)


AT_HID, AT_FIRST, AT_GAIN, AT_SHIFT, AT_IN, AT_CONVW, AT_CONVB = 0, 64, 97, 109, 121, 139, 193
AT_SKIP, AT_OUTB, AT_UPB, AT_DOWNB = 211, 217, 223, 247

SMALL_ARGS = (
    ("norm_gain", (2, 768)), ("norm_bias", (2, 768)), ("in_b1", (2304,)), ("conv_w", (3, 2304)),
    ("conv_b1", (2304,)), ("feats", (33, 1024)), ("filt_first", (33, 64)), ("filt_hidden", (2, 64, 64)),
    ("filt_bias", (3, 64)), ("filt_freq", (3, 64)), ("filt_last", (64, 768)), ("decay1", (768,)),
    ("skip1", (768,)), ("out_b1", (768,)), ("up_b1", (3072,)), ("down_b1", (768,)),
)

SCRATCH = (
    ("in_w", (768, 2304), bf16), ("out_w", (768, 768), bf16), ("up_w", (768, 3072), bf16),
    ("down_w", (3072, 768), bf16), ("tables", (4, 256, 256), bf16),
    ("in_b", (1, 2304), f32), ("conv_b", (1, 2304), f32), ("skip", (1, 768), f32),
    ("out_b", (1, 768), f32), ("up_b", (1, 3072), f32), ("down_b", (1, 768), f32),
    ("tok", (144, 768), bf16), ("n1", (144, 768), bf16), ("hat1", (128, 768), f32),
    ("std1", (128, 1), f32), ("pp", (144, 2304), f32), ("outer", (128, 768), f32),
    ("inner", (128, 768), f32), ("value", (128, 768), f32), ("gf", (128, 768), f32),
    ("stage", (4, 768, 128), bf16), ("gat", (768, 128), bf16), ("co_in", (768, 128), bf16),
    ("gc_in", (768, 128), bf16), ("gl_in", (768, 128), bf16),
    ("xs", (768, 256), f32), ("es", (768, 256), f32), ("ys", (768, 256), f32),
    ("gtap", (768, 256), f32), ("hw_high", (768, 256), bf16), ("hw_low", (768, 256), bf16),
    ("taps", (96, 1024), f32), ("wind", (96, 1024), f32), ("dpre", (96, 1024), f32),
    ("last_t", (768, 64), f32), ("rate_t", (768, 8), f32),
    ("a1", (64, 1024), f32), ("a2", (64, 1024), f32), ("a3", (64, 1024), f32),
    ("c1", (64, 1024), f32), ("c2", (64, 1024), f32), ("c3", (64, 1024), f32),
    ("u1", (64, 1024), f32), ("u2", (64, 1024), f32), ("u3", (64, 1024), f32),
    ("g_act", (128, 3072), f32), ("act", (128, 3072), bf16), ("summed", (128, 768), f32),
    ("hat2", (128, 768), f32), ("std2", (128, 1), f32), ("resid", (128, 768), f32),
    ("g_resid", (128, 768), f32), ("g_sum", (128, 768), f32), ("g_outer", (128, 768), f32),
    ("gm", (136, 2304), f32),
    ("at_down", (2, 1536, 128), bf16), ("at_up", (2, 384, 128), bf16), ("at_in", (2, 384, 128), bf16),
    ("at_out", (2, 384, 128), bf16), ("lh_down", (768, 512), bf16), ("lh_up", (384, 256), bf16),
    ("lh_in", (384, 256), bf16), ("lh_out", (384, 256), bf16), ("rh_down", (512, 768), bf16),
    ("rh_up", (256, 3072), bf16), ("rh_in", (256, 2304), bf16), ("rh_out", (256, 768), bf16),
    ("s1a", (8, 192, 768), bf16), ("k1a", (8, 192, 768), f32), ("r1a", (8, 192, 768), bf16),
    ("s2a", (8, 96, 768), bf16), ("r2a", (8, 96, 768), bf16), ("zsa", (8, 4, 48, 384), bf16),
    ("zra", (8, 3, 48, 384), bf16), ("s2b", (3, 384, 256), bf16), ("k2b", (3, 384, 256), f32),
    ("r2b", (3, 384, 256), bf16), ("zsb", (3, 4, 96, 256), bf16), ("zrb", (3, 3, 96, 256), bf16),
    ("smf", (4, 88, 128), f32), ("q_in", (3, 88, 128), f32), ("q_sum", (88, 128), f32),
    ("o_in", (7, 8, 128), f32), ("ag", (4, 8, 32, 128), f32),
    ("f_gin", (432, 128), f32), ("f_gout", (144, 128), f32), ("f_gup", (576, 128), f32),
    ("f_gdown", (576, 128), f32), ("f_out", (128, 768), f32), ("f_gtok", (128, 768), f32),
)

SEMAPHORES = (
    ("ld", (8,)), ("ls", (16,)), ("a2a_s", (4, 7)), ("a2a_r", (4, 7)), ("halo_s", (2,)), ("halo_r", (2,)),
    ("pair_s", (12,)), ("pair_r", (12,)), ("p1_s", (8,)), ("p1_r", (8,)), ("p2_s", (11,)),
    ("p2_r", (11,)), ("z_s", (11, 3)), ("z_r", (11, 3)), ("q_s", (3,)), ("q_r", (3,)),
    ("o_s", (7,)), ("o_r", (7,)), ("ag_s", (10,)), ("ag_r", (10,)), ("st", (7,)),
)


def step_kernel(*refs):
    names = ["tokens", "out_grad", "in_w_h", "out_w_h", "up_w_h", "down_w_h", "tables_h"]
    names += ["h_" + name for name, _ in SMALL_ARGS]
    names += ["o_out", "o_gtok", "o_gin", "o_gout", "o_gup", "o_gdown", "o_small"]
    names += [name for name, _ in SMALL_ARGS]
    names += [name for name, _, _ in SCRATCH] + [name for name, _ in SEMAPHORES]
    r = types.SimpleNamespace(**dict(zip(names, refs, strict=True)))

    s = lax.axis_index("seq")
    g = lax.axis_index("grp")
    z, x = lax.div(s, 2), lax.rem(s, 2)
    y, c = lax.div(g, 2), lax.rem(g, 2)
    other = g + 1 - 2 * c
    x_step, y_step = 1 - 2 * x, 2 * (1 - 2 * y)
    first = (s + (1 - c) * x_step, g + c * y_step)
    second = (s + c * x_step, g + (1 - c) * y_step)
    cross = (s + c * x_step, other + (1 - c) * y_step)
    b1 = (1 - c) * x + c * y
    b2 = (1 - c) * y + c * x

    def at(index, size):
        return pl.ds(pl.multiple_of(index * size, size), size)

    def remote(src, dst, ss, rs, where):
        return pltpu.make_async_remote_copy(
            src_ref=src,
            dst_ref=dst,
            send_sem=ss,
            recv_sem=rs,
            device_id=where,
            device_id_type=MESH_ID,
        )

    bar = pltpu.get_barrier_semaphore()

    @pl.loop(1, 8)
    def _(k):
        pl.semaphore_signal(
            bar, inc=1, device_id=(lax.rem(s + k, 8), g), device_id_type=MESH_ID
        )

    @pl.loop(1, 4)
    def _(k):
        pl.semaphore_signal(
            bar, inc=1, device_id=(s, lax.rem(g + k, 4)), device_id_type=MESH_ID
        )

    pl.semaphore_signal(bar, inc=1, device_id=(s + x_step, other), device_id_type=MESH_ID)

    own = pl.ds(0, ROWS)
    loads = [
        pltpu.make_async_copy(r.tokens.at[0], r.tok.at[pl.ds(HALO, ROWS)], r.ld.at[0]),
        pltpu.make_async_copy(r.in_w_h, r.in_w, r.ld.at[1]),
        pltpu.make_async_copy(r.out_grad.at[0], r.rh_down.at[own], r.ld.at[2]),
        pltpu.make_async_copy(r.tables_h, r.tables, r.ld.at[3]),
        pltpu.make_async_copy(r.down_w_h, r.down_w, r.ld.at[4]),
        pltpu.make_async_copy(r.out_w_h, r.out_w, r.ld.at[5]),
        pltpu.make_async_copy(r.up_w_h, r.up_w, r.ld.at[6]),
    ]
    small_loads = [
        pltpu.make_async_copy(getattr(r, "h_" + name), getattr(r, name), r.ls.at[i])
        for i, (name, _) in enumerate(SMALL_ARGS)
    ]
    loads[0].start()
    for copy in small_loads[:2]:
        copy.start()
    loads[1].start()
    for copy in small_loads[2:]:
        copy.start()
    loads[2].start()
    loads[3].start()

    def share(index, src, dst, where):
        return remote(src, dst, r.pair_s.at[index], r.pair_r.at[index], where)

    block2, block3, block4 = pl.ds(ROWS, ROWS), pl.ds(2 * ROWS, ROWS), pl.ds(3 * ROWS, ROWS)
    shares = [
        share(0, r.rh_down.at[own], r.rh_down.at[block2], (s, other)),
        share(1, r.rh_down.at[own], r.rh_down.at[block3], first),
        share(2, r.rh_down.at[own], r.rh_down.at[block4], cross),
        share(3, r.at_down.at[1 - c, at(b2, 768)], r.lh_down.at[:, block2], (s, other)),
        share(4, r.at_down.at[c, at(1 - b1, 768)], r.lh_down.at[:, block3], first),
        share(5, r.at_down.at[1 - c, at(1 - b2, 768)], r.lh_down.at[:, block4], cross),
        share(6, r.at_in.at[1 - c], r.lh_in.at[:, block2], (s, other)),
        share(7, r.at_out.at[1 - c], r.lh_out.at[:, block2], (s, other)),
        share(8, r.at_up.at[1 - c], r.lh_up.at[:, block2], (s, other)),
        share(9, r.rh_up.at[own], r.rh_up.at[block2], (s, other)),
        share(10, r.rh_out.at[own], r.rh_out.at[block2], (s, other)),
        share(11, r.rh_in.at[own], r.rh_in.at[block2], (s, other)),
    ]

    def order_rows(v, halves):
        t = jnp.transpose(v)
        for core in range(2):
            blocks = []
            for i1 in range(2):
                for i2 in range(2):
                    ix, iy = (i1, i2) if core == 0 else (i2, i1)
                    for iz in range(4):
                        at_row = 24 * (iz * 8 + ix * 4 + iy * 2 + core)
                        blocks.append(t[at_row : at_row + 24])
            halves[core] = jnp.concatenate(blocks, axis=0).astype(bf16)

    loads[0].wait()
    hat, inv = norm_rows(r.tok[pl.ds(HALO, ROWS)].astype(f32))
    r.hat1[...] = hat
    r.std1[...] = inv
    small_loads[0].wait()
    small_loads[1].wait()
    own_norm = (hat * r.norm_gain[0:1] + r.norm_bias[0:1]).astype(bf16)
    r.n1[pl.ds(HALO, ROWS)] = own_norm
    pl.semaphore_wait(bar, 11)
    last_rows = remote(
        r.tok.at[pl.ds(ROWS, HALO)],
        r.tok.at[pl.ds(0, HALO)],
        r.halo_s.at[0],
        r.halo_r.at[0],
        (s + 1, g),
    )

    @pl.when(s < 7)
    def _():
        last_rows.start()

    order_rows(own_norm.astype(f32), r.at_in)
    r.lh_in[:, own] = r.at_in[c]
    for copy in small_loads[2:]:
        copy.wait()
    for line, flat in (
        (r.in_b, r.in_b1), (r.conv_b, r.conv_b1), (r.skip, r.skip1),
        (r.out_b, r.out_b1), (r.up_b, r.up_b1), (r.down_b, r.down_b1),
    ):
        line[...] = flat[...].reshape(line.shape)

    @pl.when(s > 0)
    def _():
        last_rows.wait_recv()

    @pl.when(s == 0)
    def _():
        r.tok[pl.ds(0, HALO)] = jnp.zeros((HALO, r.tok.shape[1]), bf16)

    hat, inv = norm_rows(r.tok[pl.ds(0, HALO)].astype(f32))
    r.n1[pl.ds(0, HALO)] = (hat * r.norm_gain[0:1] + r.norm_bias[0:1]).astype(bf16)
    loads[1].wait()
    for copy in loads[4:]:
        copy.start()
    inside = jnp.where(s > 0, 1.0, 0.0).astype(f32)
    for part, dest in enumerate((r.outer, r.inner, r.value)):
        cols = pl.ds(768 * part, 768)
        proj = (nn(r.n1[...], r.in_w[:, cols]) + r.in_b[:, cols]).astype(bf16).astype(f32)
        r.pp[pl.ds(0, HALO), cols] = proj[:HALO] * inside
        r.pp[pl.ds(HALO, ROWS), cols] = proj[HALO:]
        dest[...] = (
            r.conv_w[0:1, cols] * r.pp[pl.ds(HALO - 2, ROWS), cols]
            + r.conv_w[1:2, cols] * r.pp[pl.ds(HALO - 1, ROWS), cols]
            + r.conv_w[2:3, cols] * r.pp[pl.ds(HALO, ROWS), cols]
            + r.conv_b[:, cols]
        )
    gated = (r.inner[...] * r.value[...]).astype(bf16).astype(f32)
    r.gf[...] = gated

    def trade(which, dst):
        @pl.loop(1, 8)
        def _(k):
            peer = lax.rem(s + k, 8)
            remote(
                r.stage.at[which, at(peer, 96)],
                dst.at[at(s, 96)],
                r.a2a_s.at[which, k - 1],
                r.a2a_r.at[which, k - 1],
                (peer, g),
            ).start()

        dst[at(s, 96)] = r.stage[which, at(s, 96)]

    def arrive(which, dst):
        @pl.loop(1, 8)
        def _(k):
            peer = lax.rem(s + 8 - k, 8)
            remote(
                r.stage.at[which, at(peer, 96)],
                dst.at[at(peer, 96)],
                r.a2a_s.at[which, k - 1],
                r.a2a_r.at[which, k - 1],
                (peer, g),
            ).wait_recv()

    r.stage[0] = jnp.transpose(gated).astype(bf16)
    trade(0, r.gat)

    bias_cols = jnp.transpose(r.filt_bias[...])
    freq_cols = jnp.transpose(r.filt_freq[...])
    below = r.feats[...]
    for i, (u_ref, a_ref, c_ref) in enumerate(
        ((r.u1, r.a1, r.c1), (r.u2, r.a2, r.c2), (r.u3, r.a3, r.c3))
    ):
        weights = r.filt_first[...] if i == 0 else r.filt_hidden[i - 1]
        u = tn_high(weights, below) + bias_cols[:, i : i + 1]
        u_ref[...] = u
        below, cosine = sin_cos(freq_cols[:, i : i + 1] * u)
        a_ref[...] = below
        c_ref[...] = cosine

    r.last_t[...] = jnp.transpose(r.filt_last[...])
    r.rate_t[...] = jnp.transpose(jnp.broadcast_to(r.decay1[...].reshape(1, 768), (8, 768)))
    last = r.last_t[at(s, 96)]
    rate = r.rate_t[at(s, 96), 0:1]
    place = lax.broadcasted_iota(jnp.int32, (1, 1024), 1).astype(f32)
    r.wind[...] = jnp.exp(-rate * place)
    r.taps[...] = nn_high(last, r.a3[...]) * r.wind[...]
    r.hw_high[pl.ds(0, 96), own] = jnp.zeros((96, 128), bf16)
    r.hw_low[pl.ds(0, 96), own] = jnp.zeros((96, 128), bf16)
    for b in range(8):
        high, low = two(r.taps[:, 128 * b : 128 * b + 128])
        for half, ref in ((high, r.hw_high), (low, r.hw_low)):
            ref[96 * b : 96 * b + 96, 128:256] = half
            if b < 7:
                ref[96 * b + 96 : 96 * b + 192, 0:128] = half

    def by_table(v, which, rows, cols):
        high, low = two(v)
        table = r.tables[which, rows, cols]
        return nn(high, table) + nn(low, table) + nn(high, r.tables[which + 1, rows, cols])

    every = pl.ds(0, 256)
    low_half, high_half = pl.ds(0, 128), pl.ds(128, 128)
    loads[3].wait()
    r.es[...] = (
        nn(r.hw_high[...], r.tables[2])
        + nn(r.hw_low[...], r.tables[2])
        + nn(r.hw_high[...], r.tables[3])
    )
    loads[2].wait()
    for copy in shares[0:3]:
        copy.start()
    shares[6].start()

    arrive(0, r.gat)
    r.xs[...] = nn(r.gat[...], r.tables[2, low_half]) + nn(r.gat[...], r.tables[3, low_half])

    def pick(ref, tile, b):
        rows = pl.ds(pl.multiple_of(96 * b + 8 * tile, 8), 8)
        return ref[rows, low_half], ref[rows, high_half]

    def keep(ref, tile, b, pair_of):
        rows = pl.ds(pl.multiple_of(96 * b + 8 * tile, 8), 8)
        ref[rows, low_half] = pair_of[0]
        ref[rows, high_half] = pair_of[1]

    @pl.loop(0, 12)
    def _(tile):
        e = [pick(r.es, tile, b) for b in range(8)]
        v = [pick(r.xs, tile, b) for b in range(8)]
        for b in range(8):
            re, im = 0.0, 0.0
            for lag in range(b + 1):
                er, ei = e[lag]
                vr, vi = v[b - lag]
                re = re + er * vr - ei * vi
                im = im + er * vi + ei * vr
            keep(r.ys, tile, b, (re, im))

    conv = by_table(r.ys[...], 0, every, high_half) * (1.0 / 128.0)
    r.stage[1] = conv.astype(bf16)
    trade(1, r.co_in)

    loads[4].wait()
    for t in range(4):
        cols = pl.ds(768 * t, 768)
        r.g_act[:, cols] = nt(r.rh_down[own], r.down_w[cols])

    arrive(1, r.co_in)
    sum_f = jnp.transpose(r.co_in[...].astype(f32)) + r.skip[...] * r.gf[...]
    r.summed[...] = sum_f
    mixed = (r.outer[...] * sum_f).astype(bf16)
    loads[5].wait()
    res = r.tok[pl.ds(HALO, ROWS)].astype(f32) + nn(mixed, r.out_w[...]) + r.out_b[...]
    r.resid[...] = res
    hat, inv = norm_rows(res)
    r.hat2[...] = hat
    r.std2[...] = inv
    n2 = (hat * r.norm_gain[1:2] + r.norm_bias[1:2]).astype(bf16)
    loads[6].wait()
    for t in range(4):
        cols = pl.ds(768 * t, 768)
        act_f, slope = gelu_both(nn(n2, r.up_w[:, cols]) + r.up_b[:, cols])
        act_b = act_f.astype(bf16)
        r.act[:, cols] = act_b
        r.rh_up[own, cols] = (r.g_act[:, cols] * slope).astype(bf16)
        turned = jnp.transpose(act_b.astype(f32)).astype(bf16)
        for ix in range(2):
            for iy in range(2):
                for core in range(2):
                    i1, i2 = (ix, iy) if core == 0 else (iy, ix)
                    src = 96 * (ix * 4 + iy * 2 + core)
                    r.at_down[core, pl.ds(i1 * 768 + i2 * 384 + t * 96, 96)] = turned[src : src + 96]
    for copy in shares[3:6]:
        copy.start()
    shares[9].start()
    order_rows(n2.astype(f32), r.at_up)
    shares[8].start()
    r.lh_up[:, own] = r.at_up[c]
    order_rows(mixed.astype(f32), r.at_out)
    shares[7].start()
    r.lh_out[:, own] = r.at_out[c]
    r.lh_down[:, own] = r.at_down[c, at(b1, 768)]

    def one_a(p):
        return remote(r.s1a.at[p], r.r1a.at[p], r.p1_s.at[p], r.p1_r.at[p], first)

    def two_a(p):
        return remote(r.s2a.at[p], r.r2a.at[p], r.p2_s.at[p], r.p2_r.at[p], second)

    def zed_a(p, k):
        to = lax.rem(z + k, 4)
        return remote(
            r.zsa.at[p, to],
            r.zra.at[p, k - 1],
            r.z_s.at[p, k - 1],
            r.z_r.at[p, k - 1],
            (to * 2 + x, g),
        )

    def two_b(p):
        return remote(r.s2b.at[p], r.r2b.at[p], r.p2_s.at[8 + p], r.p2_r.at[8 + p], second)

    def zed_b(p, k):
        to = lax.rem(z + k, 4)
        return remote(
            r.zsb.at[p, to],
            r.zrb.at[p, k - 1],
            r.z_s.at[8 + p, k - 1],
            r.z_r.at[8 + p, k - 1],
            (to * 2 + x, g),
        )

    def send_a(p0, count, lh, rh):
        @pl.loop(0, count)
        def _(p):
            r.s1a[p0 + p] = nn(lh[at(1 - b1, 192)], rh[:, at(p, 768)]).astype(bf16)
            one_a(p0 + p).start()

    def stay_a(p0, count, lh, rh):
        @pl.loop(0, count)
        def _(p):
            r.k1a[p0 + p] = nn(lh[at(b1, 192)], rh[:, at(p, 768)])

    def ph1_a(p):
        one_a(p).wait_recv()
        rows = at(1 - b2, 96)
        r.s2a[p] = (r.k1a[p, rows] + r.r1a[p, rows].astype(f32)).astype(bf16)
        two_a(p).start()

    def ph2_a(p):
        two_a(p).wait_recv()
        rows = at(b2, 96)
        v = r.k1a[p, rows] + r.r1a[p, rows].astype(f32) + r.r2a[p].astype(f32)
        for iz in range(4):
            block = v[24 * iz : 24 * iz + 24]
            r.zsa[p, iz] = jnp.concatenate([block[:, :384], block[:, 384:]], axis=0).astype(bf16)
        for k in range(1, 4):
            zed_a(p, k).start()

    def ph3_a(p, dest, base, per_row):
        for k in range(1, 4):
            zed_a(p, k).wait_recv()
        v = r.zsa[p, z].astype(f32)
        for k in range(3):
            v = v + r.zra[p, k].astype(f32)
        for h in range(2):
            for j in range(3):
                dest[pl.ds(base + 3 * h + j, 24, stride=per_row)] = v[
                    24 * h : 24 * h + 24, 128 * j : 128 * j + 128
                ]

    def ph2_b(p):
        two_b(p).wait_recv()
        v = r.k2b[p] + r.r2b[p].astype(f32)
        for iz in range(4):
            r.zsb[p, iz] = v[96 * iz : 96 * iz + 96].astype(bf16)
        for k in range(1, 4):
            zed_b(p, k).start()

    def ph3_b(p):
        for k in range(1, 4):
            zed_b(p, k).wait_recv()
        v = r.zsb[p, z].astype(f32)
        for k in range(3):
            v = v + r.zrb[p, k].astype(f32)
        for j in range(2):
            r.f_gdown[pl.ds(2 * p + j, 96, stride=6)] = v[:, 128 * j : 128 * j + 128]

    def put(row, v):
        for j in range(v.shape[1] // 128):
            part, line = divmod(row + j, 64)
            r.smf[part, line : line + 1] = v[:, 128 * j : 128 * j + 128]

    e = nt(r.rh_up[own], r.up_w[...])
    hat = r.hat2[...]
    grad_f = r.rh_down[own].astype(f32)
    g_res = grad_f + norm_rows_back(e, hat, r.std2[...], r.norm_gain[1:2])
    r.g_resid[...] = g_res
    g_res_b = g_res.astype(bf16)
    r.rh_out[own] = g_res_b
    shares[10].start()
    g_mixed = nt(g_res_b, r.out_w[...])
    r.g_outer[...] = g_mixed * r.summed[...]
    g_summed = g_mixed * r.outer[...]
    r.g_sum[...] = g_summed
    r.stage[2] = jnp.transpose(g_summed).astype(bf16)
    trade(2, r.gc_in)

    shares[8].wait_recv()
    shares[9].wait_recv()
    send_a(0, 4, r.lh_up, r.rh_up)
    for copy in shares[0:6]:
        copy.wait_recv()
    for p in range(3):
        cols = pl.ds(256 * p, 256)
        r.s2b[p] = nn(r.lh_down[at(1 - b2, 384)], r.rh_down[:, cols]).astype(bf16)
        two_b(p).start()
    shares[7].wait_recv()
    shares[10].wait_recv()
    send_a(4, 1, r.lh_out, r.rh_out)
    for p in range(3):
        r.k2b[p] = nn(r.lh_down[at(b2, 384)], r.rh_down[:, 256 * p : 256 * p + 256])
    put(AT_GAIN + 6, col_sum(e * hat))
    put(AT_SHIFT + 6, col_sum(e))
    put(AT_DOWNB, col_sum(grad_f))
    put(AT_UPB, col_sum(r.rh_up[own].astype(f32)))
    put(AT_OUTB, col_sum(g_res_b.astype(f32)))
    put(AT_SKIP, col_sum(g_summed * r.gf[...]))

    arrive(2, r.gc_in)
    r.ys[...] = (
        nn(r.gc_in[...], r.tables[2, high_half]) + nn(r.gc_in[...], r.tables[3, high_half])
    ) * (1.0 / 128.0)

    @pl.loop(0, 12)
    def _(tile):
        e = [pick(r.es, tile, b) for b in range(8)]
        d = [pick(r.ys, tile, b) for b in range(8)]
        for b in range(8):
            re, im = 0.0, 0.0
            for lag in range(8 - b):
                er, ei = e[lag]
                dr, di = d[b + lag]
                re = re + er * dr + ei * di
                im = im + er * di - ei * dr
            keep(r.es, tile, b, (re, im))

    g_long = by_table(r.es[...], 0, every, low_half)
    r.stage[3] = g_long.astype(bf16)
    trade(3, r.gl_in)

    stay_a(0, 4, r.lh_up, r.rh_up)
    stay_a(4, 1, r.lh_out, r.rh_out)
    r.f_out[...] = r.resid[...] + nn(r.act[...], r.down_w[...]) + r.down_b[...]
    store_out = pltpu.make_async_copy(r.f_out, r.o_out, r.st.at[0])
    store_out.start()
    ph1_a(0)

    arrive(3, r.gl_in)
    g_gated = r.skip[...] * r.g_sum[...] + jnp.transpose(r.gl_in[...].astype(f32))
    mixes = (r.g_outer[...], g_gated * r.value[...], g_gated * r.inner[...])
    for part in range(3):
        r.gm[own, 768 * part : 768 * part + 768] = mixes[part]
    first_rows = remote(
        r.gm.at[pl.ds(0, 8)], r.gm.at[pl.ds(ROWS, 8)], r.halo_s.at[1], r.halo_r.at[1], (s - 1, g)
    )

    @pl.when(s > 0)
    def _():
        first_rows.start()

    for part in range(3):
        cols = pl.ds(768 * part, 768)
        mix = r.gm[own, cols]
        put(AT_CONVB + 6 * part, col_sum(mix))
        for tap in range(3):
            put(
                AT_CONVW + 18 * tap + 6 * part,
                col_sum(mix * r.pp[pl.ds(HALO - 2 + tap, ROWS), cols]),
            )

    ph1_a(1)

    @pl.when(s < 7)
    def _():
        first_rows.wait_recv()

    @pl.when(s == 7)
    def _():
        r.gm[pl.ds(ROWS, 8)] = jnp.zeros((8, r.gm.shape[1]), f32)

    for part in range(3):
        cols = pl.ds(768 * part, 768)
        r.rh_in[own, cols] = (
            r.conv_w[0:1, cols] * r.gm[pl.ds(2, ROWS), cols]
            + r.conv_w[1:2, cols] * r.gm[pl.ds(1, ROWS), cols]
            + r.conv_w[2:3, cols] * r.gm[pl.ds(0, ROWS), cols]
        ).astype(bf16)
    shares[11].start()
    e = nt(r.rh_in[own], r.in_w[...])
    shares[6].wait_recv()
    shares[11].wait_recv()
    send_a(5, 3, r.lh_in, r.rh_in)
    ph1_a(2)
    stay_a(5, 3, r.lh_in, r.rh_in)
    for p in range(3):
        ph2_b(p)
    hat = r.hat1[...]
    put(AT_IN, col_sum(r.rh_in[own].astype(f32)))
    put(AT_GAIN, col_sum(e * hat))
    put(AT_SHIFT, col_sum(e))
    r.f_gtok[...] = r.g_resid[...] + norm_rows_back(e, hat, r.std1[...], r.norm_gain[0:1])
    store_tok = pltpu.make_async_copy(r.f_gtok, r.o_gtok, r.st.at[1])
    store_tok.start()
    ph1_a(3)

    @pl.loop(0, 12)
    def _(tile):
        v = [pick(r.xs, tile, b) for b in range(8)]
        d = [pick(r.ys, tile, b) for b in range(8)]
        for lag in range(8):
            re, im = 0.0, 0.0
            for b in range(8 - lag):
                vr, vi = v[b]
                dr, di = d[b + lag]
                re = re + vr * dr + vi * di
                im = im + vr * di - vi * dr
            keep(r.xs, tile, lag, (re, im))

    r.gtap[...] = by_table(r.xs[...], 0, every, every)
    ph1_a(4)
    for b in range(8):
        cols = pl.ds(128 * b, 128)
        gt = r.gtap[96 * b : 96 * b + 96, 128:256]
        if b < 7:
            gt = gt + r.gtap[96 * b + 96 : 96 * b + 192, 0:128]
        r.dpre[:, cols] = gt * r.wind[:, cols]
        r.taps[:, cols] = r.taps[:, cols] * gt
    g_rate = -jnp.sum(r.taps[...] * place, axis=1, keepdims=True)
    g_last = nt_high(r.dpre[...], r.a3[...])
    for j in range(4):
        r.smf[j, 64:88, 0:64] = g_last[24 * j : 24 * j + 24]
        r.smf[j, 64:88, 64:65] = g_rate[24 * j : 24 * j + 24]
    ones = jnp.ones((8, 1024), f32)
    g_a = tn_high(last, r.dpre[...])
    for i, (u_ref, c_ref, a_ref) in enumerate(
        ((r.u3, r.c3, r.a2), (r.u2, r.c2, r.a1), (r.u1, r.c1, None))
    ):
        layer = 2 - i
        g_arg = g_a * c_ref[...]
        g_freq = nt_high(ones, g_arg * u_ref[...])[0:1]
        g_u = g_arg * freq_cols[:, layer : layer + 1]
        g_bias = nt_high(ones, g_u)[0:1]
        r.smf[1, layer : layer + 1, 64:128] = g_bias
        r.smf[1, 3 + layer : 4 + layer, 64:128] = g_freq
        if layer > 0:
            r.smf[0, 0:64, 64 * (layer - 1) : 64 * layer] = nt_high(a_ref[...], g_u)
            g_a = nn_high(r.filt_hidden[layer - 1], g_u)
        else:
            r.smf[1, 0:33, 0:64] = nt_high(r.feats[...], g_u)

    def quarter(k):
        t = lax.rem(g + k, 4)
        return remote(r.smf.at[t], r.q_in.at[k - 1], r.q_s.at[k - 1], r.q_r.at[k - 1], (s, t))

    def eighth(k):
        t = lax.rem(s + k, 8)
        return remote(
            r.q_sum.at[at(t, 8)], r.o_in.at[k - 1], r.o_s.at[k - 1], r.o_r.at[k - 1], (t, g)
        )

    def spread(k, back):
        t = lax.rem(s + k, 8)
        mine = lax.rem(s + 8 - k, 8) if back else s
        slot = r.ag.at[g, mine]
        return remote(slot, slot, r.ag_s.at[k - 1], r.ag_r.at[k - 1], (t, g))

    over_y = g + y_step
    first_slot, second_slot = r.ag.at[g], r.ag.at[over_y]
    y_send = remote(first_slot, first_slot, r.ag_s.at[7], r.ag_r.at[7], (s, over_y))
    y_back = remote(second_slot, second_slot, r.ag_s.at[7], r.ag_r.at[7], (s, over_y))
    c_send = [
        remote(slot, slot, r.ag_s.at[8 + i], r.ag_r.at[8 + i], (s, other))
        for i, slot in enumerate((first_slot, second_slot))
    ]
    third_slot, fourth_slot = r.ag.at[other], r.ag.at[other + y_step]
    c_back = [
        remote(slot, slot, r.ag_s.at[8 + i], r.ag_r.at[8 + i], (s, other))
        for i, slot in enumerate((third_slot, fourth_slot))
    ]

    for k in range(1, 4):
        quarter(k).start()

    @pl.loop(0, 3)
    def _(p):
        ph2_a(p)

    for k in range(1, 4):
        quarter(k).wait_recv()
    r.q_sum[...] = r.smf[g] + r.q_in[0] + r.q_in[1] + r.q_in[2]

    @pl.loop(1, 8)
    def _(k):
        eighth(k).start()

    @pl.loop(5, 8)
    def _(p):
        ph1_a(p)

    ph2_a(3)
    ph2_a(4)

    @pl.loop(1, 8)
    def _(k):
        eighth(k).wait_recv()

    r.ag[g, s, pl.ds(0, 8)] = r.q_sum[at(s, 8)] + jnp.sum(r.o_in[...], axis=0)
    r.ag[g, s, pl.ds(8, 24)] = r.q_sum[pl.ds(64, 24)]

    @pl.loop(1, 8)
    def _(k):
        spread(k, False).start()

    for p in range(3):
        ph3_b(p)

    @pl.loop(1, 8)
    def _(k):
        spread(k, True).wait_recv()

    y_send.start()

    @pl.loop(0, 4)
    def _(p):
        ph3_a(p, r.f_gup, 6 * p, 24)

    @pl.loop(5, 8)
    def _(p):
        ph2_a(p)

    ph3_a(4, r.f_gout, 0, 6)
    y_back.wait_recv()
    for copy in c_send:
        copy.start()

    stores = [
        store_out,
        store_tok,
        pltpu.make_async_copy(r.f_gdown, r.o_gdown, r.st.at[2]),
        pltpu.make_async_copy(r.f_gup, r.o_gup, r.st.at[3]),
        pltpu.make_async_copy(r.f_gout, r.o_gout, r.st.at[4]),
        pltpu.make_async_copy(r.f_gin, r.o_gin, r.st.at[5]),
        pltpu.make_async_copy(r.ag, r.o_small, r.st.at[6]),
    ]
    for copy in stores[2:5]:
        copy.start()
    for copy in c_back:
        copy.wait_recv()
    stores[6].start()

    @pl.loop(0, 3)
    def _(p):
        ph3_a(5 + p, r.f_gin, 6 * p, 18)

    stores[5].start()

    @pl.when(s < 7)
    def _():
        last_rows.wait_send()

    @pl.when(s > 0)
    def _():
        first_rows.wait_send()

    for copy in shares:
        copy.wait_send()

    @pl.loop(0, 4)
    def _(which):
        @pl.loop(1, 8)
        def _(k):
            remote(
                r.stage.at[which, pl.ds(0, 96)],
                r.gat.at[pl.ds(0, 96)],
                r.a2a_s.at[which, k - 1],
                r.a2a_r.at[which, k - 1],
                (s, other),
            ).wait_send()

    @pl.loop(0, 8)
    def _(p):
        one_a(p).wait_send()
        two_a(p).wait_send()
        for k in range(1, 4):
            zed_a(p, k).wait_send()

    @pl.loop(0, 3)
    def _(p):
        two_b(p).wait_send()
        for k in range(1, 4):
            zed_b(p, k).wait_send()

    for k in range(1, 4):
        quarter(k).wait_send()

    @pl.loop(1, 8)
    def _(k):
        eighth(k).wait_send()
        spread(k, False).wait_send()

    y_send.wait_send()
    for copy in c_send:
        copy.wait_send()
    for copy in stores:
        copy.wait()


def finish_kernel(
    i_out, i_gtok, i_gin, i_gout, i_gup, i_gdown, i_small,
    out, gtok, gain, shift, gin, in_b, conv_w, conv_b, first, hidden, bias, freq,
    last, decay, skip, gout, out_b, gup, up_b, gdown, down_b,
    h_out, h_gtok, h_gin, h_gout, h_gup, h_gdown, small, sem_in, sem_out,
):
    bulk = (
        (i_small, small, None),
        (i_out, h_out, out.at[0]),
        (i_gtok, h_gtok, gtok.at[0]),
        (i_gin, h_gin, gin),
        (i_gout, h_gout, gout),
        (i_gup, h_gup, gup),
        (i_gdown, h_gdown, gdown),
    )
    enter = [pltpu.make_async_copy(a, b, sem_in.at[i]) for i, (a, b, _) in enumerate(bulk)]
    leave = [
        pltpu.make_async_copy(b, d, sem_out.at[i]) for i, (_, b, d) in enumerate(bulk) if i > 0
    ]
    for copy in enter:
        copy.start()
    for i in range(6):
        enter[i + 1].wait()
        leave[i].start()
    enter[0].wait()
    rows = jnp.concatenate([small[i, j, 0:8, :] for i in range(4) for j in range(8)], axis=0)

    def fetch(at_row, dest, dest_row, wide):
        for j in range(wide):
            dest[dest_row : dest_row + 1, 128 * j : 128 * j + 128] = rows[at_row + j : at_row + j + 1]

    def line(at_row, dest):
        dest[...] = rows[at_row : at_row + dest.shape[0] // 128].reshape(dest.shape[0])

    for i in range(2):
        fetch(AT_GAIN + 6 * i, gain, i, 6)
        fetch(AT_SHIFT + 6 * i, shift, i, 6)
        hidden[i] = rows[AT_HID : AT_HID + 64, 64 * i : 64 * i + 64]
    for i in range(3):
        fetch(AT_CONVW + 18 * i, conv_w, i, 18)
    line(AT_IN, in_b)
    line(AT_CONVB, conv_b)
    line(AT_SKIP, skip)
    line(AT_OUTB, out_b)
    line(AT_UPB, up_b)
    line(AT_DOWNB, down_b)
    first[...] = rows[AT_FIRST : AT_FIRST + 33, 0:64]
    bias[...] = rows[AT_FIRST : AT_FIRST + 3, 64:128]
    freq[...] = rows[AT_FIRST + 3 : AT_FIRST + 6, 64:128]
    channels = jnp.transpose(
        jnp.concatenate([small[j, i, 8:32, :] for i in range(8) for j in range(4)], axis=0)
    )
    last[...] = channels[0:64]
    decay[...] = channels[64:65].reshape(768)
    for copy in leave:
        copy.wait()


def one_kernel_body(tokens, out_grad, norm_gain, norm_bias, in_weight, in_bias, conv_weight, conv_bias,
                    filt_first, filt_hidden, filt_bias, filt_freq, filt_last, decay_rates, skip_scale,
                    out_weight, out_bias, up_weight, up_bias, down_weight, down_bias):
    width, hidden = up_weight.shape
    length = tokens.shape[1] * lax.axis_size("seq")
    any_spec = pl.BlockSpec(memory_space=pl.ANY)
    vmem_spec = pl.BlockSpec(memory_space=pltpu.VMEM)

    def vm(*shape, dtype=f32):
        return pltpu.VMEM(shape, dtype)

    def dma(*shape):
        return pltpu.SemaphoreType.DMA(shape)

    def shape(*dims):
        return jax.ShapeDtypeStruct(dims, f32)

    outs = pl.pallas_call(
        step_kernel,
        out_shape=[
            shape(128, width), shape(128, width), shape(432, 128), shape(144, 128),
            shape(576, 128), shape(576, 128), shape(4, 8, 32, 128),
        ],
        in_specs=[any_spec] * 23,
        out_specs=[any_spec] * 7,
        scratch_shapes=[vm(*dims) for _, dims in SMALL_ARGS]
        + [vm(*dims, dtype=dtype) for _, dims, dtype in SCRATCH]
        + [dma(*dims) for _, dims in SEMAPHORES],
        compiler_params=pltpu.CompilerParams(
            collective_id=0, has_side_effects=True, vmem_limit_bytes=62 * 1024 * 1024
        ),
        name="hyena_step",
    )(
        tokens, out_grad, in_weight, out_weight, up_weight, down_weight,
        jnp.asarray(fourier_tables()),
        norm_gain, norm_bias, in_bias, conv_weight, conv_bias,
        jnp.asarray(feature_table(length, (filt_first.shape[0] - 1) // 2)),
        filt_first, filt_hidden, filt_bias, filt_freq, filt_last, decay_rates, skip_scale, out_bias,
        up_bias, down_bias,
    )
    done = pl.pallas_call(
        finish_kernel,
        out_shape=[
            shape(1, 128, width), shape(1, 128, width), shape(2, width), shape(2, width), shape(432, 128),
            shape(3 * width), shape(3, 3 * width), shape(3 * width), shape(33, 64), shape(2, 64, 64),
            shape(3, 64), shape(3, 64), shape(64, width), shape(width), shape(width), shape(144, 128),
            shape(width), shape(576, 128), shape(hidden), shape(576, 128), shape(width),
        ],
        in_specs=[any_spec] * 7,
        out_specs=[any_spec, any_spec, vmem_spec, vmem_spec, any_spec]
        + [vmem_spec] * 10
        + [any_spec, vmem_spec, any_spec, vmem_spec, any_spec, vmem_spec],
        scratch_shapes=[
            vm(128, width), vm(128, width), vm(432, 128), vm(144, 128), vm(576, 128), vm(576, 128),
            vm(4, 8, 32, 128), dma(7), dma(7),
        ],
        compiler_params=pltpu.CompilerParams(vmem_limit_bytes=60 * 1024 * 1024),
        name="hyena_finish",
    )(*outs)
    flat = (4, 15, 17, 19)
    return tuple(v.reshape(-1) if i in flat else v for i, v in enumerate(done))


def solution(mesh):
    small_mesh = mesh.shape["seq"] == 8 and mesh.shape["grp"] == 4
    return jax.shard_map(
        one_kernel_body if small_mesh else body,
        mesh=mesh,
        in_specs=(P("grp", "seq", None), P("grp", "seq", None)) + (P(),) * 19,
        out_specs=(
            P("grp", "seq", None),
            P("grp", "seq", None),
            P(),
            P(),
            P(("seq", "grp")),
        )
        + (P(),) * 10
        + (P(("seq", "grp")), P(), P(("seq", "grp")), P(), P(("seq", "grp")), P()),
        check_vma=False,
    )
```

time: 147 us -> 120 us (0.82)
  Pallas kernels: 140 us -> 119 us
  local copies, waits for them, and re-layouts: 6.72 us -> 0 us
    pallas_call x1, Pallas kernels: 136 us -> 116 us  [one_kernel_body(): pl.pallas_call(step_kernel, out_shape=[shape(128, width), shape(128, widt...]
    unnamed x14 -> x0, local copies, waits for them, and re-layouts: 6.72 us -> none
where the time goes in v3:
time: 120 us
  Pallas kernels  119 us (99%)
    pallas_call x1, Pallas kernels, one_kernel_body(): pl.pallas_call(step_kernel, out_shape=[shape(128, width), shape(128, widt...  116 us
    pallas_call x1, Pallas kernels, one_kernel_body(): pl.pallas_call(finish_kernel, out_shape=[shape(1, 128, width), shape(1, 1...  3.21 us

profile of v3, /device:TPU:0, one launch (start us, length us, event | category | flops | bytes accessed | tf_op | source)
XLA Modules:
  0.0 120.0 jit_solution(985408811173524031)
XLA Ops:
  0.7 115.9 %hyena_step.1 = (f32[128,768]{1,0:T(8,128)}, f32[128,768]{1,0:T(8,128)}, f32[432,128]{1,0:T(8,128)}, f32[144,128]{1,0:T(8,128)}, f32[576,128]{1,0:T(8,128)}, /*i...) custom-call(bf16[1,128,768]{2,1,0:T(8,128)(2,1)} %refs_0_.1, bf16[1,128,768]{2,1,0:T(8,128)(2,1)} %refs_1_.1, ...), custom_call_target="tpu_custom_call" | custom-call | tf_op jit(solution)/shard_map/hyena_step/pallas_call | solution.py:1274
  116.6 3.2 %hyena_finish.1 = (f32[1,128,768]{2,1,0:T(8,128)}, f32[1,128,768]{2,1,0:T(8,128)}, f32[2,768]{1,0:T(2,128)}, f32[2,768]{1,0:T(2,128)}, f32[432,128]{1,0:T(8,128)...) custom-call(f32[128,768]{1,0:T(8,128)} %get-tuple-element.49.i_out, ...), custom_call_target="tpu_custom_call" | custom-call | tf_op jit(solution)/shard_map/hyena_finish/pallas_call | solution.py:1297

commit v4 on v3

--- a/solution.py
+++ b/solution.py
@@ -456,9 +456,11 @@
     ("lh_in", (384, 256), bf16), ("lh_out", (384, 256), bf16), ("rh_down", (512, 768), bf16),
     ("rh_up", (256, 3072), bf16), ("rh_in", (256, 2304), bf16), ("rh_out", (256, 768), bf16),
     ("s1a", (8, 192, 768), bf16), ("k1a", (8, 192, 768), f32), ("r1a", (8, 192, 768), bf16),
-    ("s2a", (8, 96, 768), bf16), ("r2a", (8, 96, 768), bf16), ("zsa", (8, 4, 48, 384), bf16),
-    ("zra", (8, 3, 48, 384), bf16), ("s2b", (3, 384, 256), bf16), ("k2b", (3, 384, 256), f32),
-    ("r2b", (3, 384, 256), bf16), ("zsb", (3, 4, 96, 256), bf16), ("zrb", (3, 3, 96, 256), bf16),
+    ("s2a", (8, 96, 768), bf16), ("r2a", (8, 96, 768), bf16), ("s3a", (8, 4, 48, 384), bf16),
+    ("r3a", (8, 2, 48, 384), bf16), ("s4a", (8, 48, 384), bf16), ("r4a", (8, 48, 384), bf16),
+    ("s2b", (3, 384, 256), bf16), ("k2b", (3, 384, 256), f32), ("r2b", (3, 384, 256), bf16),
+    ("s3b", (3, 4, 96, 256), bf16), ("r3b", (3, 2, 96, 256), bf16), ("s4b", (3, 96, 256), bf16),
+    ("r4b", (3, 96, 256), bf16),
     ("smf", (4, 88, 128), f32), ("q_in", (3, 88, 128), f32), ("q_sum", (88, 128), f32),
     ("o_in", (7, 8, 128), f32), ("ag", (4, 8, 32, 128), f32),
     ("f_gin", (432, 128), f32), ("f_gout", (144, 128), f32), ("f_gup", (576, 128), f32),
@@ -468,7 +470,7 @@
 SEMAPHORES = (
     ("ld", (8,)), ("ls", (16,)), ("a2a_s", (4, 7)), ("a2a_r", (4, 7)), ("halo_s", (2,)), ("halo_r", (2,)),
     ("pair_s", (12,)), ("pair_r", (12,)), ("p1_s", (8,)), ("p1_r", (8,)), ("p2_s", (11,)),
-    ("p2_r", (11,)), ("z_s", (11, 3)), ("z_r", (11, 3)), ("q_s", (3,)), ("q_r", (3,)),
+    ("p2_r", (11,)), ("p3_s", (11,)), ("p3_r", (11,)), ("p4_s", (11,)), ("p4_r", (11,)), ("q_s", (3,)), ("q_r", (3,)),
     ("o_s", (7,)), ("o_r", (7,)), ("ag_s", (10,)), ("ag_r", (10,)), ("st", (7,)),
 )
 
@@ -492,6 +494,8 @@
     cross = (s + c * x_step, other + (1 - c) * y_step)
     b1 = (1 - c) * x + c * y
     b2 = (1 - c) * y + c * x
+    z2, z1 = lax.div(z, 2), lax.rem(z, 2)
+    near, far = (s + 2 - 4 * z1, g), (s + 4 - 8 * z2, g)
 
     def at(index, size):
         return pl.ds(pl.multiple_of(index * size, size), size)
@@ -787,34 +791,29 @@
     def two_a(p):
         return remote(r.s2a.at[p], r.r2a.at[p], r.p2_s.at[p], r.p2_r.at[p], second)
 
-    def zed_a(p, k):
-        to = lax.rem(z + k, 4)
+    def three_a(p):
         return remote(
-            r.zsa.at[p, to],
-            r.zra.at[p, k - 1],
-            r.z_s.at[p, k - 1],
-            r.z_r.at[p, k - 1],
-            (to * 2 + x, g),
+            r.s3a.at[p, at(1 - z1, 2)], r.r3a.at[p], r.p3_s.at[p], r.p3_r.at[p], near
         )
+
+    def four_a(p):
+        return remote(r.s4a.at[p], r.r4a.at[p], r.p4_s.at[p], r.p4_r.at[p], far)
 
     def two_b(p):
         return remote(r.s2b.at[p], r.r2b.at[p], r.p2_s.at[8 + p], r.p2_r.at[8 + p], second)
 
-    def zed_b(p, k):
-        to = lax.rem(z + k, 4)
+    def three_b(p):
         return remote(
-            r.zsb.at[p, to],
-            r.zrb.at[p, k - 1],
-            r.z_s.at[8 + p, k - 1],
-            r.z_r.at[8 + p, k - 1],
-            (to * 2 + x, g),
+            r.s3b.at[p, at(1 - z1, 2)], r.r3b.at[p], r.p3_s.at[8 + p], r.p3_r.at[8 + p], near
         )
 
-    def send_a(p0, count, lh, rh):
+    def four_b(p):
+        return remote(r.s4b.at[p], r.r4b.at[p], r.p4_s.at[8 + p], r.p4_r.at[8 + p], far)
+
+    def make_a(p0, count, lh, rh):
         @pl.loop(0, count)
         def _(p):
             r.s1a[p0 + p] = nn(lh[at(1 - b1, 192)], rh[:, at(p, 768)]).astype(bf16)
-            one_a(p0 + p).start()
 
     def stay_a(p0, count, lh, rh):
         @pl.loop(0, count)
@@ -833,16 +832,21 @@
         v = r.k1a[p, rows] + r.r1a[p, rows].astype(f32) + r.r2a[p].astype(f32)
         for iz in range(4):
             block = v[24 * iz : 24 * iz + 24]
-            r.zsa[p, iz] = jnp.concatenate([block[:, :384], block[:, 384:]], axis=0).astype(bf16)
-        for k in range(1, 4):
-            zed_a(p, k).start()
-
-    def ph3_a(p, dest, base, per_row):
-        for k in range(1, 4):
-            zed_a(p, k).wait_recv()
-        v = r.zsa[p, z].astype(f32)
-        for k in range(3):
-            v = v + r.zra[p, k].astype(f32)
+            r.s3a[p, 2 * (iz % 2) + iz // 2] = jnp.concatenate(
+                [block[:, :384], block[:, 384:]], axis=0
+            ).astype(bf16)
+        three_a(p).start()
+
+    def ph3_a(p):
+        three_a(p).wait_recv()
+        r.s4a[p] = (
+            r.s3a[p, 2 * z1 + 1 - z2].astype(f32) + r.r3a[p, 1 - z2].astype(f32)
+        ).astype(bf16)
+        four_a(p).start()
+
+    def ph4_a(p, dest, base, per_row):
+        four_a(p).wait_recv()
+        v = r.s3a[p, 2 * z1 + z2].astype(f32) + r.r3a[p, z2].astype(f32) + r.r4a[p].astype(f32)
         for h in range(2):
             for j in range(3):
                 dest[pl.ds(base + 3 * h + j, 24, stride=per_row)] = v[
@@ -853,16 +857,19 @@
         two_b(p).wait_recv()
         v = r.k2b[p] + r.r2b[p].astype(f32)
         for iz in range(4):
-            r.zsb[p, iz] = v[96 * iz : 96 * iz + 96].astype(bf16)
-        for k in range(1, 4):
-            zed_b(p, k).start()
+            r.s3b[p, 2 * (iz % 2) + iz // 2] = v[96 * iz : 96 * iz + 96].astype(bf16)
+        three_b(p).start()
 
     def ph3_b(p):
-        for k in range(1, 4):
-            zed_b(p, k).wait_recv()
-        v = r.zsb[p, z].astype(f32)
-        for k in range(3):
-            v = v + r.zrb[p, k].astype(f32)
+        three_b(p).wait_recv()
+        r.s4b[p] = (
+            r.s3b[p, 2 * z1 + 1 - z2].astype(f32) + r.r3b[p, 1 - z2].astype(f32)
+        ).astype(bf16)
+        four_b(p).start()
+
+    def ph4_b(p):
+        four_b(p).wait_recv()
+        v = r.s3b[p, 2 * z1 + z2].astype(f32) + r.r3b[p, z2].astype(f32) + r.r4b[p].astype(f32)
         for j in range(2):
             r.f_gdown[pl.ds(2 * p + j, 96, stride=6)] = v[:, 128 * j : 128 * j + 128]
 
@@ -888,18 +895,20 @@
 
     shares[8].wait_recv()
     shares[9].wait_recv()
-    send_a(0, 4, r.lh_up, r.rh_up)
+    make_a(0, 4, r.lh_up, r.rh_up)
+    one_a(0).start()
     for copy in shares[0:6]:
         copy.wait_recv()
     for p in range(3):
         cols = pl.ds(256 * p, 256)
         r.s2b[p] = nn(r.lh_down[at(1 - b2, 384)], r.rh_down[:, cols]).astype(bf16)
-        two_b(p).start()
+        if p == 0:
+            two_b(p).start()
+    for p in range(3):
+        r.k2b[p] = nn(r.lh_down[at(b2, 384)], r.rh_down[:, 256 * p : 256 * p + 256])
     shares[7].wait_recv()
     shares[10].wait_recv()
-    send_a(4, 1, r.lh_out, r.rh_out)
-    for p in range(3):
-        r.k2b[p] = nn(r.lh_down[at(b2, 384)], r.rh_down[:, 256 * p : 256 * p + 256])
+    make_a(4, 1, r.lh_out, r.rh_out)
     put(AT_GAIN + 6, col_sum(e * hat))
     put(AT_SHIFT + 6, col_sum(e))
     put(AT_DOWNB, col_sum(grad_f))
@@ -929,12 +938,15 @@
     r.stage[3] = g_long.astype(bf16)
     trade(3, r.gl_in)
 
+    one_a(1).start()
+    two_b(1).start()
     stay_a(0, 4, r.lh_up, r.rh_up)
     stay_a(4, 1, r.lh_out, r.rh_out)
+    ph2_b(0)
+    ph1_a(0)
     r.f_out[...] = r.resid[...] + nn(r.act[...], r.down_w[...]) + r.down_b[...]
     store_out = pltpu.make_async_copy(r.f_out, r.o_out, r.st.at[0])
     store_out.start()
-    ph1_a(0)
 
     arrive(3, r.gl_in)
     g_gated = r.skip[...] * r.g_sum[...] + jnp.transpose(r.gl_in[...].astype(f32))
@@ -949,6 +961,8 @@
     def _():
         first_rows.start()
 
+    one_a(2).start()
+    two_b(2).start()
     for part in range(3):
         cols = pl.ds(768 * part, 768)
         mix = r.gm[own, cols]
@@ -958,8 +972,6 @@
                 AT_CONVW + 18 * tap + 6 * part,
                 col_sum(mix * r.pp[pl.ds(HALO - 2 + tap, ROWS), cols]),
             )
-
-    ph1_a(1)
 
     @pl.when(s < 7)
     def _():
@@ -980,11 +992,15 @@
     e = nt(r.rh_in[own], r.in_w[...])
     shares[6].wait_recv()
     shares[11].wait_recv()
-    send_a(5, 3, r.lh_in, r.rh_in)
+    make_a(5, 3, r.lh_in, r.rh_in)
+    for p in (5, 6, 7, 3, 4):
+        one_a(p).start()
+    ph1_a(1)
+    ph2_b(1)
+    ph3_b(0)
+    stay_a(5, 3, r.lh_in, r.rh_in)
     ph1_a(2)
-    stay_a(5, 3, r.lh_in, r.rh_in)
-    for p in range(3):
-        ph2_b(p)
+    ph2_b(2)
     hat = r.hat1[...]
     put(AT_IN, col_sum(r.rh_in[own].astype(f32)))
     put(AT_GAIN, col_sum(e * hat))
@@ -992,7 +1008,8 @@
     r.f_gtok[...] = r.g_resid[...] + norm_rows_back(e, hat, r.std1[...], r.norm_gain[0:1])
     store_tok = pltpu.make_async_copy(r.f_gtok, r.o_gtok, r.st.at[1])
     store_tok.start()
-    ph1_a(3)
+    ph2_a(0)
+    ph3_b(1)
 
     @pl.loop(0, 12)
     def _(tile):
@@ -1008,7 +1025,9 @@
             keep(r.xs, tile, lag, (re, im))
 
     r.gtap[...] = by_table(r.xs[...], 0, every, every)
-    ph1_a(4)
+    ph2_a(1)
+    ph3_a(0)
+    ph3_b(2)
     for b in range(8):
         cols = pl.ds(128 * b, 128)
         gt = r.gtap[96 * b : 96 * b + 96, 128:256]
@@ -1072,10 +1091,10 @@
     for k in range(1, 4):
         quarter(k).start()
 
-    @pl.loop(0, 3)
-    def _(p):
-        ph2_a(p)
-
+    ph2_a(2)
+    ph3_a(1)
+    ph1_a(5)
+    ph1_a(6)
     for k in range(1, 4):
         quarter(k).wait_recv()
     r.q_sum[...] = r.smf[g] + r.q_in[0] + r.q_in[1] + r.q_in[2]
@@ -1084,12 +1103,9 @@
     def _(k):
         eighth(k).start()
 
-    @pl.loop(5, 8)
-    def _(p):
-        ph1_a(p)
-
-    ph2_a(3)
-    ph2_a(4)
+    ph3_a(2)
+    ph1_a(7)
+    ph2_a(5)
 
     @pl.loop(1, 8)
     def _(k):
@@ -1102,8 +1118,14 @@
     def _(k):
         spread(k, False).start()
 
+    ph1_a(3)
+    ph2_a(6)
+    ph3_a(5)
+    ph1_a(4)
+    ph2_a(7)
+    ph3_a(6)
     for p in range(3):
-        ph3_b(p)
+        ph4_b(p)
 
     @pl.loop(1, 8)
     def _(k):
@@ -1111,18 +1133,23 @@
 
     y_send.start()
 
-    @pl.loop(0, 4)
+    @pl.loop(0, 3)
     def _(p):
-        ph3_a(p, r.f_gup, 6 * p, 24)
-
-    @pl.loop(5, 8)
+        ph4_a(p, r.f_gup, 6 * p, 24)
+
+    ph2_a(3)
+    ph3_a(7)
+    ph2_a(4)
+    ph3_a(3)
+
+    @pl.loop(0, 3)
     def _(p):
-        ph2_a(p)
-
-    ph3_a(4, r.f_gout, 0, 6)
+        ph4_a(5 + p, r.f_gin, 6 * p, 18)
+
     y_back.wait_recv()
     for copy in c_send:
         copy.start()
+    ph3_a(4)
 
     stores = [
         store_out,
@@ -1133,17 +1160,15 @@
         pltpu.make_async_copy(r.f_gin, r.o_gin, r.st.at[5]),
         pltpu.make_async_copy(r.ag, r.o_small, r.st.at[6]),
     ]
-    for copy in stores[2:5]:
-        copy.start()
+    stores[2].start()
+    stores[5].start()
     for copy in c_back:
         copy.wait_recv()
     stores[6].start()
-
-    @pl.loop(0, 3)
-    def _(p):
-        ph3_a(5 + p, r.f_gin, 6 * p, 18)
-
-    stores[5].start()
+    ph4_a(3, r.f_gup, 18, 24)
+    stores[3].start()
+    ph4_a(4, r.f_gout, 0, 6)
+    stores[4].start()
 
     @pl.when(s < 7)
     def _():
@@ -1172,14 +1197,14 @@
     def _(p):
         one_a(p).wait_send()
         two_a(p).wait_send()
-        for k in range(1, 4):
-            zed_a(p, k).wait_send()
+        three_a(p).wait_send()
+        four_a(p).wait_send()
 
     @pl.loop(0, 3)
     def _(p):
         two_b(p).wait_send()
-        for k in range(1, 4):
-            zed_b(p, k).wait_send()
+        three_b(p).wait_send()
+        four_b(p).wait_send()
 
     for k in range(1, 4):
         quarter(k).wait_send()

time: 120 us -> 105 us (0.88)
  Pallas kernels: 119 us -> 105 us
    pallas_call x1, Pallas kernels: 116 us -> 101 us  [one_kernel_body(): pl.pallas_call(step_kernel, out_shape=[shape(128, width), shape(128, widt...]
where the time goes in v4:
time: 105 us
  Pallas kernels  105 us (100%)
    pallas_call x1, Pallas kernels, one_kernel_body(): pl.pallas_call(step_kernel, out_shape=[shape(128, width), shape(128, widt...  101 us
    pallas_call x1, Pallas kernels, one_kernel_body(): pl.pallas_call(finish_kernel, out_shape=[shape(1, 128, width), shape(1, 1...  3.21 us

profile of v4, /device:TPU:0, one launch (start us, length us, event | category | flops | bytes accessed | tf_op | source)
XLA Modules:
  0.0 105.3 jit_solution(8849223010061381295)
XLA Ops:
  0.7 101.3 %hyena_step.1 = (f32[128,768]{1,0:T(8,128)}, f32[128,768]{1,0:T(8,128)}, f32[432,128]{1,0:T(8,128)}, f32[144,128]{1,0:T(8,128)}, f32[576,128]{1,0:T(8,128)}, /*i...) custom-call(bf16[1,128,768]{2,1,0:T(8,128)(2,1)} %refs_0_.1, bf16[1,128,768]{2,1,0:T(8,128)(2,1)} %refs_1_.1, ...), custom_call_target="tpu_custom_call" | custom-call | tf_op jit(solution)/shard_map/hyena_step/pallas_call | solution.py:1299
  102.0 3.2 %hyena_finish.1 = (f32[1,128,768]{2,1,0:T(8,128)}, f32[1,128,768]{2,1,0:T(8,128)}, f32[2,768]{1,0:T(2,128)}, f32[2,768]{1,0:T(2,128)}, f32[432,128]{1,0:T(8,128)...) custom-call(f32[128,768]{1,0:T(8,128)} %get-tuple-element.49.i_out, ...), custom_call_target="tpu_custom_call" | custom-call | tf_op jit(solution)/shard_map/hyena_finish/pallas_call | solution.py:1322

commit v5 on v4

--- a/solution.py
+++ b/solution.py
@@ -441,7 +441,7 @@
     ("stage", (4, 768, 128), bf16), ("gat", (768, 128), bf16), ("co_in", (768, 128), bf16),
     ("gc_in", (768, 128), bf16), ("gl_in", (768, 128), bf16),
     ("xs", (768, 256), f32), ("es", (768, 256), f32), ("ys", (768, 256), f32),
-    ("gtap", (768, 256), f32), ("hw_high", (768, 256), bf16), ("hw_low", (768, 256), bf16),
+    ("hw_high", (768, 256), bf16), ("hw_low", (768, 256), bf16),
     ("taps", (96, 1024), f32), ("wind", (96, 1024), f32), ("dpre", (96, 1024), f32),
     ("last_t", (768, 64), f32), ("rate_t", (768, 8), f32),
     ("a1", (64, 1024), f32), ("a2", (64, 1024), f32), ("a3", (64, 1024), f32),
@@ -451,26 +451,31 @@
     ("hat2", (128, 768), f32), ("std2", (128, 1), f32), ("resid", (128, 768), f32),
     ("g_resid", (128, 768), f32), ("g_sum", (128, 768), f32), ("g_outer", (128, 768), f32),
     ("gm", (136, 2304), f32),
-    ("at_down", (2, 1536, 128), bf16), ("at_up", (2, 384, 128), bf16), ("at_in", (2, 384, 128), bf16),
-    ("at_out", (2, 384, 128), bf16), ("lh_down", (768, 512), bf16), ("lh_up", (384, 256), bf16),
+    ("at_down", (2, 1536, 128), bf16), ("at_up", (2, 384, 128), bf16), ("at_upz", (2, 384, 128), bf16), ("at_in", (2, 384, 128), bf16),
+    ("at_out", (2, 384, 128), bf16), ("lh_down", (768, 512), bf16), ("lh_up", (384, 256), bf16), ("lh_upz", (384, 256), bf16),
     ("lh_in", (384, 256), bf16), ("lh_out", (384, 256), bf16), ("rh_down", (512, 768), bf16),
     ("rh_up", (256, 3072), bf16), ("rh_in", (256, 2304), bf16), ("rh_out", (256, 768), bf16),
-    ("s1a", (8, 192, 768), bf16), ("k1a", (8, 192, 768), f32), ("r1a", (8, 192, 768), bf16),
-    ("s2a", (8, 96, 768), bf16), ("r2a", (8, 96, 768), bf16), ("s3a", (8, 4, 48, 384), bf16),
-    ("r3a", (8, 2, 48, 384), bf16), ("s4a", (8, 48, 384), bf16), ("r4a", (8, 48, 384), bf16),
+    ("s1a", (7, 192, 768), bf16), ("k1a", (7, 192, 768), f32), ("r1a", (7, 192, 768), bf16),
+    ("s2a", (7, 96, 768), bf16), ("r2a", (7, 96, 768), bf16), ("s3a", (7, 4, 48, 384), bf16),
+    ("r3a", (7, 2, 48, 384), bf16), ("s4a", (7, 48, 384), bf16), ("r4a", (7, 48, 384), bf16),
     ("s2b", (3, 384, 256), bf16), ("k2b", (3, 384, 256), f32), ("r2b", (3, 384, 256), bf16),
     ("s3b", (3, 4, 96, 256), bf16), ("r3b", (3, 2, 96, 256), bf16), ("s4b", (3, 96, 256), bf16),
     ("r4b", (3, 96, 256), bf16),
+    ("s1z", (192, 768), bf16), ("k1z", (192, 768), f32), ("r1z", (192, 768), bf16),
+    ("s2z", (96, 768), bf16), ("r2z", (96, 768), bf16), ("k3z", (48, 768), f32),
+    ("s3z", (48, 768), bf16), ("r3z", (48, 768), bf16), ("k4z", (24, 768), f32),
+    ("s4z", (48, 384), bf16), ("r4z", (48, 384), bf16),
     ("smf", (4, 88, 128), f32), ("q_in", (3, 88, 128), f32), ("q_sum", (88, 128), f32),
     ("o_in", (7, 8, 128), f32), ("ag", (4, 8, 32, 128), f32),
     ("f_gin", (432, 128), f32), ("f_gout", (144, 128), f32), ("f_gup", (576, 128), f32),
-    ("f_gdown", (576, 128), f32), ("f_out", (128, 768), f32), ("f_gtok", (128, 768), f32),
+    ("f_gdown", (576, 128), f32),
 )
 
 SEMAPHORES = (
     ("ld", (8,)), ("ls", (16,)), ("a2a_s", (4, 7)), ("a2a_r", (4, 7)), ("halo_s", (2,)), ("halo_r", (2,)),
-    ("pair_s", (12,)), ("pair_r", (12,)), ("p1_s", (8,)), ("p1_r", (8,)), ("p2_s", (11,)),
-    ("p2_r", (11,)), ("p3_s", (11,)), ("p3_r", (11,)), ("p4_s", (11,)), ("p4_r", (11,)), ("q_s", (3,)), ("q_r", (3,)),
+    ("pair_s", (13,)), ("pair_r", (13,)), ("p1_s", (8,)), ("p1_r", (8,)), ("p2_s", (11,)),
+    ("p2_r", (11,)), ("p3_s", (11,)), ("p3_r", (11,)), ("p4_s", (11,)), ("p4_r", (11,)),
+    ("zf_s", (4,)), ("zf_r", (4,)), ("q_s", (3,)), ("q_r", (3,)),
     ("o_s", (7,)), ("o_r", (7,)), ("ag_s", (10,)), ("ag_r", (10,)), ("st", (7,)),
 )
 
@@ -566,19 +571,24 @@
         share(9, r.rh_up.at[own], r.rh_up.at[block2], (s, other)),
         share(10, r.rh_out.at[own], r.rh_out.at[block2], (s, other)),
         share(11, r.rh_in.at[own], r.rh_in.at[block2], (s, other)),
+        share(12, r.at_upz.at[1 - c], r.lh_upz.at[:, block2], (s, other)),
     ]
 
-    def order_rows(v, halves):
+    def order_rows(v, halves, z_halves=None):
         t = jnp.transpose(v)
+        bits = [(i, j) for i in range(2) for j in range(2)]
         for core in range(2):
-            blocks = []
-            for i1 in range(2):
-                for i2 in range(2):
-                    ix, iy = (i1, i2) if core == 0 else (i2, i1)
-                    for iz in range(4):
-                        at_row = 24 * (iz * 8 + ix * 4 + iy * 2 + core)
-                        blocks.append(t[at_row : at_row + 24])
+
+            def block(i1, i2, iz):
+                ix, iy = (i1, i2) if core == 0 else (i2, i1)
+                at_row = 24 * (iz * 8 + ix * 4 + iy * 2 + core)
+                return t[at_row : at_row + 24]
+
+            blocks = [block(i1, i2, iz) for i1, i2 in bits for iz in range(4)]
             halves[core] = jnp.concatenate(blocks, axis=0).astype(bf16)
+            if z_halves is not None:
+                blocks = [block(i1, i2, 2 * j2 + j1) for j1, j2 in bits for i1, i2 in bits]
+                z_halves[core] = jnp.concatenate(blocks, axis=0).astype(bf16)
 
     loads[0].wait()
     hat, inv = norm_rows(r.tok[pl.ds(HALO, ROWS)].astype(f32))
@@ -777,9 +787,11 @@
     for copy in shares[3:6]:
         copy.start()
     shares[9].start()
-    order_rows(n2.astype(f32), r.at_up)
+    order_rows(n2.astype(f32), r.at_up, r.at_upz)
+    shares[12].start()
     shares[8].start()
     r.lh_up[:, own] = r.at_up[c]
+    r.lh_upz[:, own] = r.at_upz[c]
     order_rows(mixed.astype(f32), r.at_out)
     shares[7].start()
     r.lh_out[:, own] = r.at_out[c]
@@ -810,15 +822,15 @@
     def four_b(p):
         return remote(r.s4b.at[p], r.r4b.at[p], r.p4_s.at[8 + p], r.p4_r.at[8 + p], far)
 
-    def make_a(p0, count, lh, rh):
+    def make_a(p0, count, lh, rh, c0=0):
         @pl.loop(0, count)
         def _(p):
-            r.s1a[p0 + p] = nn(lh[at(1 - b1, 192)], rh[:, at(p, 768)]).astype(bf16)
-
-    def stay_a(p0, count, lh, rh):
+            r.s1a[p0 + p] = nn(lh[at(1 - b1, 192)], rh[:, at(c0 + p, 768)]).astype(bf16)
+
+    def stay_a(p0, count, lh, rh, c0=0):
         @pl.loop(0, count)
         def _(p):
-            r.k1a[p0 + p] = nn(lh[at(b1, 192)], rh[:, at(p, 768)])
+            r.k1a[p0 + p] = nn(lh[at(b1, 192)], rh[:, at(c0 + p, 768)])
 
     def ph1_a(p):
         one_a(p).wait_recv()
@@ -872,6 +884,51 @@
         v = r.s3b[p, 2 * z1 + z2].astype(f32) + r.r3b[p, z2].astype(f32) + r.r4b[p].astype(f32)
         for j in range(2):
             r.f_gdown[pl.ds(2 * p + j, 96, stride=6)] = v[:, 128 * j : 128 * j + 128]
+
+    hops = [
+        remote(src, dst, r.zf_s.at[i], r.zf_r.at[i], where)
+        for i, (src, dst, where) in enumerate(
+            ((r.s1z, r.r1z, near), (r.s2z, r.r2z, far), (r.s3z, r.r3z, first), (r.s4z, r.r4z, second))
+        )
+    ]
+
+    def zf1():
+        r.s1z[...] = nn(r.lh_upz[at(1 - z1, 192)], r.rh_up[:, 0:768]).astype(bf16)
+        hops[0].start()
+
+    def zf2():
+        hops[0].wait_recv()
+        rows = at(1 - z2, 96)
+        r.s2z[...] = (r.k1z[rows] + r.r1z[rows].astype(f32)).astype(bf16)
+        hops[1].start()
+
+    def zf3():
+        hops[1].wait_recv()
+        for ref, half in ((r.s3z, 1 - b1), (r.k3z, b1)):
+            rows = pl.ds(pl.multiple_of(96 * z2 + 48 * half, 48), 48)
+            v = r.k1z[rows] + r.r1z[rows].astype(f32) + r.r2z[at(half, 48)].astype(f32)
+            ref[...] = v.astype(ref.dtype)
+        hops[2].start()
+
+    def zf4():
+        hops[2].wait_recv()
+        v = r.k3z[...] + r.r3z[...].astype(f32)
+        lower, upper = v[:24], v[24:]
+        sent = jnp.where(b2 == 0, upper, lower)
+        r.k4z[...] = jnp.where(b2 == 0, lower, upper)
+        r.s4z[...] = jnp.concatenate([sent[:, :384], sent[:, 384:]], axis=0).astype(bf16)
+        hops[3].start()
+
+    def zf5():
+        hops[3].wait_recv()
+        got = r.r4z[...].astype(f32)
+        for h in range(2):
+            for j in range(3):
+                k = 3 * h + j
+                r.f_gup[pl.ds(k, 24, stride=24)] = (
+                    r.k4z[:, 128 * k : 128 * k + 128]
+                    + got[24 * h : 24 * h + 24, 128 * j : 128 * j + 128]
+                )
 
     def put(row, v):
         for j in range(v.shape[1] // 128):
@@ -893,9 +950,11 @@
     r.stage[2] = jnp.transpose(g_summed).astype(bf16)
     trade(2, r.gc_in)
 
+    shares[12].wait_recv()
+    shares[9].wait_recv()
+    zf1()
     shares[8].wait_recv()
-    shares[9].wait_recv()
-    make_a(0, 4, r.lh_up, r.rh_up)
+    make_a(0, 3, r.lh_up, r.rh_up, 1)
     one_a(0).start()
     for copy in shares[0:6]:
         copy.wait_recv()
@@ -908,7 +967,8 @@
         r.k2b[p] = nn(r.lh_down[at(b2, 384)], r.rh_down[:, 256 * p : 256 * p + 256])
     shares[7].wait_recv()
     shares[10].wait_recv()
-    make_a(4, 1, r.lh_out, r.rh_out)
+    make_a(3, 1, r.lh_out, r.rh_out)
+    r.k1z[...] = nn(r.lh_upz[at(z1, 192)], r.rh_up[:, 0:768])
     put(AT_GAIN + 6, col_sum(e * hat))
     put(AT_SHIFT + 6, col_sum(e))
     put(AT_DOWNB, col_sum(grad_f))
@@ -940,12 +1000,13 @@
 
     one_a(1).start()
     two_b(1).start()
-    stay_a(0, 4, r.lh_up, r.rh_up)
-    stay_a(4, 1, r.lh_out, r.rh_out)
+    zf2()
+    stay_a(0, 3, r.lh_up, r.rh_up, 1)
+    stay_a(3, 1, r.lh_out, r.rh_out)
     ph2_b(0)
     ph1_a(0)
-    r.f_out[...] = r.resid[...] + nn(r.act[...], r.down_w[...]) + r.down_b[...]
-    store_out = pltpu.make_async_copy(r.f_out, r.o_out, r.st.at[0])
+    r.resid[...] = r.resid[...] + nn(r.act[...], r.down_w[...]) + r.down_b[...]
+    store_out = pltpu.make_async_copy(r.resid, r.o_out, r.st.at[0])
     store_out.start()
 
     arrive(3, r.gl_in)
@@ -954,7 +1015,7 @@
     for part in range(3):
         r.gm[own, 768 * part : 768 * part + 768] = mixes[part]
     first_rows = remote(
-        r.gm.at[pl.ds(0, 8)], r.gm.at[pl.ds(ROWS, 8)], r.halo_s.at[1], r.halo_r.at[1], (s - 1, g)
+        r.gm.at[pl.ds(0, 2)], r.gm.at[pl.ds(ROWS, 2)], r.halo_s.at[1], r.halo_r.at[1], (s - 1, g)
     )
 
     @pl.when(s > 0)
@@ -992,21 +1053,22 @@
     e = nt(r.rh_in[own], r.in_w[...])
     shares[6].wait_recv()
     shares[11].wait_recv()
-    make_a(5, 3, r.lh_in, r.rh_in)
-    for p in (5, 6, 7, 3, 4):
+    make_a(4, 3, r.lh_in, r.rh_in)
+    for p in (4, 5, 6):
         one_a(p).start()
+    zf3()
     ph1_a(1)
     ph2_b(1)
     ph3_b(0)
-    stay_a(5, 3, r.lh_in, r.rh_in)
+    stay_a(4, 3, r.lh_in, r.rh_in)
     ph1_a(2)
     ph2_b(2)
     hat = r.hat1[...]
     put(AT_IN, col_sum(r.rh_in[own].astype(f32)))
     put(AT_GAIN, col_sum(e * hat))
     put(AT_SHIFT, col_sum(e))
-    r.f_gtok[...] = r.g_resid[...] + norm_rows_back(e, hat, r.std1[...], r.norm_gain[0:1])
-    store_tok = pltpu.make_async_copy(r.f_gtok, r.o_gtok, r.st.at[1])
+    r.g_resid[...] = r.g_resid[...] + norm_rows_back(e, hat, r.std1[...], r.norm_gain[0:1])
+    store_tok = pltpu.make_async_copy(r.g_resid, r.o_gtok, r.st.at[1])
     store_tok.start()
     ph2_a(0)
     ph3_b(1)
@@ -1024,15 +1086,16 @@
                 im = im + vr * di - vi * dr
             keep(r.xs, tile, lag, (re, im))
 
-    r.gtap[...] = by_table(r.xs[...], 0, every, every)
+    r.es[...] = by_table(r.xs[...], 0, every, every)
+    ph1_a(4)
     ph2_a(1)
     ph3_a(0)
     ph3_b(2)
     for b in range(8):
         cols = pl.ds(128 * b, 128)
-        gt = r.gtap[96 * b : 96 * b + 96, 128:256]
+        gt = r.es[96 * b : 96 * b + 96, 128:256]
         if b < 7:
-            gt = gt + r.gtap[96 * b + 96 : 96 * b + 192, 0:128]
+            gt = gt + r.es[96 * b + 96 : 96 * b + 192, 0:128]
         r.dpre[:, cols] = gt * r.wind[:, cols]
         r.taps[:, cols] = r.taps[:, cols] * gt
     g_rate = -jnp.sum(r.taps[...] * place, axis=1, keepdims=True)
@@ -1091,10 +1154,11 @@
     for k in range(1, 4):
         quarter(k).start()
 
+    one_a(3).start()
+    zf4()
+    ph1_a(5)
     ph2_a(2)
     ph3_a(1)
-    ph1_a(5)
-    ph1_a(6)
     for k in range(1, 4):
         quarter(k).wait_recv()
     r.q_sum[...] = r.smf[g] + r.q_in[0] + r.q_in[1] + r.q_in[2]
@@ -1103,9 +1167,9 @@
     def _(k):
         eighth(k).start()
 
+    ph2_a(4)
+    ph1_a(6)
     ph3_a(2)
-    ph1_a(7)
-    ph2_a(5)
 
     @pl.loop(1, 8)
     def _(k):
@@ -1118,12 +1182,11 @@
     def _(k):
         spread(k, False).start()
 
+    ph2_a(5)
+    ph3_a(4)
     ph1_a(3)
     ph2_a(6)
     ph3_a(5)
-    ph1_a(4)
-    ph2_a(7)
-    ph3_a(6)
     for p in range(3):
         ph4_b(p)
 
@@ -1132,24 +1195,22 @@
         spread(k, True).wait_recv()
 
     y_send.start()
+    ph2_a(3)
+    ph3_a(6)
+    zf5()
 
     @pl.loop(0, 3)
     def _(p):
-        ph4_a(p, r.f_gup, 6 * p, 24)
-
-    ph2_a(3)
-    ph3_a(7)
-    ph2_a(4)
-    ph3_a(3)
+        ph4_a(p, r.f_gup, 6 * p + 6, 24)
 
     @pl.loop(0, 3)
     def _(p):
-        ph4_a(5 + p, r.f_gin, 6 * p, 18)
-
+        ph4_a(4 + p, r.f_gin, 6 * p, 18)
+
+    ph3_a(3)
     y_back.wait_recv()
     for copy in c_send:
         copy.start()
-    ph3_a(4)
 
     stores = [
         store_out,
@@ -1161,13 +1222,12 @@
         pltpu.make_async_copy(r.ag, r.o_small, r.st.at[6]),
     ]
     stores[2].start()
+    stores[3].start()
     stores[5].start()
     for copy in c_back:
         copy.wait_recv()
     stores[6].start()
-    ph4_a(3, r.f_gup, 18, 24)
-    stores[3].start()
-    ph4_a(4, r.f_gout, 0, 6)
+    ph4_a(3, r.f_gout, 0, 6)
     stores[4].start()
 
     @pl.when(s < 7)
@@ -1193,7 +1253,10 @@
                 (s, other),
             ).wait_send()
 
-    @pl.loop(0, 8)
+    for copy in hops:
+        copy.wait_send()
+
+    @pl.loop(0, 7)
     def _(p):
         one_a(p).wait_send()
         two_a(p).wait_send()

time: 105 us -> 97.2 us (0.926)
  Pallas kernels: 105 us -> 96.2 us
    pallas_call x1, Pallas kernels: 101 us -> 93 us  [one_kernel_body(): pl.pallas_call(step_kernel, out_shape=[shape(128, width), shape(128, widt...]
where the time goes in v5:
time: 97.2 us; the launch traced here: 97.1 us
  Pallas kernels  96.2 us (99%)
    pallas_call x1, Pallas kernels, one_kernel_body(): pl.pallas_call(step_kernel, out_shape=[shape(128, width), shape(128, widt...  93 us
    pallas_call x1, Pallas kernels, one_kernel_body(): pl.pallas_call(finish_kernel, out_shape=[shape(1, 128, width), shape(1, 1...  3.21 us

profile of v5, /device:TPU:0, one launch (start us, length us, event | category | flops | bytes accessed | tf_op | source)
XLA Modules:
  0.0 97.1 jit_solution(9262374544859733751)
XLA Ops:
  0.7 93.0 %hyena_step.1 = (f32[128,768]{1,0:T(8,128)}, f32[128,768]{1,0:T(8,128)}, f32[432,128]{1,0:T(8,128)}, f32[144,128]{1,0:T(8,128)}, f32[576,128]{1,0:T(8,128)}, /*i...) custom-call(bf16[1,128,768]{2,1,0:T(8,128)(2,1)} %refs_0_.1, bf16[1,128,768]{2,1,0:T(8,128)(2,1)} %refs_1_.1, ...), custom_call_target="tpu_custom_call" | custom-call | tf_op jit(solution)/shard_map/hyena_step/pallas_call | solution.py:1362
  93.7 3.2 %hyena_finish.1 = (f32[1,128,768]{2,1,0:T(8,128)}, f32[1,128,768]{2,1,0:T(8,128)}, f32[2,768]{1,0:T(2,128)}, f32[2,768]{1,0:T(2,128)}, f32[432,128]{1,0:T(8,128)...) custom-call(f32[128,768]{1,0:T(8,128)} %get-tuple-element.49.i_out, ...), custom_call_target="tpu_custom_call" | custom-call | tf_op jit(solution)/shard_map/hyena_finish/pallas_call | solution.py:1385

commit v6 on v5

--- a/solution.py
+++ b/solution.py
@@ -448,8 +448,8 @@
     ("c1", (64, 1024), f32), ("c2", (64, 1024), f32), ("c3", (64, 1024), f32),
     ("u1", (64, 1024), f32), ("u2", (64, 1024), f32), ("u3", (64, 1024), f32),
     ("g_act", (128, 3072), f32), ("act", (128, 3072), bf16), ("summed", (128, 768), f32),
-    ("hat2", (128, 768), f32), ("std2", (128, 1), f32), ("resid", (128, 768), f32),
-    ("g_resid", (128, 768), f32), ("g_sum", (128, 768), f32), ("g_outer", (128, 768), f32),
+    ("hat2", (128, 768), f32), ("std2", (128, 1), f32),
+    ("g_sum", (128, 768), f32), ("g_outer", (128, 768), f32),
     ("gm", (136, 2304), f32),
     ("at_down", (2, 1536, 128), bf16), ("at_up", (2, 384, 128), bf16), ("at_upz", (2, 384, 128), bf16), ("at_in", (2, 384, 128), bf16),
     ("at_out", (2, 384, 128), bf16), ("lh_down", (768, 512), bf16), ("lh_up", (384, 256), bf16), ("lh_upz", (384, 256), bf16),
@@ -467,8 +467,7 @@
     ("s4z", (48, 384), bf16), ("r4z", (48, 384), bf16),
     ("smf", (4, 88, 128), f32), ("q_in", (3, 88, 128), f32), ("q_sum", (88, 128), f32),
     ("o_in", (7, 8, 128), f32), ("ag", (4, 8, 32, 128), f32),
-    ("f_gin", (432, 128), f32), ("f_gout", (144, 128), f32), ("f_gup", (576, 128), f32),
-    ("f_gdown", (576, 128), f32),
+
 )
 
 SEMAPHORES = (
@@ -476,7 +475,7 @@
     ("pair_s", (13,)), ("pair_r", (13,)), ("p1_s", (8,)), ("p1_r", (8,)), ("p2_s", (11,)),
     ("p2_r", (11,)), ("p3_s", (11,)), ("p3_r", (11,)), ("p4_s", (11,)), ("p4_r", (11,)),
     ("zf_s", (4,)), ("zf_r", (4,)), ("q_s", (3,)), ("q_r", (3,)),
-    ("o_s", (7,)), ("o_r", (7,)), ("ag_s", (10,)), ("ag_r", (10,)), ("st", (7,)),
+    ("o_s", (7,)), ("o_r", (7,)), ("ag_s", (10,)), ("ag_r", (10,)),
 )
 
 
@@ -649,31 +648,32 @@
     gated = (r.inner[...] * r.value[...]).astype(bf16).astype(f32)
     r.gf[...] = gated
 
+    across, over_two, next_z = 3 - z, lax.rem(z + 2, 4), z + 1 - 2 * z1
+    peers = [
+        2 * to_z + to_x
+        for to_z, to_x in (
+            (across, 1 - x), (across, x), (over_two, 1 - x), (over_two, x),
+            (next_z, 1 - x), (next_z, x), (z, 1 - x),
+        )
+    ]
+
+    def swap(which, k, dst, slot):
+        return remote(
+            r.stage.at[which, at(peers[k], 96)],
+            dst.at[at(slot, 96)],
+            r.a2a_s.at[which, k],
+            r.a2a_r.at[which, k],
+            (peers[k], g),
+        )
+
     def trade(which, dst):
-        @pl.loop(1, 8)
-        def _(k):
-            peer = lax.rem(s + k, 8)
-            remote(
-                r.stage.at[which, at(peer, 96)],
-                dst.at[at(s, 96)],
-                r.a2a_s.at[which, k - 1],
-                r.a2a_r.at[which, k - 1],
-                (peer, g),
-            ).start()
-
+        for k in range(7):
+            swap(which, k, dst, s).start()
         dst[at(s, 96)] = r.stage[which, at(s, 96)]
 
     def arrive(which, dst):
-        @pl.loop(1, 8)
-        def _(k):
-            peer = lax.rem(s + 8 - k, 8)
-            remote(
-                r.stage.at[which, at(peer, 96)],
-                dst.at[at(peer, 96)],
-                r.a2a_s.at[which, k - 1],
-                r.a2a_r.at[which, k - 1],
-                (peer, g),
-            ).wait_recv()
+        for k in range(7):
+            swap(which, k, dst, peers[k]).wait_recv()
 
     r.stage[0] = jnp.transpose(gated).astype(bf16)
     trade(0, r.gat)
@@ -765,7 +765,7 @@
     mixed = (r.outer[...] * sum_f).astype(bf16)
     loads[5].wait()
     res = r.tok[pl.ds(HALO, ROWS)].astype(f32) + nn(mixed, r.out_w[...]) + r.out_b[...]
-    r.resid[...] = res
+    r.o_out[...] = res
     hat, inv = norm_rows(res)
     r.hat2[...] = hat
     r.std2[...] = inv
@@ -883,7 +883,7 @@
         four_b(p).wait_recv()
         v = r.s3b[p, 2 * z1 + z2].astype(f32) + r.r3b[p, z2].astype(f32) + r.r4b[p].astype(f32)
         for j in range(2):
-            r.f_gdown[pl.ds(2 * p + j, 96, stride=6)] = v[:, 128 * j : 128 * j + 128]
+            r.o_gdown[pl.ds(2 * p + j, 96, stride=6)] = v[:, 128 * j : 128 * j + 128]
 
     hops = [
         remote(src, dst, r.zf_s.at[i], r.zf_r.at[i], where)
@@ -925,7 +925,7 @@
         for h in range(2):
             for j in range(3):
                 k = 3 * h + j
-                r.f_gup[pl.ds(k, 24, stride=24)] = (
+                r.o_gup[pl.ds(k, 24, stride=24)] = (
                     r.k4z[:, 128 * k : 128 * k + 128]
                     + got[24 * h : 24 * h + 24, 128 * j : 128 * j + 128]
                 )
@@ -939,7 +939,7 @@
     hat = r.hat2[...]
     grad_f = r.rh_down[own].astype(f32)
     g_res = grad_f + norm_rows_back(e, hat, r.std2[...], r.norm_gain[1:2])
-    r.g_resid[...] = g_res
+    r.o_gtok[...] = g_res
     g_res_b = g_res.astype(bf16)
     r.rh_out[own] = g_res_b
     shares[10].start()
@@ -950,10 +950,43 @@
     r.stage[2] = jnp.transpose(g_summed).astype(bf16)
     trade(2, r.gc_in)
 
+    def quarter(k):
+        t = lax.rem(g + k, 4)
+        return remote(r.smf.at[t], r.q_in.at[k - 1], r.q_s.at[k - 1], r.q_r.at[k - 1], (s, t))
+
+    def eighth(k):
+        t = peers[k]
+        return remote(r.q_sum.at[at(t, 8)], r.o_in.at[k], r.o_s.at[k], r.o_r.at[k], (t, g))
+
+    def spread(k, back):
+        slot = r.ag.at[g, peers[k] if back else s]
+        return remote(slot, slot, r.ag_s.at[k], r.ag_r.at[k], (peers[k], g))
+
+    over_y = g + y_step
+    first_slot, second_slot = r.ag.at[g], r.ag.at[over_y]
+    y_send = remote(first_slot, first_slot, r.ag_s.at[7], r.ag_r.at[7], (s, over_y))
+    y_back = remote(second_slot, second_slot, r.ag_s.at[7], r.ag_r.at[7], (s, over_y))
+    c_send = [
+        remote(slot, slot, r.ag_s.at[8 + i], r.ag_r.at[8 + i], (s, other))
+        for i, slot in enumerate((first_slot, second_slot))
+    ]
+    third_slot, fourth_slot = r.ag.at[other], r.ag.at[other + y_step]
+    c_back = [
+        remote(slot, slot, r.ag_s.at[8 + i], r.ag_r.at[8 + i], (s, other))
+        for i, slot in enumerate((third_slot, fourth_slot))
+    ]
+
+    put(AT_GAIN + 6, col_sum(e * hat))
+    put(AT_SHIFT + 6, col_sum(e))
+    put(AT_DOWNB, col_sum(grad_f))
+    put(AT_UPB, col_sum(r.rh_up[own].astype(f32)))
+    put(AT_OUTB, col_sum(g_res_b.astype(f32)))
+    put(AT_SKIP, col_sum(g_summed * r.gf[...]))
+    shares[8].wait_recv()
+    shares[9].wait_recv()
     shares[12].wait_recv()
-    shares[9].wait_recv()
-    zf1()
-    shares[8].wait_recv()
+    r.s1z[...] = nn(r.lh_upz[at(1 - z1, 192)], r.rh_up[:, 0:768]).astype(bf16)
+    hops[0].start()
     make_a(0, 3, r.lh_up, r.rh_up, 1)
     one_a(0).start()
     for copy in shares[0:6]:
@@ -961,21 +994,14 @@
     for p in range(3):
         cols = pl.ds(256 * p, 256)
         r.s2b[p] = nn(r.lh_down[at(1 - b2, 384)], r.rh_down[:, cols]).astype(bf16)
-        if p == 0:
-            two_b(p).start()
+    two_b(0).start()
     for p in range(3):
-        r.k2b[p] = nn(r.lh_down[at(b2, 384)], r.rh_down[:, 256 * p : 256 * p + 256])
+        cols = pl.ds(256 * p, 256)
+        r.k2b[p] = nn(r.lh_down[at(b2, 384)], r.rh_down[:, cols])
     shares[7].wait_recv()
     shares[10].wait_recv()
     make_a(3, 1, r.lh_out, r.rh_out)
     r.k1z[...] = nn(r.lh_upz[at(z1, 192)], r.rh_up[:, 0:768])
-    put(AT_GAIN + 6, col_sum(e * hat))
-    put(AT_SHIFT + 6, col_sum(e))
-    put(AT_DOWNB, col_sum(grad_f))
-    put(AT_UPB, col_sum(r.rh_up[own].astype(f32)))
-    put(AT_OUTB, col_sum(g_res_b.astype(f32)))
-    put(AT_SKIP, col_sum(g_summed * r.gf[...]))
-
     arrive(2, r.gc_in)
     r.ys[...] = (
         nn(r.gc_in[...], r.tables[2, high_half]) + nn(r.gc_in[...], r.tables[3, high_half])
@@ -997,7 +1023,6 @@
     g_long = by_table(r.es[...], 0, every, low_half)
     r.stage[3] = g_long.astype(bf16)
     trade(3, r.gl_in)
-
     one_a(1).start()
     two_b(1).start()
     zf2()
@@ -1005,10 +1030,7 @@
     stay_a(3, 1, r.lh_out, r.rh_out)
     ph2_b(0)
     ph1_a(0)
-    r.resid[...] = r.resid[...] + nn(r.act[...], r.down_w[...]) + r.down_b[...]
-    store_out = pltpu.make_async_copy(r.resid, r.o_out, r.st.at[0])
-    store_out.start()
-
+    r.o_out[...] = r.o_out[...] + nn(r.act[...], r.down_w[...]) + r.down_b[...]
     arrive(3, r.gl_in)
     g_gated = r.skip[...] * r.g_sum[...] + jnp.transpose(r.gl_in[...].astype(f32))
     mixes = (r.g_outer[...], g_gated * r.value[...], g_gated * r.inner[...])
@@ -1050,12 +1072,13 @@
             + r.conv_w[2:3, cols] * r.gm[pl.ds(0, ROWS), cols]
         ).astype(bf16)
     shares[11].start()
-    e = nt(r.rh_in[own], r.in_w[...])
+    r.g_sum[...] = nt(r.rh_in[own], r.in_w[...])
     shares[6].wait_recv()
     shares[11].wait_recv()
     make_a(4, 3, r.lh_in, r.rh_in)
-    for p in (4, 5, 6):
-        one_a(p).start()
+    one_a(4).start()
+    one_a(5).start()
+    one_a(6).start()
     zf3()
     ph1_a(1)
     ph2_b(1)
@@ -1063,16 +1086,14 @@
     stay_a(4, 3, r.lh_in, r.rh_in)
     ph1_a(2)
     ph2_b(2)
+    e = r.g_sum[...]
     hat = r.hat1[...]
     put(AT_IN, col_sum(r.rh_in[own].astype(f32)))
     put(AT_GAIN, col_sum(e * hat))
     put(AT_SHIFT, col_sum(e))
-    r.g_resid[...] = r.g_resid[...] + norm_rows_back(e, hat, r.std1[...], r.norm_gain[0:1])
-    store_tok = pltpu.make_async_copy(r.g_resid, r.o_gtok, r.st.at[1])
-    store_tok.start()
+    r.o_gtok[...] = r.o_gtok[...] + norm_rows_back(e, hat, r.std1[...], r.norm_gain[0:1])
     ph2_a(0)
     ph3_b(1)
-
     @pl.loop(0, 12)
     def _(tile):
         v = [pick(r.xs, tile, b) for b in range(8)]
@@ -1121,39 +1142,8 @@
         else:
             r.smf[1, 0:33, 0:64] = nt_high(r.feats[...], g_u)
 
-    def quarter(k):
-        t = lax.rem(g + k, 4)
-        return remote(r.smf.at[t], r.q_in.at[k - 1], r.q_s.at[k - 1], r.q_r.at[k - 1], (s, t))
-
-    def eighth(k):
-        t = lax.rem(s + k, 8)
-        return remote(
-            r.q_sum.at[at(t, 8)], r.o_in.at[k - 1], r.o_s.at[k - 1], r.o_r.at[k - 1], (t, g)
-        )
-
-    def spread(k, back):
-        t = lax.rem(s + k, 8)
-        mine = lax.rem(s + 8 - k, 8) if back else s
-        slot = r.ag.at[g, mine]
-        return remote(slot, slot, r.ag_s.at[k - 1], r.ag_r.at[k - 1], (t, g))
-
-    over_y = g + y_step
-    first_slot, second_slot = r.ag.at[g], r.ag.at[over_y]
-    y_send = remote(first_slot, first_slot, r.ag_s.at[7], r.ag_r.at[7], (s, over_y))
-    y_back = remote(second_slot, second_slot, r.ag_s.at[7], r.ag_r.at[7], (s, over_y))
-    c_send = [
-        remote(slot, slot, r.ag_s.at[8 + i], r.ag_r.at[8 + i], (s, other))
-        for i, slot in enumerate((first_slot, second_slot))
-    ]
-    third_slot, fourth_slot = r.ag.at[other], r.ag.at[other + y_step]
-    c_back = [
-        remote(slot, slot, r.ag_s.at[8 + i], r.ag_r.at[8 + i], (s, other))
-        for i, slot in enumerate((third_slot, fourth_slot))
-    ]
-
     for k in range(1, 4):
         quarter(k).start()
-
     one_a(3).start()
     zf4()
     ph1_a(5)
@@ -1162,73 +1152,45 @@
     for k in range(1, 4):
         quarter(k).wait_recv()
     r.q_sum[...] = r.smf[g] + r.q_in[0] + r.q_in[1] + r.q_in[2]
-
-    @pl.loop(1, 8)
-    def _(k):
+    for k in range(7):
         eighth(k).start()
-
     ph2_a(4)
     ph1_a(6)
     ph3_a(2)
-
-    @pl.loop(1, 8)
-    def _(k):
+    for k in range(7):
         eighth(k).wait_recv()
-
     r.ag[g, s, pl.ds(0, 8)] = r.q_sum[at(s, 8)] + jnp.sum(r.o_in[...], axis=0)
     r.ag[g, s, pl.ds(8, 24)] = r.q_sum[pl.ds(64, 24)]
-
-    @pl.loop(1, 8)
-    def _(k):
+    for k in range(7):
         spread(k, False).start()
-
     ph2_a(5)
     ph3_a(4)
     ph1_a(3)
     ph2_a(6)
     ph3_a(5)
-    for p in range(3):
-        ph4_b(p)
-
-    @pl.loop(1, 8)
-    def _(k):
+    for k in range(7):
         spread(k, True).wait_recv()
-
     y_send.start()
     ph2_a(3)
     ph3_a(6)
+    ph4_b(0)
+    ph4_b(1)
+    ph4_b(2)
+    ph3_a(3)
     zf5()
-
-    @pl.loop(0, 3)
-    def _(p):
-        ph4_a(p, r.f_gup, 6 * p + 6, 24)
-
-    @pl.loop(0, 3)
-    def _(p):
-        ph4_a(4 + p, r.f_gin, 6 * p, 18)
-
-    ph3_a(3)
+    ph4_a(0, r.o_gup, 6, 24)
+    ph4_a(1, r.o_gup, 12, 24)
+    ph4_a(2, r.o_gup, 18, 24)
     y_back.wait_recv()
     for copy in c_send:
         copy.start()
-
-    stores = [
-        store_out,
-        store_tok,
-        pltpu.make_async_copy(r.f_gdown, r.o_gdown, r.st.at[2]),
-        pltpu.make_async_copy(r.f_gup, r.o_gup, r.st.at[3]),
-        pltpu.make_async_copy(r.f_gout, r.o_gout, r.st.at[4]),
-        pltpu.make_async_copy(r.f_gin, r.o_gin, r.st.at[5]),
-        pltpu.make_async_copy(r.ag, r.o_small, r.st.at[6]),
-    ]
-    stores[2].start()
-    stores[3].start()
-    stores[5].start()
+    ph4_a(4, r.o_gin, 0, 18)
+    ph4_a(5, r.o_gin, 6, 18)
+    ph4_a(6, r.o_gin, 12, 18)
     for copy in c_back:
         copy.wait_recv()
-    stores[6].start()
-    ph4_a(3, r.f_gout, 0, 6)
-    stores[4].start()
+    r.o_small[...] = r.ag[...]
+    ph4_a(3, r.o_gout, 0, 6)
 
     @pl.when(s < 7)
     def _():
@@ -1272,43 +1234,26 @@
     for k in range(1, 4):
         quarter(k).wait_send()
 
-    @pl.loop(1, 8)
-    def _(k):
+    for k in range(7):
         eighth(k).wait_send()
         spread(k, False).wait_send()
 
     y_send.wait_send()
     for copy in c_send:
         copy.wait_send()
-    for copy in stores:
-        copy.wait()
 
 
 def finish_kernel(
-    i_out, i_gtok, i_gin, i_gout, i_gup, i_gdown, i_small,
+    i_out, i_gtok, i_gin, i_gout, i_gup, i_gdown, small,
     out, gtok, gain, shift, gin, in_b, conv_w, conv_b, first, hidden, bias, freq,
-    last, decay, skip, gout, out_b, gup, up_b, gdown, down_b,
-    h_out, h_gtok, h_gin, h_gout, h_gup, h_gdown, small, sem_in, sem_out,
+    last, decay, skip, gout, out_b, gup, up_b, gdown, down_b, sems,
 ):
     bulk = (
-        (i_small, small, None),
-        (i_out, h_out, out.at[0]),
-        (i_gtok, h_gtok, gtok.at[0]),
-        (i_gin, h_gin, gin),
-        (i_gout, h_gout, gout),
-        (i_gup, h_gup, gup),
-        (i_gdown, h_gdown, gdown),
-    )
-    enter = [pltpu.make_async_copy(a, b, sem_in.at[i]) for i, (a, b, _) in enumerate(bulk)]
-    leave = [
-        pltpu.make_async_copy(b, d, sem_out.at[i]) for i, (_, b, d) in enumerate(bulk) if i > 0
-    ]
-    for copy in enter:
+        (i_out, out.at[0]), (i_gtok, gtok.at[0]), (i_gin, gin), (i_gout, gout), (i_gup, gup), (i_gdown, gdown),
+    )
+    leave = [pltpu.make_async_copy(a, b, sems.at[i]) for i, (a, b) in enumerate(bulk)]
+    for copy in leave:
         copy.start()
-    for i in range(6):
-        enter[i + 1].wait()
-        leave[i].start()
-    enter[0].wait()
     rows = jnp.concatenate([small[i, j, 0:8, :] for i in range(4) for j in range(8)], axis=0)
 
     def fetch(at_row, dest, dest_row, wide):
@@ -1362,16 +1307,16 @@
     outs = pl.pallas_call(
         step_kernel,
         out_shape=[
-            shape(128, width), shape(128, width), shape(432, 128), shape(144, 128),
-            shape(576, 128), shape(576, 128), shape(4, 8, 32, 128),
+            vm(128, width), vm(128, width), vm(432, 128), vm(144, 128),
+            vm(576, 128), vm(576, 128), vm(4, 8, 32, 128),
         ],
         in_specs=[any_spec] * 23,
-        out_specs=[any_spec] * 7,
+        out_specs=[vmem_spec] * 7,
         scratch_shapes=[vm(*dims) for _, dims in SMALL_ARGS]
         + [vm(*dims, dtype=dtype) for _, dims, dtype in SCRATCH]
         + [dma(*dims) for _, dims in SEMAPHORES],
         compiler_params=pltpu.CompilerParams(
-            collective_id=0, has_side_effects=True, vmem_limit_bytes=62 * 1024 * 1024
+            collective_id=0, has_side_effects=True, vmem_limit_bytes=60 * 1024 * 1024
         ),
         name="hyena_step",
     )(
@@ -1390,15 +1335,12 @@
             shape(3, 64), shape(3, 64), shape(64, width), shape(width), shape(width), shape(144, 128),
             shape(width), shape(576, 128), shape(hidden), shape(576, 128), shape(width),
         ],
-        in_specs=[any_spec] * 7,
+        in_specs=[vmem_spec] * 7,
         out_specs=[any_spec, any_spec, vmem_spec, vmem_spec, any_spec]
         + [vmem_spec] * 10
         + [any_spec, vmem_spec, any_spec, vmem_spec, any_spec, vmem_spec],
-        scratch_shapes=[
-            vm(128, width), vm(128, width), vm(432, 128), vm(144, 128), vm(576, 128), vm(576, 128),
-            vm(4, 8, 32, 128), dma(7), dma(7),
-        ],
-        compiler_params=pltpu.CompilerParams(vmem_limit_bytes=60 * 1024 * 1024),
+        scratch_shapes=[dma(6)],
+        compiler_params=pltpu.CompilerParams(vmem_limit_bytes=32 * 1024 * 1024),
         name="hyena_finish",
     )(*outs)
     flat = (4, 15, 17, 19)

time: 97.2 us -> 94.3 us (0.970)
  Pallas kernels: 96.2 us -> 93.2 us
    pallas_call x1, Pallas kernels: 93 us -> 91.2 us  [one_kernel_body(): pl.pallas_call(step_kernel, out_shape=[vm(128, width), vm(128, width), vm...]
    pallas_call x1, Pallas kernels: 3.21 us -> 2 us  [one_kernel_body(): pl.pallas_call(finish_kernel, out_shape=[shape(1, 128, width), shape(1, 1...]
where the time goes in v6:
time: 94.3 us; the launch traced here: 94.1 us
  Pallas kernels  93.2 us (99%)
    pallas_call x1, Pallas kernels, one_kernel_body(): pl.pallas_call(step_kernel, out_shape=[vm(128, width), vm(128, width), vm...  91.2 us
    pallas_call x1, Pallas kernels, one_kernel_body(): pl.pallas_call(finish_kernel, out_shape=[shape(1, 128, width), shape(1, 1...  2 us

profile of v6, /device:TPU:0, one launch (start us, length us, event | category | flops | bytes accessed | tf_op | source)
XLA Modules:
  0.0 94.1 jit_solution(14639601584167405387)
XLA Ops:
  0.7 91.2 %hyena_step.1 = (f32[128,768]{1,0:T(8,128)S(1)}, f32[128,768]{1,0:T(8,128)S(1)}, f32[432,128]{1,0:T(8,128)S(1)}, f32[144,128]{1,0:T(8,128)S(1)}, f32[576,128]{1,...) custom-call(bf16[1,128,768]{2,1,0:T(8,128)(2,1)} %refs_0_.1, bf16[1,128,768]{2,1,0:T(8,128)(2,1)} %refs_1_.1, ...), custom_call_target="tpu_custom_call" | custom-call | tf_op jit(solution)/shard_map/hyena_step/pallas_call | solution.py:1307
  91.9 2.0 %hyena_finish.1 = (f32[1,128,768]{2,1,0:T(8,128)}, f32[1,128,768]{2,1,0:T(8,128)}, f32[2,768]{1,0:T(2,128)}, f32[2,768]{1,0:T(2,128)}, f32[432,128]{1,0:T(8,128)...) custom-call(f32[128,768]{1,0:T(8,128)S(1)} %get-tuple-element.49.i_o, ...), custom_call_target="tpu_custom_call" | custom-call | tf_op jit(solution)/shard_map/hyena_finish/pallas_call | solution.py:1330

commit v7 on v6

--- a/solution.py
+++ b/solution.py
@@ -466,7 +466,7 @@
     ("s3z", (48, 768), bf16), ("r3z", (48, 768), bf16), ("k4z", (24, 768), f32),
     ("s4z", (48, 384), bf16), ("r4z", (48, 384), bf16),
     ("smf", (4, 88, 128), f32), ("q_in", (3, 88, 128), f32), ("q_sum", (88, 128), f32),
-    ("o_in", (7, 8, 128), f32), ("ag", (4, 8, 32, 128), f32),
+    ("o_in", (7, 8, 128), f32), ("ag", (4, 8, 32, 128), bf16),
 
 )
 
@@ -1159,8 +1159,8 @@
     ph3_a(2)
     for k in range(7):
         eighth(k).wait_recv()
-    r.ag[g, s, pl.ds(0, 8)] = r.q_sum[at(s, 8)] + jnp.sum(r.o_in[...], axis=0)
-    r.ag[g, s, pl.ds(8, 24)] = r.q_sum[pl.ds(64, 24)]
+    eighth_sum = r.q_sum[at(s, 8)] + jnp.sum(r.o_in[...], axis=0)
+    r.ag[g, s] = jnp.concatenate([eighth_sum, r.q_sum[pl.ds(64, 24)]], axis=0).astype(bf16)
     for k in range(7):
         spread(k, False).start()
     ph2_a(5)
@@ -1254,7 +1254,8 @@
     leave = [pltpu.make_async_copy(a, b, sems.at[i]) for i, (a, b) in enumerate(bulk)]
     for copy in leave:
         copy.start()
-    rows = jnp.concatenate([small[i, j, 0:8, :] for i in range(4) for j in range(8)], axis=0)
+    slots = [[small[i, j].astype(f32) for j in range(8)] for i in range(4)]
+    rows = jnp.concatenate([slots[i][j][0:8] for i in range(4) for j in range(8)], axis=0)
 
     def fetch(at_row, dest, dest_row, wide):
         for j in range(wide):
@@ -1279,7 +1280,7 @@
     bias[...] = rows[AT_FIRST : AT_FIRST + 3, 64:128]
     freq[...] = rows[AT_FIRST + 3 : AT_FIRST + 6, 64:128]
     channels = jnp.transpose(
-        jnp.concatenate([small[j, i, 8:32, :] for i in range(8) for j in range(4)], axis=0)
+        jnp.concatenate([slots[j][i][8:32] for i in range(8) for j in range(4)], axis=0)
     )
     last[...] = channels[0:64]
     decay[...] = channels[64:65].reshape(768)
@@ -1308,7 +1309,7 @@
         step_kernel,
         out_shape=[
             vm(128, width), vm(128, width), vm(432, 128), vm(144, 128),
-            vm(576, 128), vm(576, 128), vm(4, 8, 32, 128),
+            vm(576, 128), vm(576, 128), vm(4, 8, 32, 128, dtype=bf16),
         ],
         in_specs=[any_spec] * 23,
         out_specs=[vmem_spec] * 7,

time: 94.3 us -> 93 us (0.986)
  Pallas kernels: 93.2 us -> 91.9 us
    pallas_call x1, Pallas kernels: 91.2 us -> 89.9 us  [one_kernel_body(): pl.pallas_call(step_kernel, out_shape=[vm(128, width), vm(128, width), vm...]
where the time goes in v7:
time: 93 us; the launch traced here: 92.8 us
  Pallas kernels  91.9 us (99%)
    pallas_call x1, Pallas kernels, one_kernel_body(): pl.pallas_call(step_kernel, out_shape=[vm(128, width), vm(128, width), vm...  89.9 us
    pallas_call x1, Pallas kernels, one_kernel_body(): pl.pallas_call(finish_kernel, out_shape=[shape(1, 128, width), shape(1, 1...  2.01 us

profile of v7, /device:TPU:0, one launch (start us, length us, event | category | flops | bytes accessed | tf_op | source)
XLA Modules:
  0.0 92.8 jit_solution(7602282331118307843)
XLA Ops:
  0.7 89.9 %hyena_step.1 = (f32[128,768]{1,0:T(8,128)S(1)}, f32[128,768]{1,0:T(8,128)S(1)}, f32[432,128]{1,0:T(8,128)S(1)}, f32[144,128]{1,0:T(8,128)S(1)}, f32[576,128]{1,...) custom-call(bf16[1,128,768]{2,1,0:T(8,128)(2,1)} %refs_0_.1, bf16[1,128,768]{2,1,0:T(8,128)(2,1)} %refs_1_.1, ...), custom_call_target="tpu_custom_call" | custom-call | tf_op jit(solution)/shard_map/hyena_step/pallas_call | solution.py:1308
  90.6 2.0 %hyena_finish.1 = (f32[1,128,768]{2,1,0:T(8,128)}, f32[1,128,768]{2,1,0:T(8,128)}, f32[2,768]{1,0:T(2,128)}, f32[2,768]{1,0:T(2,128)}, f32[432,128]{1,0:T(8,128)...) custom-call(f32[128,768]{1,0:T(8,128)S(1)} %get-tuple-element.49.i_o, ...), custom_call_target="tpu_custom_call" | custom-call | tf_op jit(solution)/shard_map/hyena_finish/pallas_call | solution.py:1331

commit v8 on v7

--- a/solution.py
+++ b/solution.py
@@ -1173,9 +1173,6 @@
     y_send.start()
     ph2_a(3)
     ph3_a(6)
-    ph4_b(0)
-    ph4_b(1)
-    ph4_b(2)
     ph3_a(3)
     zf5()
     ph4_a(0, r.o_gup, 6, 24)
@@ -1187,6 +1184,9 @@
     ph4_a(4, r.o_gin, 0, 18)
     ph4_a(5, r.o_gin, 6, 18)
     ph4_a(6, r.o_gin, 12, 18)
+    ph4_b(0)
+    ph4_b(1)
+    ph4_b(2)
     for copy in c_back:
         copy.wait_recv()
     r.o_small[...] = r.ag[...]

time: 93 us -> 93 us (level)
  no operation moved by 1% of the time
where the time goes in v8:
time: 93 us; the launch traced here: 92.8 us
  Pallas kernels  91.9 us (99%)
    pallas_call x1, Pallas kernels, one_kernel_body(): pl.pallas_call(step_kernel, out_shape=[vm(128, width), vm(128, width), vm...  89.9 us
    pallas_call x1, Pallas kernels, one_kernel_body(): pl.pallas_call(finish_kernel, out_shape=[shape(1, 128, width), shape(1, 1...  2.01 us

profile of v8, /device:TPU:0, one launch (start us, length us, event | category | flops | bytes accessed | tf_op | source)
XLA Modules:
  0.0 92.8 jit_solution(17492932039002587669)
XLA Ops:
  0.7 89.9 %hyena_step.1 = (f32[128,768]{1,0:T(8,128)S(1)}, f32[128,768]{1,0:T(8,128)S(1)}, f32[432,128]{1,0:T(8,128)S(1)}, f32[144,128]{1,0:T(8,128)S(1)}, f32[576,128]{1,...) custom-call(bf16[1,128,768]{2,1,0:T(8,128)(2,1)} %refs_0_.1, bf16[1,128,768]{2,1,0:T(8,128)(2,1)} %refs_1_.1, ...), custom_call_target="tpu_custom_call" | custom-call | tf_op jit(solution)/shard_map/hyena_step/pallas_call | solution.py:1308
  90.6 2.0 %hyena_finish.1 = (f32[1,128,768]{2,1,0:T(8,128)}, f32[1,128,768]{2,1,0:T(8,128)}, f32[2,768]{1,0:T(2,128)}, f32[2,768]{1,0:T(2,128)}, f32[432,128]{1,0:T(8,128)...) custom-call(f32[128,768]{1,0:T(8,128)S(1)} %get-tuple-element.49.i_o, ...), custom_call_target="tpu_custom_call" | custom-call | tf_op jit(solution)/shard_map/hyena_finish/pallas_call | solution.py:1331
